TPU v7x, 512 devices: a whole 4x8x8 slice. The times are simulated.
512 devices in a mesh: expert: 64 (over z, y), dp: 8 (over x, core).
Axes of the slice: x: 4, y: 8, z: 8, core: 2. Of those that a mesh axis runs over, the one named last changes fastest.
Arguments:
- attn_win: bfloat16 [64, 1024, 768], P('dp', 'expert'), may hold values from -6 to 6
- shortcut: bfloat16 [64, 1024, 768], P('dp', 'expert'), may hold values from -6 to 6
- d_out: bfloat16 [64, 1024, 768], P('dp', 'expert'), may hold values from -6 to 6
- expert_ids: int32 [8, 64, 128, 2], P('dp', 'expert'), may hold values from 0 to 63, all different within a row; in each aligned block of 128 rows (0 to 127, 128 to 255, ..., all dimensions but the last counted through in order) at most 5 rows name the same one
- gate_probs: float32 [8, 64, 128, 2], P('dp', 'expert'), may hold values from 0.1 to 1
- shift_offsets: int32 [2], replicated, may hold values from 1 to 4, as said below
- w_in: bfloat16 [64, 768, 1536], P('expert', None, 'dp'), may hold values from -0.21875 to 0.21875
- w_out: bfloat16 [64, 1536, 768], P('expert', 'dp'), may hold values from -0.15625 to 0.15625
Outputs:
- block_out: bfloat16 [64, 1024, 768], P('dp', 'expert')
- d_shortcut: bfloat16 [64, 1024, 768], P('dp', 'expert')
- d_attn: bfloat16 [64, 1024, 768], P('dp', 'expert')
- d_gates: float32 [8, 64, 128, 2], P('dp', 'expert')
- grad_in: float32 [64, 768, 1536], P('expert', None, 'dp')
- grad_out: float32 [64, 1536, 768], P('expert', 'dp')
Inputs may be any that keep to these rules, and one draw needn't show every extreme that they name: `expert_ids`: in each device's tile no expert is named by more than 5 tokens, a bound that some block reaches. `shift_offsets`: one of the two offsets equals 4.
All inputs are finite; a program needn't handle non-finite values.
Results may differ from a plain program's by a relative error of at most 0.0061.
Values may be sent and summed in bfloat16 or wider, within the bound.
No kernel may reach another device: no remote copies, remote signals or barrier semaphores. Data moves between devices by JAX's collectives and lax.ppermute only.
A program may use at most 128 MiB of HBM per device.

v0:
```python
import jax
import jax.numpy as jnp
from jax import lax
from jax.sharding import PartitionSpec as P

SHIFT = 4
CAP = 5


def with_halo(block, sides, width):
    for axis, dim in sides:
        count = lax.axis_size(axis)
        forward = [(i, i + 1) for i in range(count - 1)]
        forward.append((count - 1, 0))
        backward = [(target, source) for source, target in forward]
        low = lax.ppermute(
            lax.slice_in_dim(block, block.shape[dim] - width, None, axis=dim), axis, forward
        )
        high = lax.ppermute(lax.slice_in_dim(block, 0, width, axis=dim), axis, backward)
        block = jnp.concatenate([low, block, high], axis=dim)
    return block


def slope_of(hidden):
    cdf = 0.5 * (1.0 + lax.erf(hidden * 0.7071067811865476))
    pdf = jnp.exp(-0.5 * hidden * hidden) * 0.3989422804014327
    return cdf + hidden * pdf


def rolled(field, row_off, col_off):
    padded = with_halo(field, (("dp", 0), ("expert", 1)), SHIFT)
    start_row = SHIFT + row_off
    start_col = SHIFT + col_off
    return lax.dynamic_slice(padded, (start_row, start_col, jnp.int32(0)), field.shape)


def before_send(buffer, n_src, local_count):
    return buffer.reshape(n_src, local_count * CAP, buffer.shape[-1])


def after_send(arrived, n_src, local_count):
    width = arrived.shape[-1]
    arrived = arrived.reshape(n_src, local_count, CAP, width).transpose(1, 0, 2, 3)
    return arrived.reshape(local_count, n_src * CAP, width)


def before_return(rows, n_src, local_count):
    width = rows.shape[-1]
    shaped = rows.reshape(local_count, n_src, CAP, width).transpose(1, 0, 2, 3)
    return shaped.reshape(n_src, local_count * CAP, width)


def after_return(returned, n_src, local_count):
    return returned.reshape(n_src * local_count * CAP, returned.shape[-1])


def to_experts(buffer, n_src, local_count):
    arrived = lax.all_to_all(
        before_send(buffer, n_src, local_count), "expert", split_axis=0, concat_axis=0, tiled=True
    )
    return after_send(arrived, n_src, local_count)


def from_experts(rows, n_src, local_count):
    returned = lax.all_to_all(
        before_return(rows, n_src, local_count), "expert", split_axis=0, concat_axis=0, tiled=True
    )
    return after_return(returned, n_src, local_count)


def forward_experts(u_exp, full_in, full_out):
    hidden = jnp.einsum("erd,edf->erf", u_exp, full_in, preferred_element_type=jnp.float32)
    act = jax.nn.gelu(hidden, approximate=False).astype(jnp.bfloat16)
    y_exp = jnp.einsum("erf,efd->erd", act, full_out, preferred_element_type=jnp.float32).astype(
        jnp.bfloat16
    )
    return (hidden, act, y_exp)


def backward_experts(g_exp, hidden, full_in, full_out):
    dact = jnp.einsum("erd,efd->erf", g_exp, full_out, preferred_element_type=jnp.float32)
    dhid = (dact * slope_of(hidden)).astype(jnp.bfloat16)
    q_exp = jnp.einsum("erf,edf->erd", dhid, full_in, preferred_element_type=jnp.float32).astype(
        jnp.bfloat16
    )
    return (dhid, q_exp)


def per_device(attn_win, shortcut, d_out, expert_ids, gate_probs, shift_offsets, w_in, w_out):
    tile_rows, tile_cols, width = attn_win.shape
    tokens = tile_rows * tile_cols
    local_count = w_in.shape[0]
    n_src = lax.axis_size("expert")
    total_experts = local_count * n_src
    n_slots = total_experts * CAP
    row_off = shift_offsets[0]
    col_off = shift_offsets[1]
    x = shortcut.astype(jnp.float32) + rolled(attn_win, -row_off, -col_off).astype(jnp.float32)
    x = x.reshape(tokens, width)
    feature_average = jnp.mean(x, axis=-1, keepdims=True)
    centered_input = x - feature_average
    inverse_deviation = lax.rsqrt(
        jnp.mean(centered_input * centered_input, axis=-1, keepdims=True) + 1e-05
    )
    standardized_input = centered_input * inverse_deviation
    normalized_tokens = standardized_input.astype(jnp.bfloat16)
    ids = expert_ids.reshape(tokens, 2)
    gates = gate_probs.reshape(tokens, 2)
    onehot = (ids.reshape(2 * tokens, 1) == jnp.arange(total_experts, dtype=jnp.int32)).astype(
        jnp.int32
    )
    before = jnp.cumsum(onehot, axis=0) - onehot
    pos = jnp.sum(before * onehot, axis=-1).reshape(tokens, 2)
    slot = ids * CAP + pos
    picker = (jnp.arange(n_slots, dtype=jnp.int32)[:, None] == slot.reshape(1, 2 * tokens)).astype(
        jnp.bfloat16
    )
    full_in, full_out = (
        lax.all_gather(w_in, "dp", axis=2, tiled=True),
        lax.all_gather(w_out, "dp", axis=1, tiled=True),
    )
    dout_tok = d_out.reshape(tokens, width).astype(jnp.float32)
    sent = jnp.dot(
        picker, jnp.repeat(normalized_tokens, 2, axis=0), preferred_element_type=jnp.float32
    ).astype(jnp.bfloat16)
    weighted = (
        (gates[:, :, None] * dout_tok[:, None, :]).astype(jnp.bfloat16).reshape(2 * tokens, width)
    )
    g_sent = jnp.dot(picker, weighted, preferred_element_type=jnp.float32).astype(jnp.bfloat16)
    u_exp = to_experts(sent, n_src, local_count)
    hidden, act, y_exp = forward_experts(u_exp, full_in, full_out)
    y_slots = from_experts(y_exp, n_src, local_count)
    g_exp = to_experts(g_sent, n_src, local_count)
    dhid, q_exp = backward_experts(g_exp, hidden, full_in, full_out)
    q_slots = from_experts(q_exp, n_src, local_count)
    y_tok = jnp.take(y_slots, slot, axis=0).astype(jnp.float32)
    moe = gates[:, 0:1] * y_tok[:, 0, :] + gates[:, 1:2] * y_tok[:, 1, :]
    block_out = (x + moe).astype(jnp.bfloat16).reshape(tile_rows, tile_cols, width)
    d_gates = jnp.sum(dout_tok[:, None, :] * y_tok, axis=-1)
    q_tok = jnp.take(q_slots, slot, axis=0).astype(jnp.float32)
    upstream_gradient = q_tok[:, 0, :] + q_tok[:, 1, :]
    layernorm_input_gradient = inverse_deviation * (
        upstream_gradient
        - jnp.mean(upstream_gradient, axis=-1, keepdims=True)
        - standardized_input
        * jnp.mean(upstream_gradient * standardized_input, axis=-1, keepdims=True)
    )
    d_shortcut = (
        (dout_tok + layernorm_input_gradient)
        .astype(jnp.bfloat16)
        .reshape(tile_rows, tile_cols, width)
    )
    d_attn = rolled(d_shortcut, row_off, col_off)
    u_piece = lax.all_gather(u_exp, "dp", axis=1, tiled=True)
    g_piece = lax.all_gather(g_exp, "dp", axis=1, tiled=True)
    h_piece = jnp.einsum("erd,edf->erf", u_piece, w_in, preferred_element_type=jnp.float32)
    a_piece = jax.nn.gelu(h_piece, approximate=False).astype(jnp.bfloat16)
    da_piece = jnp.einsum("erd,efd->erf", g_piece, w_out, preferred_element_type=jnp.float32)
    p_piece = (da_piece * slope_of(h_piece)).astype(jnp.bfloat16)
    first = jnp.einsum("erd,erf->edf", u_piece, p_piece, preferred_element_type=jnp.float32)
    second = jnp.einsum("erf,erd->efd", a_piece, g_piece, preferred_element_type=jnp.float32)
    return (block_out, d_shortcut, d_attn, d_gates.reshape(1, 1, tokens, 2), first, second)


def solution(mesh):
    in_specs = (
        P("dp", "expert", None),
        P("dp", "expert", None),
        P("dp", "expert", None),
        P("dp", "expert", None, None),
        P("dp", "expert", None, None),
        P(),
        P("expert", None, "dp"),
        P("expert", "dp", None),
    )
    out_specs = (
        P("dp", "expert", None),
        P("dp", "expert", None),
        P("dp", "expert", None),
        P("dp", "expert", None, None),
        P("expert", None, "dp"),
        P("expert", "dp", None),
    )
    return jax.shard_map(
        per_device, mesh=mesh, in_specs=in_specs, out_specs=out_specs, check_vma=False
    )
```

profile of v0, /device:TPU:1, one launch (start us, length us, event | category | flops | bytes accessed | tf_op | source)
XLA Modules:
  0.0 219.0 jit_solution(17717711683582613230)
XLA Ops:
  7.2 0.7 all-gather.5.cloned.1.call-update
  8.0 0.7 all-gather.7.cloned.1.call-update
  8.7 1.0 fusion.224
  9.7 2.6 %collective-permute-start = (bf16[4,16,768]{2,1,0:T(8,128)(2,1)S(1)}, bf16[4,16,768]{2,1,0:T(8,128)(2,1)S(1)}, u32[]{:S(2)}, u32[]{:S(2)}) collective-permute-start(bf16[4,16,768]{2,1,0:T(8,128)(2,1)S(1)} %get-tuple-element.38), channel_id=1, source_target_pairs={{0,1},{1,2},{2,3},{3,4},{4,5},{5,6},{6,7},{7,0},{8,9},{9,10},{10,1... | collective-permute-start | bytes 294920 | tf_op jit(solution)/shard_map/ppermute | solution.py:16
  12.3 4.3 %collective-permute-start.1 = (bf16[4,16,768]{2,1,0:T(8,128)(2,1)S(1)}, bf16[4,16,768]{2,1,0:T(8,128)(2,1)S(1)}, u32[]{:S(2)}, u32[]{:S(2)}) collective-permute-start(bf16[4,16,768]{2,1,0:T(8,128)(2,1)S(1)} %get-tuple-element.37), channel_id=1, source_target_pairs={{1,0},{2,1},{3,2},{4,3},{5,4},{6,5},{7,6},{0,7},{9,8},{10,9},{11,1... | collective-permute-start | bytes 294920 | tf_op jit(solution)/shard_map/ppermute | solution.py:19
  16.6 0.8 copy.27
  17.5 0.1 eq.40
  17.7 0.6 reduce-window.6
  18.3 0.2 slice_reduce_fusion
  18.7 0.9 constant_dynamic-update-slice_fusion.1
  19.7 10.3 %collective-permute-start.3 = (bf16[16,4,768]{2,1,0:T(4,128)(2,1)S(1)}, bf16[16,4,768]{2,1,0:T(4,128)(2,1)S(1)}, u32[]{:S(2)}, u32[]{:S(2)}) collective-permute-start(bf16[16,4,768]{2,1,0:T(4,128)(2,1)S(1)} %get-tuple-element.34), channel_id=1, source_target_pairs={{8,0},{16,8},{24,16},{32,24},{40,32},{48,40},{56,48},{64,56},{72,6... | collective-permute-start | bytes 294920 | tf_op jit(solution)/shard_map/ppermute | solution.py:19
  30.0 1.9 collective-permute-start.2
  31.9 0.6 fusion.225
  33.9 4.8 %collective-permute-done.2 = bf16[16,4,768]{2,1,0:T(4,128)(2,1)S(1)} collective-permute-done((bf16[16,4,768]{2,1,0:T(4,128)(2,1)S(1)}, bf16[16,4,768]{2,1,0:T(4,128)(2,1)S(1)}, u32[]{:S(2)}, u32[]{:S(2)}) %collective-permute-start.2) | collective-permute-done | bytes 98336 | tf_op jit(solution)/shard_map/ppermute | solution.py:16
  38.7 0.3 fusion.220
  39.1 0.2 multiply_reduce_fusion.1
  39.5 0.2 broadcast_in_dim.8
  39.7 0.1 reshape.407
  39.9 0.3 convolution_convert_fusion.1
  40.2 0.2 reshape.408
  40.4 24.0 %all_to_all.20 = bf16[64,5,768]{2,1,0:T(8,128)(2,1)S(1)} all-to-all(bf16[64,5,768]{2,1,0:T(8,128)(2,1)S(1)} %reshape.408), channel_id=1, replica_groups=mesh['expert'=64,'dp'=8] {'expert'}, dimensions={0} | all-to-all | bytes 983040 | tf_op jit(solution)/shard_map/all_to_all | solution.py:58
  64.4 1.0 reshape_transpose_reshape.14
  65.5 0.3 mul.221
  65.8 0.5 mul.222
  66.5 0.1 mul.219
  66.6 1.1 convolution_convert_fusion
  67.7 1.3 reshape.414
  69.0 28.0 %all_to_all.21 = bf16[64,5,768]{2,1,0:T(8,128)(2,1)S(1)} all-to-all(bf16[64,5,768]{2,1,0:T(8,128)(2,1)S(1)} %reshape.414), channel_id=1, replica_groups=mesh['expert'=64,'dp'=8] {'expert'}, dimensions={0} | all-to-all | bytes 983040 | tf_op jit(solution)/shard_map/all_to_all | solution.py:58
  97.0 1.0 reshape_transpose_reshape.15
  98.0 0.2 reshape.415
  98.2 0.2 reshape.409
  98.5 4.1 %fusion.16 = f32[320,1536]{1,0:T(8,128)} fusion(bf16[320,768]{1,0:T(8,128)(2,1)S(1)} %reshape.409, bf16[1,768,1536]{1,2,0:T(8,128)(2,1)} %all-gather.5.cloned.1.call-done), kind=kOutput, calls=%fused_computation.22 | convolution fusion | flops 754974720 | bytes 4816896 | tf_op jit(solution)/shard_map/erd,edf->erf/dot_general | solution.py:72
  102.5 4.9 %fusion.46 = bf16[320,768]{1,0:T(8,128)(2,1)S(1)} fusion(bf16[1,768,1536]{1,2,0:T(8,128)(2,1)} %all-gather.5.cloned.1.call-done, bf16[320,768]{1,0:T(8,128)(2,1)S(1)} %reshape.415, bf16[1,1536,768]{2,1,0:T(8,128)(2,1)} %all-gather.7.cloned.1.call-done, f32[320,1536]{1,0:T(8,128)} %fusion.16), kind=kOutput, calls=%fused_computation.68 | convolution fusion | flops 1515110400 | bytes 7667712 | tf_op jit(solution)/shard_map/erf,edf->erd/dot_general | solution.py:83
  107.5 1.1 reshape_transpose_reshape.13
  108.6 8.5 %all-to-all-start.3 = ((bf16[64,5,768]{2,1,0:T(8,128)(2,1)}), bf16[64,5,768]{2,1,0:T(8,128)(2,1)S(1)}, u32[]{:S(2)}, u32[]{:S(2)}) async-start(bf16[64,5,768]{2,1,0:T(8,128)(2,1)} %reshape_transpose_reshape.13), calls=%async_computation.3 | async-start | bytes 1572864 | tf_op jit(solution)/shard_map/all_to_all | solution.py:65
  117.1 7.3 %fusion.49 = bf16[320,768]{1,0:T(8,128)(2,1)S(1)} fusion(bf16[1,1536,768]{2,1,0:T(8,128)(2,1)} %all-gather.7.cloned.1.call-done, f32[320,1536]{1,0:T(8,128)} %fusion.16), kind=kOutput, calls=%fused_computation.69 | convolution fusion | flops 787169280 | bytes 4816896 | tf_op jit(solution)/shard_map/erf,efd->erd/dot_general | solution.py:74
  124.4 1.2 reshape_transpose_reshape.12
  125.6 11.0 %all-to-all-done.3 = bf16[64,5,768]{2,1,0:T(8,128)(2,1)S(1)} async-done(((bf16[64,5,768]{2,1,0:T(8,128)(2,1)}), bf16[64,5,768]{2,1,0:T(8,128)(2,1)S(1)}, u32[]{:S(2)}, u32[]{:S(2)}) %all-to-all-start.3) | async-done | bytes 491552 | tf_op jit(solution)/shard_map/all_to_all | solution.py:65
  136.5 8.4 %all-to-all-start.1 = ((bf16[64,5,768]{2,1,0:T(8,128)(2,1)}), bf16[64,5,768]{2,1,0:T(8,128)(2,1)S(1)}, u32[]{:S(2)}, u32[]{:S(2)}) async-start(bf16[64,5,768]{2,1,0:T(8,128)(2,1)} %reshape_transpose_reshape.12), calls=%async_computation.1 | async-start | bytes 1572864 | tf_op jit(solution)/shard_map/all_to_all | solution.py:65
  148.0 0.1 copy.31
  148.4 0.2 reshape.416
  148.6 1.2 gather_fusion.1
  149.8 0.2 reshape.450
  149.9 14.5 %all-to-all-done.1 = bf16[64,5,768]{2,1,0:T(8,128)(2,1)S(1)} async-done(((bf16[64,5,768]{2,1,0:T(8,128)(2,1)}), bf16[64,5,768]{2,1,0:T(8,128)(2,1)S(1)}, u32[]{:S(2)}, u32[]{:S(2)}) %all-to-all-start.1) | async-done | bytes 491552 | tf_op jit(solution)/shard_map/all_to_all | solution.py:65
  164.5 0.2 reshape.412
  164.7 1.2 gather_fusion
  165.9 0.2 reshape.446
  166.0 0.8 fusion.125
  166.8 2.3 %fusion.219 = (f32[128]{0:T(128)S(1)}, f32[128,1,768]{2,1,0:T(1,128)S(1)}, f32[128,1,768]{2,1,0:T(1,128)S(1)}, f32[128,1,768]{2,1,0:T(1,128)}) fusion(f32[128,2,768]{2,1,0:T(2,128)S(1)} %get-tuple-element.39, f32[128,2,768]{2,1,0:T(2,128)S(1)} %get-tuple-element.40), kind=kLoop, calls=%fused_computation.271 | loop fusion | flops 196480 | bytes 2753024 | tf_op jit(solution)/shard_map/reduce_sum | solution.py:144
  169.2 0.2 fusion.126
  169.6 1.0 copy.37
  170.6 0.2 fusion.130
  170.8 6.3 %collective-permute-start.5 = (bf16[4,16,768]{2,1,0:T(8,128)(2,1)S(1)}, bf16[4,16,768]{2,1,0:T(8,128)(2,1)S(1)}, u32[]{:S(2)}, u32[]{:S(2)}) collective-permute-start(bf16[4,16,768]{2,1,0:T(8,128)(2,1)S(1)} %bitcast.125), channel_id=1, source_target_pairs={{1,0},{2,1},{3,2},{4,3},{5,4},{6,5},{7,6},{0,7},{9,8},{10,9},{11,1... | collective-permute-start | bytes 294920 | tf_op jit(solution)/shard_map/ppermute | solution.py:19
  177.1 3.5 %collective-permute-start.4 = (bf16[4,16,768]{2,1,0:T(8,128)(2,1)S(1)}, bf16[4,16,768]{2,1,0:T(8,128)(2,1)S(1)}, u32[]{:S(2)}, u32[]{:S(2)}) collective-permute-start(bf16[4,16,768]{2,1,0:T(8,128)(2,1)S(1)} %bitcast.124), channel_id=1, source_target_pairs={{0,1},{1,2},{2,3},{3,4},{4,5},{5,6},{6,7},{7,0},{8,9},{9,10},{10,1... | collective-permute-start | bytes 294920 | tf_op jit(solution)/shard_map/ppermute | solution.py:16
  180.7 0.9 add_convert_fusion
  181.6 1.4 collective-permute-done.5
  183.0 3.1 %collective-permute-start.6 = (bf16[16,4,768]{2,1,0:T(4,128)(2,1)S(1)}, bf16[16,4,768]{2,1,0:T(4,128)(2,1)S(1)}, u32[]{:S(2)}, u32[]{:S(2)}) collective-permute-start(bf16[16,4,768]{2,1,0:T(4,128)(2,1)S(1)} %get-tuple-element.30), channel_id=1, source_target_pairs={{0,8},{8,16},{16,24},{24,32},{32,40},{40,48},{48,56},{56,64},{64,7... | collective-permute-start | bytes 294920 | tf_op jit(solution)/shard_map/ppermute | solution.py:16
  186.2 5.7 %collective-permute-start.7 = (bf16[16,4,768]{2,1,0:T(4,128)(2,1)S(1)}, bf16[16,4,768]{2,1,0:T(4,128)(2,1)S(1)}, u32[]{:S(2)}, u32[]{:S(2)}) collective-permute-start(bf16[16,4,768]{2,1,0:T(4,128)(2,1)S(1)} %get-tuple-element.29), channel_id=1, source_target_pairs={{8,0},{16,8},{24,16},{32,24},{40,32},{48,40},{56,48},{64,56},{72,6... | collective-permute-start | bytes 294920 | tf_op jit(solution)/shard_map/ppermute | solution.py:19
  191.9 0.8 multiply_reduce_fusion
  192.6 0.6 copy.36
  193.3 1.3 fusion.138
  194.6 3.6 %fusion.5 = f32[2560,192]{0,1:T(8,128)S(1)} fusion(bf16[1,2560,768]{2,1,0:T(8,128)(2,1)} %all-gather.9.cloned.1.call-done, bf16[1,768,192]{1,2,0:T(8,128)(2,1)S(1)} %copy-done.2), kind=kOutput, calls=%fused_computation.8 | convolution fusion | flops 754974720 | bytes 6193152 | tf_op jit(solution)/shard_map/erd,edf->erf/dot_general | solution.py:156
  198.2 6.4 %fusion.52 = f32[1,768,192]{1,2,0:T(8,128)} fusion(bf16[1,2560,768]{2,1,0:T(8,128)(2,1)} %all-gather.9.cloned.1.call-done, bf16[1,2560,768]{2,1,0:T(8,128)(2,1)} %all-gather.11.cloned.1.call-done, f32[2560,192]{0,1:T(8,128)S(1)} %fusion.5, bf16[1,192,768]{2,1,0:T(8,128)(2,1)S(1)} %copy-done.3), kind=kOutput, calls=%fused_computation.72 | convolution fusion | flops 1514864640 | bytes 10715136 | tf_op jit(solution)/shard_map/erd,erf->edf/dot_general | solution.py:160
  204.6 7.9 %fusion.55 = f32[1,192,768]{2,1,0:T(8,128)} fusion(bf16[1,2560,768]{2,1,0:T(8,128)(2,1)} %all-gather.11.cloned.1.call-done, f32[2560,192]{0,1:T(8,128)S(1)} %fusion.5), kind=kOutput, calls=%fused_computation.73 | convolution fusion | flops 786923520 | bytes 6488064 | tf_op jit(solution)/shard_map/erf,erd->efd/dot_general | solution.py:161
  (65 shorter events, 2.1 us)
Async XLA Ops:
  7.2 24.8 %copy-start.7 = (s32[2]{0:T(128)S(1)}, s32[2]{0:T(128)}, u32[]{:S(2)}) copy-start(s32[2]{0:T(128)} %param.15) | copy-start | bytes 28
  7.2 31.5 %copy-start.4 = (bf16[8,16,768]{2,1,0:T(8,128)(2,1)S(1)}, bf16[8,16,768]{2,1,0:T(8,128)(2,1)}, u32[]{:S(2)}) copy-start(bf16[8,16,768]{2,1,0:T(8,128)(2,1)} %param.11) | copy-start | bytes 589828
  7.2 91.3 %all-gather.5.cloned.1.call-start = ((), (), s32[]{:S(2)}) async-start(), calls=%async_computation.4 | async-start | bytes 2654208 | tf_op jit(solution)/shard_map/all_gather | solution.py:119
  7.9 94.6 %all-gather.7.cloned.1.call-start = ((), (), s32[]{:S(2)}) async-start(), calls=%async_computation.5 | async-start | bytes 2654208 | tf_op jit(solution)/shard_map/all_gather | solution.py:120
  8.7 185.9 %all-gather.9.cloned.1.call-start = ((), (), s32[]{:S(2)}) async-start(), calls=%async_computation.6 | async-start | bytes 4423680 | tf_op jit(solution)/shard_map/all_gather | solution.py:154
  9.7 9.0 %collective-permute-start = (bf16[4,16,768]{2,1,0:T(8,128)(2,1)S(1)}, bf16[4,16,768]{2,1,0:T(8,128)(2,1)S(1)}, u32[]{:S(2)}, u32[]{:S(2)}) collective-permute-start(bf16[4,16,768]{2,1,0:T(8,128)(2,1)S(1)} %get-tuple-element.38), channel_id=1, source_target_pairs={{0,1},{1,2},{2,3},{3,4},{4,5},{5,6},{6,7},{7,0},{8,9},{9,10},{10,1... | collective-permute-start | bytes 294920 | tf_op jit(solution)/shard_map/ppermute | solution.py:16
  12.3 7.3 %collective-permute-start.1 = (bf16[4,16,768]{2,1,0:T(8,128)(2,1)S(1)}, bf16[4,16,768]{2,1,0:T(8,128)(2,1)S(1)}, u32[]{:S(2)}, u32[]{:S(2)}) collective-permute-start(bf16[4,16,768]{2,1,0:T(8,128)(2,1)S(1)} %get-tuple-element.37), channel_id=1, source_target_pairs={{1,0},{2,1},{3,2},{4,3},{5,4},{6,5},{7,6},{0,7},{9,8},{10,9},{11,1... | collective-permute-start | bytes 294920 | tf_op jit(solution)/shard_map/ppermute | solution.py:19
  19.7 14.1 %collective-permute-start.3 = (bf16[16,4,768]{2,1,0:T(4,128)(2,1)S(1)}, bf16[16,4,768]{2,1,0:T(4,128)(2,1)S(1)}, u32[]{:S(2)}, u32[]{:S(2)}) collective-permute-start(bf16[16,4,768]{2,1,0:T(4,128)(2,1)S(1)} %get-tuple-element.34), channel_id=1, source_target_pairs={{8,0},{16,8},{24,16},{32,24},{40,32},{48,40},{56,48},{64,56},{72,6... | collective-permute-start | bytes 294920 | tf_op jit(solution)/shard_map/ppermute | solution.py:19
  30.0 8.7 %collective-permute-start.2 = (bf16[16,4,768]{2,1,0:T(4,128)(2,1)S(1)}, bf16[16,4,768]{2,1,0:T(4,128)(2,1)S(1)}, u32[]{:S(2)}, u32[]{:S(2)}) collective-permute-start(bf16[16,4,768]{2,1,0:T(4,128)(2,1)S(1)} %get-tuple-element.33), channel_id=1, source_target_pairs={{0,8},{8,16},{16,24},{24,32},{32,40},{40,48},{48,56},{56,64},{64,7... | collective-permute-start | bytes 294920 | tf_op jit(solution)/shard_map/ppermute | solution.py:16
  40.4 25.1 %copy-start = (bf16[8,16,768]{2,1,0:T(8,128)(2,1)S(1)}, bf16[8,16,768]{2,1,0:T(8,128)(2,1)}, u32[]{:S(2)}) copy-start(bf16[8,16,768]{2,1,0:T(8,128)(2,1)} %param.12) | copy-start | bytes 589828
  65.4 1.0 copy-start.6
  65.4 132.8 %all-gather.11.cloned.1.call-start = ((), (), s32[]{:S(2)}) async-start(), calls=%async_computation.7 | async-start | bytes 4423680 | tf_op jit(solution)/shard_map/all_gather | solution.py:155
  108.6 28.0 %all-to-all-start.3 = ((bf16[64,5,768]{2,1,0:T(8,128)(2,1)}), bf16[64,5,768]{2,1,0:T(8,128)(2,1)S(1)}, u32[]{:S(2)}, u32[]{:S(2)}) async-start(bf16[64,5,768]{2,1,0:T(8,128)(2,1)} %reshape_transpose_reshape.13), calls=%async_computation.3 | async-start | bytes 1572864 | tf_op jit(solution)/shard_map/all_to_all | solution.py:65
  124.4 23.4 %copy-start.5 = (s32[1,1,128,2]{2,3,1,0:T(2,128)S(1)}, s32[1,1,128,2]{2,3,1,0:T(2,128)}, u32[]{:S(2)}) copy-start(s32[1,1,128,2]{2,3,1,0:T(2,128)} %param.13) | copy-start | bytes 3076
  136.5 27.9 %all-to-all-start.1 = ((bf16[64,5,768]{2,1,0:T(8,128)(2,1)}), bf16[64,5,768]{2,1,0:T(8,128)(2,1)S(1)}, u32[]{:S(2)}, u32[]{:S(2)}) async-start(bf16[64,5,768]{2,1,0:T(8,128)(2,1)} %reshape_transpose_reshape.12), calls=%async_computation.1 | async-start | bytes 1572864 | tf_op jit(solution)/shard_map/all_to_all | solution.py:65
  170.8 12.1 %collective-permute-start.5 = (bf16[4,16,768]{2,1,0:T(8,128)(2,1)S(1)}, bf16[4,16,768]{2,1,0:T(8,128)(2,1)S(1)}, u32[]{:S(2)}, u32[]{:S(2)}) collective-permute-start(bf16[4,16,768]{2,1,0:T(8,128)(2,1)S(1)} %bitcast.125), channel_id=1, source_target_pairs={{1,0},{2,1},{3,2},{4,3},{5,4},{6,5},{7,6},{0,7},{9,8},{10,9},{11,1... | collective-permute-start | bytes 294920 | tf_op jit(solution)/shard_map/ppermute | solution.py:19
  177.1 5.8 %collective-permute-start.4 = (bf16[4,16,768]{2,1,0:T(8,128)(2,1)S(1)}, bf16[4,16,768]{2,1,0:T(8,128)(2,1)S(1)}, u32[]{:S(2)}, u32[]{:S(2)}) collective-permute-start(bf16[4,16,768]{2,1,0:T(8,128)(2,1)S(1)} %bitcast.124), channel_id=1, source_target_pairs={{0,1},{1,2},{2,3},{3,4},{4,5},{5,6},{6,7},{7,0},{8,9},{9,10},{10,1... | collective-permute-start | bytes 294920 | tf_op jit(solution)/shard_map/ppermute | solution.py:16
  181.6 16.6 %copy-start.1 = (bf16[8,16,768]{2,1,0:T(8,128)(2,1)}, bf16[8,16,768]{2,1,0:T(8,128)(2,1)S(1)}, u32[]{:S(2)}) copy-start(bf16[8,16,768]{2,1,0:T(8,128)(2,1)S(1)} %get-tuple-element.31) | copy-start | bytes 589828
  181.6 13.0 %copy-start.2 = (bf16[1,768,192]{1,2,0:T(8,128)(2,1)S(1)}, bf16[1,768,192]{1,2,0:T(8,128)(2,1)}, u32[]{:S(2)}) copy-start(bf16[1,768,192]{1,2,0:T(8,128)(2,1)} %param.16) | copy-start | bytes 884740
  183.0 10.3 %collective-permute-start.6 = (bf16[16,4,768]{2,1,0:T(4,128)(2,1)S(1)}, bf16[16,4,768]{2,1,0:T(4,128)(2,1)S(1)}, u32[]{:S(2)}, u32[]{:S(2)}) collective-permute-start(bf16[16,4,768]{2,1,0:T(4,128)(2,1)S(1)} %get-tuple-element.30), channel_id=1, source_target_pairs={{0,8},{8,16},{16,24},{24,32},{32,40},{40,48},{48,56},{56,64},{64,7... | collective-permute-start | bytes 294920 | tf_op jit(solution)/shard_map/ppermute | solution.py:16
  186.2 7.1 %collective-permute-start.7 = (bf16[16,4,768]{2,1,0:T(4,128)(2,1)S(1)}, bf16[16,4,768]{2,1,0:T(4,128)(2,1)S(1)}, u32[]{:S(2)}, u32[]{:S(2)}) collective-permute-start(bf16[16,4,768]{2,1,0:T(4,128)(2,1)S(1)} %get-tuple-element.29), channel_id=1, source_target_pairs={{8,0},{16,8},{24,16},{32,24},{40,32},{48,40},{56,48},{64,56},{72,6... | collective-permute-start | bytes 294920 | tf_op jit(solution)/shard_map/ppermute | solution.py:19
  194.6 3.6 %copy-start.3 = (bf16[1,192,768]{2,1,0:T(8,128)(2,1)S(1)}, bf16[1,192,768]{2,1,0:T(8,128)(2,1)}, u32[]{:S(2)}) copy-start(bf16[1,192,768]{2,1,0:T(8,128)(2,1)} %param.17) | copy-start | bytes 884740
Sparse Core Ops, SparseCore 0:
  10.1 36.8 all-gather.4
  49.2 31.5 all-gather.6
  83.5 36.8 all-gather.8
  122.9 36.3 all-gather.10
where the time goes:
time: 222 us; the launch traced here: 219 us
  starting transfers between devices  54.9 us (25%)
  blocking collectives  52 us (23%)
  matrix products  35.5 us (16%)
  waiting for transfers between devices  33.2 us (15%)
  between operations  18.1 us (8%)
  local copies, waits for them, and re-layouts  17.3 us (8%)
  other arithmetic  8.04 us (4%)
    all_to_all x2, blocking collectives, to_experts(): lax.all_to_all(before_send(buffer, n_src, local_count), 'expert', split_a...  52 us
    ppermute x4, starting transfers between devices, with_halo(): lax.ppermute(lax.slice_in_dim(block, 0, width, axis=dim), axis, backward)  26.6 us
    all_to_all x2, waiting for transfers between devices, from_experts(): lax.all_to_all(before_return(rows, n_src, local_count), 'expert', split_a...  25.5 us
    all_to_all x2, starting transfers between devices, from_experts(): lax.all_to_all(before_return(rows, n_src, local_count), 'expert', split_a...  17 us
    ppermute x4, starting transfers between devices, with_halo(): lax.ppermute(lax.slice_in_dim(block, block.shape[dim] - width, None, axis...  11.2 us
    dot_general x1, matrix products, per_device(): jnp.einsum('erf,erd->efd', a_piece, g_piece, preferred_element_type=jnp.f...  7.9 us
    dot_general x1, matrix products, forward_experts(): jnp.einsum('erf,efd->erd', act, full_out, preferred_element_type=jnp.floa...  7.27 us
    dot_general x1, matrix products, per_device(): jnp.einsum('erd,erf->edf', u_piece, p_piece, preferred_element_type=jnp.f...  6.38 us
  transfers between devices with their start and end apart: 14, of which 4 were waited for; matrix products, arithmetic and copies ran while one was open for 21% of the time, Pallas kernels for 0%

commit v1 on v0

v1 whole, which is shorter than its diff:
```python
import functools

import jax
import jax.numpy as jnp
from jax import lax
from jax.experimental import pallas as pl
from jax.experimental.pallas import tpu as pltpu
from jax.sharding import PartitionSpec as P

CAP = 5
WIRE_ROWS = 8
WIDE = 512
EPS = 1e-05
VMEM = pl.BlockSpec(memory_space=pltpu.VMEM)
SMEM = pl.BlockSpec(memory_space=pltpu.SMEM)


def iota(shape, dim):
    return lax.broadcasted_iota(jnp.int32, shape, dim)


def ones_where(mask):
    return jnp.where(mask, 1.0, 0.0).astype(jnp.bfloat16)


def dot(a, b):
    return jnp.dot(a, b, preferred_element_type=jnp.float32)


def dot_t(a, b):
    return lax.dot_general(a, b, (((1,), (1,)), ((), ())), preferred_element_type=jnp.float32)


def t_dot(a, b):
    return lax.dot_general(a, b, (((0,), (0,)), ((), ())), preferred_element_type=jnp.float32)


def call(body, outs, *args, flops=0, traffic=0, specs=None, **kw):
    return pl.pallas_call(
        body,
        out_shape=outs,
        in_specs=[VMEM] * len(args) if specs is None else specs,
        out_specs=jax.tree.map(lambda _: VMEM, outs),
        compiler_params=pltpu.CompilerParams(vmem_limit_bytes=32 * 1024 * 1024),
        cost_estimate=pl.CostEstimate(flops=flops, bytes_accessed=traffic, transcendentals=0),
        **kw,
    )(*args)


def wire_masks(row, n):
    at = iota((row.shape[0], n), 1)
    pos = row & 7
    tail = row - pos + CAP + (pos >> 1)
    odd = (pos & 1) == 1
    left = jnp.where(odd, -1, tail)
    right = jnp.where(odd, tail, -1)
    return ones_where(at == row), ones_where(at == left), ones_where(at == right)


def from_wire(masks, wire):
    head, left, right = masks
    half = WIDE // 2
    return (
        dot(head, wire),
        dot(left, wire[:, :half]) + dot(right, wire[:, half:]),
    )


def to_wire(masks, rows, turned):
    head, left, right = masks
    f = t_dot if turned else dot
    tail = rows[:, WIDE:]
    return f(head, rows[:, :WIDE]) + jnp.concatenate([f(left, tail), f(right, tail)], axis=1)


def dispatch_g(ids_ref, gates_ref, dout_ref, sent_ref, row_ref):
    tokens = ids_ref.shape[0]
    n = sent_ref.shape[0]
    experts = n // WIRE_ROWS
    ids = ids_ref[...]
    lane = iota((tokens, experts), 1)
    first = jnp.where(ids[:, 0:1] == lane, 1.0, 0.0)
    second = jnp.where(ids[:, 1:2] == lane, 1.0, 0.0)
    lower = ones_where(iota((tokens, tokens), 0) > iota((tokens, tokens), 1))
    before = dot(lower, (first + second).astype(jnp.bfloat16))
    pos0 = jnp.sum(before * first, axis=1, keepdims=True).astype(jnp.int32)
    pos1 = jnp.sum(before * second, axis=1, keepdims=True).astype(jnp.int32)
    row0 = ids[:, 0:1] * WIRE_ROWS + pos0
    row1 = ids[:, 1:2] * WIRE_ROWS + pos1
    row_ref[:, 0:1] = row0
    row_ref[:, 1:2] = row1
    dout = dout_ref[...].astype(jnp.float32)
    gates = gates_ref[...]
    g = jnp.concatenate(
        [(gates[:, 0:1] * dout).astype(jnp.bfloat16), (gates[:, 1:2] * dout).astype(jnp.bfloat16)], axis=0
    )
    row = jnp.concatenate([row0, row1], axis=0)
    sent_ref[...] = to_wire(wire_masks(row, n), g, True).astype(jnp.bfloat16)


def normalize(x):
    m = jnp.mean(x, axis=-1, keepdims=True)
    c = x - m
    r = lax.rsqrt(jnp.mean(c * c, axis=-1, keepdims=True) + EPS)
    return c * r, r


def shifted(i, j, tr, tc, own, row_edge, col_edge, corner):
    i_in = (i >= 0) & (i < tr)
    j_in = (j >= 0) & (j < tc)
    ei = jnp.where(i < 0, i + 4, i - tr)
    ej = jnp.where(j < 0, j + 4, j - tc)

    def pick(mask, index, src):
        index = jnp.where(mask, index, -1)
        return dot(ones_where(index == iota((index.shape[0], src.shape[0]), 1)), src)

    return (
        pick(i_in & j_in, i * tc + j, own)
        + pick((~i_in) & j_in, ei * tc + j, row_edge)
        + pick(i_in & (~j_in), i * 4 + ej, col_edge)
        + pick((~i_in) & (~j_in), ei * 4 + ej, corner)
    )


def dispatch_u(tr, tc, off_ref, row_ref, short_ref, attn_ref, up_ref, left_ref, corner_ref, sent_ref, x_ref):
    tokens = short_ref.shape[0]
    t = iota((tokens, 1), 0)
    i = t // tc - off_ref[0]
    j = t % tc - off_ref[1]
    rolled = shifted(i, j, tr, tc, attn_ref[...], up_ref[...], left_ref[...], corner_ref[...])
    x = short_ref[...].astype(jnp.float32) + rolled
    x_ref[...] = x
    xhat, _ = normalize(x)
    u = xhat.astype(jnp.bfloat16)
    u = jnp.concatenate([u, u], axis=0)
    row = jnp.concatenate([row_ref[:, 0:1], row_ref[:, 1:2]], axis=0)
    sent_ref[...] = to_wire(wire_masks(row, sent_ref.shape[0]), u, True).astype(jnp.bfloat16)


def experts_body(rg_ref, ru_ref, w_ref, q_ref, y_ref, grad_ref, u_s, g_s, q_s, y_s):
    step = pl.program_id(0)
    n = rg_ref.shape[0]
    peers = n // WIRE_ROWS
    slots = peers * CAP

    @pl.when(step == 0)
    def _():
        s = iota((slots, 1), 0)
        masks = wire_masks((s % peers) * WIRE_ROWS + s // peers, n)
        for src, dst in ((ru_ref, u_s), (rg_ref, g_s)):
            head, tail = from_wire(masks, src[...])
            dst[:, :WIDE] = head.astype(jnp.bfloat16)
            dst[:, WIDE:] = tail.astype(jnp.bfloat16)

    u = u_s[...]
    g = g_s[...]
    block, _, part, width = w_ref.shape
    w1 = w_ref[:, 0].reshape(block * part, width)
    w2 = w_ref[:, 1].reshape(block * part, width)
    h = dot_t(u, w1)
    da = dot_t(g, w2)
    cdf = 0.5 * (1.0 + lax.erf(h * 0.7071067811865476))
    pdf = jnp.exp(-0.5 * h * h) * 0.3989422804014327
    a = (h * cdf).astype(jnp.bfloat16)
    p = (da * (cdf + h * pdf)).astype(jnp.bfloat16)
    q = dot(p, w1)
    y = dot(a, w2)
    grad_ref[:, 0] = t_dot(p, u).astype(jnp.bfloat16).reshape(block, part, width)
    grad_ref[:, 1] = t_dot(a, g).astype(jnp.bfloat16).reshape(block, part, width)

    @pl.when(step == 0)
    def _():
        q_s[...] = q
        y_s[...] = y

    @pl.when(step > 0)
    def _():
        q_s[...] += q
        y_s[...] += y

    @pl.when(step == pl.num_programs(0) - 1)
    def _():
        s = iota((slots, 1), 0)
        masks = wire_masks((s % peers) * WIRE_ROWS + s // peers, n)
        q_ref[...] = to_wire(masks, q_s[...].astype(jnp.bfloat16), True).astype(jnp.bfloat16)
        y_ref[...] = to_wire(masks, y_s[...].astype(jnp.bfloat16), True).astype(jnp.bfloat16)


def experts(rg, ru, w):
    n = rg.shape[0]
    parts, _, part, width = w.shape
    slots = n // WIRE_ROWS * CAP
    block = 2
    hidden = parts * part
    whole = pl.BlockSpec((n, WIDE), lambda i: (0, 0))
    piece = pl.BlockSpec((block, 2, part, width), lambda i: (i, 0, 0, 0))
    wire = jax.ShapeDtypeStruct((n, WIDE), jnp.bfloat16)
    return pl.pallas_call(
        experts_body,
        grid=(parts // block,),
        out_shape=(wire, wire, jax.ShapeDtypeStruct(w.shape, jnp.bfloat16)),
        in_specs=[whole, whole, piece],
        out_specs=(whole, whole, piece),
        scratch_shapes=[
            pltpu.VMEM((slots, width), jnp.bfloat16),
            pltpu.VMEM((slots, width), jnp.bfloat16),
            pltpu.VMEM((slots, width), jnp.float32),
            pltpu.VMEM((slots, width), jnp.float32),
        ],
        compiler_params=pltpu.CompilerParams(
            dimension_semantics=("arbitrary",), vmem_limit_bytes=48 * 1024 * 1024
        ),
        cost_estimate=pl.CostEstimate(
            flops=12 * slots * hidden * width,
            bytes_accessed=8 * hidden * width,
            transcendentals=2 * slots * hidden,
        ),
    )(rg, ru, w)


def combine_q(tr, tc, rq_ref, row_ref, x_ref, dout_ref, ds_ref, up_ref, left_ref, corner_ref):
    wire = rq_ref[...]
    masks = [wire_masks(row_ref[:, k : k + 1], wire.shape[0]) for k in range(2)]
    both = tuple(a + b for a, b in zip(*masks))
    du = jnp.concatenate(from_wire(both, wire), axis=1)
    xhat, r = normalize(x_ref[...])
    dx = r * (
        du
        - jnp.mean(du, axis=-1, keepdims=True)
        - xhat * jnp.mean(du * xhat, axis=-1, keepdims=True)
    )
    ds = (dout_ref[...].astype(jnp.float32) + dx).astype(jnp.bfloat16)
    ds_ref[...] = ds
    up_ref[...] = ds[: 4 * tc]
    n = 4 * tr
    s = iota((n, 1), 0)
    edge = dot(ones_where((s // 4) * tc + s % 4 == iota((n, ds.shape[0]), 1)), ds).astype(jnp.bfloat16)
    left_ref[...] = edge
    corner_ref[...] = edge[:16]


def roll_back(tr, tc, off_ref, ds_ref, down_ref, right_ref, corner_ref, out_ref):
    t = iota((ds_ref.shape[0], 1), 0)
    i = t // tc + off_ref[0]
    j = t % tc + off_ref[1]
    out_ref[...] = shifted(
        i, j, tr, tc, ds_ref[...], down_ref[...], right_ref[...], corner_ref[...]
    ).astype(jnp.bfloat16)


def combine_y(ry_ref, row_ref, gates_ref, x_ref, dout_ref, out_ref, dg_ref):
    wire = ry_ref[...]
    dout = dout_ref[...].astype(jnp.float32)
    gates = gates_ref[...]
    total = x_ref[...]
    for k in range(2):
        y = jnp.concatenate(from_wire(wire_masks(row_ref[:, k : k + 1], wire.shape[0]), wire), axis=1)
        total = total + gates[:, k : k + 1] * y
        dg_ref[:, k : k + 1] = jnp.sum(dout * y, axis=-1, keepdims=True)
    out_ref[...] = total.astype(jnp.bfloat16)


def exchange(wire, n):
    wire = wire.reshape(n, WIRE_ROWS, WIDE)
    out = lax.all_to_all(wire, "expert", split_axis=0, concat_axis=0, tiled=True)
    return out.reshape(n * WIRE_ROWS, WIDE)


def edges(row_edge, col_edge, corner, step):
    n_dp, n_ex = lax.axis_size("dp"), lax.axis_size("expert")
    by_dp = [(i, (i + step) % n_dp) for i in range(n_dp)]
    by_ex = [(i, (i + step) % n_ex) for i in range(n_ex)]
    by_both = [
        (q * n_dp + p, (q + step) % n_ex * n_dp + (p + step) % n_dp)
        for q in range(n_ex)
        for p in range(n_dp)
    ]
    return (
        lax.ppermute(row_edge, "dp", by_dp),
        lax.ppermute(col_edge, "expert", by_ex),
        lax.ppermute(corner, ("expert", "dp"), by_both),
    )


def per_device(attn_win, shortcut, d_out, expert_ids, gate_probs, shift_offsets, w_in, w_out):
    tr, tc, width = attn_win.shape
    tokens = tr * tc
    n_ex = lax.axis_size("expert")
    n = n_ex * WIRE_ROWS
    bf16 = functools.partial(jax.ShapeDtypeStruct, dtype=jnp.bfloat16)
    f32 = functools.partial(jax.ShapeDtypeStruct, dtype=jnp.float32)
    ids = expert_ids.reshape(tokens, 2)
    gates = gate_probs.reshape(tokens, 2)
    dout = d_out.reshape(tokens, width)
    attn = attn_win.reshape(tokens, width)
    short = shortcut.reshape(tokens, width)

    w_own = jnp.concatenate([w_in.transpose(0, 2, 1), w_out], axis=0)[None]
    w_all = lax.all_gather(w_own, "dp", axis=0, tiled=True)

    col_edge = attn_win[:, tc - 4 :]
    up, left, corner = edges(
        attn_win[tr - 4 :].reshape(4 * tc, width),
        col_edge.reshape(tr * 4, width),
        col_edge[tr - 4 :].reshape(16, width),
        1,
    )
    sent_g, row = call(
        dispatch_g,
        (bf16((n, WIDE)), jax.ShapeDtypeStruct((tokens, 2), jnp.int32)),
        ids, gates, dout,
        flops=4 * 256 * n * WIDE, traffic=1 << 20,
    )
    rg = exchange(sent_g, n_ex)
    sent_u, x = call(
        functools.partial(dispatch_u, tr, tc),
        (bf16((n, WIDE)), f32((tokens, width))),
        shift_offsets, row, short, attn, up, left, corner,
        specs=[SMEM] + [VMEM] * 6,
        flops=4 * 256 * n * WIDE, traffic=1 << 21,
    )
    ru = exchange(sent_u, n_ex)
    q_wire, y_wire, grads = experts(rg, ru, w_all)
    rq = exchange(q_wire, n_ex)
    ry = exchange(y_wire, n_ex)
    grad = lax.psum_scatter(grads, "dp", scatter_dimension=0, tiled=True).astype(jnp.float32)
    grad_in = grad[:, 0].transpose(0, 2, 1)
    grad_out = grad[:, 1]
    ds, up_b, left_b, corner_b = call(
        functools.partial(combine_q, tr, tc),
        (bf16((tokens, width)), bf16((4 * tc, width)), bf16((4 * tr, width)), bf16((16, width))),
        rq, row, x, dout,
        flops=4 * tokens * n * WIDE, traffic=1 << 21,
    )
    down, right, corner_r = edges(up_b, left_b, corner_b, -1)
    block_out, d_gates = call(
        combine_y,
        (bf16((tokens, width)), f32((tokens, 2))),
        ry, row, gates, x, dout,
        flops=8 * tokens * n * WIDE, traffic=1 << 21,
    )
    d_attn = call(
        functools.partial(roll_back, tr, tc),
        bf16((tokens, width)),
        shift_offsets, ds, down, right, corner_r,
        specs=[SMEM] + [VMEM] * 4,
        flops=2 * tokens * 256 * width, traffic=1 << 19,
    )
    tile = (tr, tc, width)
    return (
        block_out.reshape(tile),
        ds.reshape(tile),
        d_attn.reshape(tile),
        d_gates.reshape(1, 1, tokens, 2),
        grad_in,
        grad_out,
    )


def solution(mesh):
    tile = P("dp", "expert", None)
    pairs = P("dp", "expert", None, None)
    first, second = P("expert", None, "dp"), P("expert", "dp", None)
    return jax.shard_map(
        per_device,
        mesh=mesh,
        in_specs=(tile, tile, tile, pairs, pairs, P(), first, second),
        out_specs=(tile, tile, tile, pairs, first, second),
        check_vma=False,
    )
```

time: 222 us -> 156 us (0.70)
  the two profiles are of different devices: /device:TPU:1 before, /device:TPU:10 now
where the time goes in v1:
time: 156 us; the launch traced here: 155 us
  blocking collectives  55 us (35%)
  starting transfers between devices  37.7 us (24%)
  Pallas kernels  20.5 us (13%)
  between operations  14.2 us (9%)
  waiting for transfers between devices  14.1 us (9%)
  local copies, waits for them, and re-layouts  10.4 us (7%)
  other arithmetic  3.06 us (2%)
    all_to_all x2, blocking collectives, exchange(): lax.all_to_all(wire, 'expert', split_axis=0, concat_axis=0, tiled=True)  55 us
    all_to_all x2, starting transfers between devices, exchange(): lax.all_to_all(wire, 'expert', split_axis=0, concat_axis=0, tiled=True)  21.8 us
    pallas_call x1, Pallas kernels, experts(): pl.pallas_call(experts_body, grid=(parts // block,), out_shape=(wire, wir...  13 us
    all_to_all x2, waiting for transfers between devices, exchange(): lax.all_to_all(wire, 'expert', split_axis=0, concat_axis=0, tiled=True)  12 us
    ppermute x2, starting transfers between devices, edges(): lax.ppermute(corner, ('expert', 'dp'), by_both)  10.1 us
    pallas_call x5, Pallas kernels, call(): pl.pallas_call(body, out_shape=outs, in_specs=[VMEM] * len(args) if specs...  7.53 us
    unnamed x17, local copies, waits for them, and re-layouts  6.58 us
    ppermute x2, starting transfers between devices, edges(): lax.ppermute(col_edge, 'expert', by_ex)  5.72 us
  transfers between devices with their start and end apart: 10, of which 3 were waited for; matrix products, arithmetic and copies ran while one was open for 3% of the time, Pallas kernels for 5%

profile of v1, /device:TPU:10, one launch (start us, length us, event | category | flops | bytes accessed | tf_op | source)
XLA Modules:
  0.0 154.8 jit_solution(1148033701645669646)
XLA Ops:
  7.2 0.0 all-gather.3.cloned.1.call-start
  7.2 1.9 %pad_maximum_fusion = bf16[2,192,768]{2,1,0:T(8,128)(2,1)} fusion(bf16[1,192,768]{2,1,0:T(8,128)(2,1)} %param.15, bf16[1,192,768]{2,1,0:T(8,128)(2,1)} %bitcast.42), kind=kLoop, calls=%fused_computation.2 | loop fusion | flops 294912 | bytes 1179648 | tf_op jit(solution)/shard_map/concatenate | solution.py:299
  9.1 0.0 all-gather.3.cloned.1.call-update
  9.2 0.8 copy.20
  9.9 0.8 copy.21
  10.7 0.0 copy-start
  10.7 0.9 copy-done
  11.7 1.8 %shard_map.127 = (bf16[512,512]{1,0:T(8,128)(2,1)}, s32[128,2]{1,0:T(8,128)S(1)}) custom-call(s32[128,2]{1,0:T(8,128)S(1)} %bitcast.40, f32[128,2]{1,0:T(8,128)S(1)} %bitcast.35, bf16[128,768]{1,0:T(8,128)(2,1)S(1)} %bitcast.28), custom_call_target="tpu_custom_call" | custom-call | flops 268435456 | bytes 1048576 | tf_op jit(solution)/shard_map/pallas_call | solution.py:39
  13.4 16.6 %all-to-all-start = ((bf16[64,8,512]{2,1,0:T(8,128)(2,1)}), bf16[64,8,512]{2,1,0:T(8,128)(2,1)S(1)}, u32[]{:S(2)}, u32[]{:S(2)}) async-start(bf16[64,8,512]{2,1,0:T(8,128)(2,1)} %bitcast.3), calls=%async_computation | async-start | bytes 1048576 | tf_op jit(solution)/shard_map/all_to_all | solution.py:266
  30.0 0.0 reduce-scatter.2.cloned.1.call-start
  30.1 0.9 slice.16
  31.0 0.0 collective-permute-start
  31.0 1.0 slice.17
  32.0 3.4 %collective-permute-start.1 = (bf16[32,768]{1,0:T(8,128)(2,1)S(1)}, bf16[32,768]{1,0:T(8,128)(2,1)S(1)}, u32[]{:S(2)}, u32[]{:S(2)}) collective-permute-start(bf16[32,768]{1,0:T(8,128)(2,1)S(1)} %reshape.80), channel_id=1, source_target_pairs={{0,8},{8,16},{16,24},{24,32},{32,40},{40,48},{48,56},{56,64},{64,7... | collective-permute-start | bytes 147464 | tf_op jit(solution)/shard_map/ppermute | solution.py:281
  35.4 0.8 slice.18
  36.2 4.2 %collective-permute-start.2 = (bf16[16,768]{1,0:T(8,128)(2,1)S(1)}, bf16[16,768]{1,0:T(8,128)(2,1)S(1)}, u32[]{:S(2)}, u32[]{:S(2)}) collective-permute-start(bf16[16,768]{1,0:T(8,128)(2,1)S(1)} %reshape.81), channel_id=1, source_target_pairs={{0,9},{1,10},{2,11},{3,12},{4,13},{5,14},{6,15},{7,8},{8,17},{9,18... | collective-permute-start | bytes 73736 | tf_op jit(solution)/shard_map/ppermute | solution.py:282
  40.5 2.0 %collective-permute-done.2.corner_ref = bf16[16,768]{1,0:T(8,128)(2,1)S(1)} collective-permute-done((bf16[16,768]{1,0:T(8,128)(2,1)S(1)}, bf16[16,768]{1,0:T(8,128)(2,1)S(1)}, u32[]{:S(2)}, u32[]{:S(2)}) %collective-permute-start.2) | collective-permute-done | bytes 24608 | tf_op jit(solution)/shard_map/ppermute | solution.py:282
  42.4 0.0 collective-permute-done.1.left_ref
  42.4 0.0 collective-permute-done.up_ref
  42.4 0.0 copy-start.3
  42.4 0.9 copy-done.3
  43.4 0.0 copy-start.4
  43.4 0.7 copy-done.4
  44.0 0.0 copy-start.6
  44.0 0.9 copy-done.6
  45.0 1.7 %shard_map.128 = (bf16[512,512]{1,0:T(8,128)(2,1)S(1)}, f32[128,768]{1,0:T(8,128)S(1)}) custom-call(s32[2]{0:T(128)S(1)} %copy-done.4, s32[128,2]{1,0:T(8,128)S(1)} %get-tuple-element.20.row_ref, bf16[128,768]{1,0:T(8,128)(2,1)S(1)} %bitcast.41, bf16[128,768]{1,0:T(8,128)(2,1)S(1)} %bitcast.38, bf16[64,768]{1,0:T(8,128)(2,1)S(1)} %collective-permute-done.up_ref, ...), custom_call_target="tpu_custom_call" | custom-call | flops 268435456 | bytes 2097152 | tf_op jit(solution)/shard_map/pallas_call | solution.py:39
  46.6 2.7 %all-to-all-done = bf16[64,8,512]{2,1,0:T(8,128)(2,1)S(1)} async-done(((bf16[64,8,512]{2,1,0:T(8,128)(2,1)}), bf16[64,8,512]{2,1,0:T(8,128)(2,1)S(1)}, u32[]{:S(2)}, u32[]{:S(2)}) %all-to-all-start) | async-done | bytes 524320 | tf_op jit(solution)/shard_map/all_to_all | solution.py:266
  49.4 30.4 %all_to_all.20 = bf16[64,8,512]{2,1,0:T(8,128)(2,1)S(1)} all-to-all(bf16[64,8,512]{2,1,0:T(8,128)(2,1)S(1)} %bitcast.33), channel_id=1, replica_groups=mesh['expert'=64,'dp'=8] {'expert'}, dimensions={0} | all-to-all | bytes 1048576 | tf_op jit(solution)/shard_map/all_to_all | solution.py:266
  79.8 0.0 all-gather.3.cloned.1.call-done
  79.8 13.0 %shard_map.129 = (bf16[512,512]{1,0:T(8,128)(2,1)S(1)}, bf16[512,512]{1,0:T(8,128)(2,1)}, bf16[8,2,192,768]{3,2,1,0:T(8,128)(2,1)}) custom-call(bf16[512,512]{1,0:T(8,128)(2,1)S(1)} %bitcast.31, bf16[512,512]{1,0:T(8,128)(2,1)S(1)} %bitcast.34, bf16[8,2,192,768]{3,2,1,0:T(8,128)(2,1)} %bitcast.45), custom_call_target="tpu_custom_call" | custom-call | flops 4529848320 | bytes 9437184 | tf_op jit(solution)/shard_map/pallas_call | solution.py:199
  92.7 0.0 copy-start.1
  92.7 0.0 copy-start.5
  92.7 0.0 reduce-scatter.2.cloned.1.call-update
  92.8 24.6 %all_to_all.21 = bf16[64,8,512]{2,1,0:T(8,128)(2,1)S(1)} all-to-all(bf16[64,8,512]{2,1,0:T(8,128)(2,1)S(1)} %bitcast.32), channel_id=1, replica_groups=mesh['expert'=64,'dp'=8] {'expert'}, dimensions={0} | all-to-all | bytes 1048576 | tf_op jit(solution)/shard_map/all_to_all | solution.py:266
  117.3 5.2 %all-to-all-start.2 = ((bf16[64,8,512]{2,1,0:T(8,128)(2,1)}), bf16[64,8,512]{2,1,0:T(8,128)(2,1)S(1)}, u32[]{:S(2)}, u32[]{:S(2)}) async-start(bf16[64,8,512]{2,1,0:T(8,128)(2,1)} %bitcast.12), calls=%async_computation.2 | async-start | bytes 1048576 | tf_op jit(solution)/shard_map/all_to_all | solution.py:266
  122.5 0.0 copy-done.1
  122.5 1.3 shard_map.131
  123.8 0.0 collective-permute-start.3
  123.8 2.4 %collective-permute-start.4 = (bf16[32,768]{1,0:T(8,128)(2,1)S(1)}, bf16[32,768]{1,0:T(8,128)(2,1)S(1)}, u32[]{:S(2)}, u32[]{:S(2)}) collective-permute-start(bf16[32,768]{1,0:T(8,128)(2,1)S(1)} %get-tuple-element.28), channel_id=1, source_target_pairs={{0,504},{8,0},{16,8},{24,16},{32,24},{40,32},{48,40},{56,48},{64,5... | collective-permute-start | bytes 147464 | tf_op jit(solution)/shard_map/ppermute | solution.py:281
  126.2 5.8 %collective-permute-start.5 = (bf16[16,768]{1,0:T(8,128)(2,1)S(1)}, bf16[16,768]{1,0:T(8,128)(2,1)S(1)}, u32[]{:S(2)}, u32[]{:S(2)}) collective-permute-start(bf16[16,768]{1,0:T(8,128)(2,1)S(1)} %get-tuple-element.29), channel_id=1, source_target_pairs={{0,511},{1,504},{2,505},{3,506},{4,507},{5,508},{6,509},{7,510},{8... | collective-permute-start | bytes 73736 | tf_op jit(solution)/shard_map/ppermute | solution.py:282
  132.0 9.3 %all-to-all-done.2 = bf16[64,8,512]{2,1,0:T(8,128)(2,1)S(1)} async-done(((bf16[64,8,512]{2,1,0:T(8,128)(2,1)}), bf16[64,8,512]{2,1,0:T(8,128)(2,1)S(1)}, u32[]{:S(2)}, u32[]{:S(2)}) %all-to-all-start.2) | async-done | bytes 524320 | tf_op jit(solution)/shard_map/all_to_all | solution.py:266
  141.3 1.2 shard_map.130
  142.6 0.6 copy.22
  143.2 0.0 collective-permute-done.5.corner_ref
  143.2 0.0 collective-permute-done.4.right_ref
  143.2 0.0 collective-permute-done.3.down_ref
  143.2 0.0 copy-done.5
  143.2 0.0 copy-start.2
  143.2 0.9 copy-done.2
  144.2 1.6 %shard_map.132 = bf16[128,768]{1,0:T(8,128)(2,1)} custom-call(s32[2]{0:T(128)S(1)} %copy-done.5, bf16[128,768]{1,0:T(8,128)(2,1)S(1)} %copy-done.2, bf16[64,768]{1,0:T(8,128)(2,1)S(1)} %collective-permute-done.3.down_ref, bf16[32,768]{1,0:T(8,128)(2,1)S(1)} %collective-permute-done.4.right_ref, bf16[16,768]{1,0:T(8,128)(2,1)S(1)} %collective-permute-done.5.corner_ref), custom_call_target="tpu_custom_call" | custom-call | flops 50331648 | bytes 524288 | tf_op jit(solution)/shard_map/pallas_call | solution.py:39
  145.7 0.0 reduce-scatter.2.cloned.1.call-done
  145.7 1.1 convert_element_type.3
  146.9 1.1 slice_bitcast_fusion
  (2 shorter events, 0.0 us)
Async XLA Ops:
  7.2 72.6 %all-gather.3.cloned.1.call-start = ((), (), s32[]{:S(2)}) async-start(), calls=%async_computation.6 | async-start | bytes 5308416 | tf_op jit(solution)/shard_map/all_gather | solution.py:300
  10.7 0.9 copy-start
  13.4 35.9 %all-to-all-start = ((bf16[64,8,512]{2,1,0:T(8,128)(2,1)}), bf16[64,8,512]{2,1,0:T(8,128)(2,1)S(1)}, u32[]{:S(2)}, u32[]{:S(2)}) async-start(bf16[64,8,512]{2,1,0:T(8,128)(2,1)} %bitcast.3), calls=%async_computation | async-start | bytes 1048576 | tf_op jit(solution)/shard_map/all_to_all | solution.py:266
  30.0 115.7 %reduce-scatter.2.cloned.1.call-start = ((), (), s32[]{:S(2)}) async-start(), calls=%async_computation.5 | async-start | bytes 5308416 | tf_op jit(solution)/shard_map/reduce_scatter | solution.py:327
  31.0 11.5 %collective-permute-start = (bf16[64,768]{1,0:T(8,128)(2,1)S(1)}, bf16[64,768]{1,0:T(8,128)(2,1)S(1)}, u32[]{:S(2)}, u32[]{:S(2)}) collective-permute-start(bf16[64,768]{1,0:T(8,128)(2,1)S(1)} %bitcast.44), channel_id=1, source_target_pairs={{0,1},{1,2},{2,3},{3,4},{4,5},{5,6},{6,7},{7,0},{8,9},{9,10},{10,1... | collective-permute-start | bytes 294920 | tf_op jit(solution)/shard_map/ppermute | solution.py:280
  32.0 10.4 %collective-permute-start.1 = (bf16[32,768]{1,0:T(8,128)(2,1)S(1)}, bf16[32,768]{1,0:T(8,128)(2,1)S(1)}, u32[]{:S(2)}, u32[]{:S(2)}) collective-permute-start(bf16[32,768]{1,0:T(8,128)(2,1)S(1)} %reshape.80), channel_id=1, source_target_pairs={{0,8},{8,16},{16,24},{24,32},{32,40},{40,48},{48,56},{56,64},{64,7... | collective-permute-start | bytes 147464 | tf_op jit(solution)/shard_map/ppermute | solution.py:281
  36.2 6.2 %collective-permute-start.2 = (bf16[16,768]{1,0:T(8,128)(2,1)S(1)}, bf16[16,768]{1,0:T(8,128)(2,1)S(1)}, u32[]{:S(2)}, u32[]{:S(2)}) collective-permute-start(bf16[16,768]{1,0:T(8,128)(2,1)S(1)} %reshape.81), channel_id=1, source_target_pairs={{0,9},{1,10},{2,11},{3,12},{4,13},{5,14},{6,15},{7,8},{8,17},{9,18... | collective-permute-start | bytes 73736 | tf_op jit(solution)/shard_map/ppermute | solution.py:282
  42.4 0.9 copy-start.3
  43.4 0.7 copy-start.4
  44.0 0.9 copy-start.6
  92.7 29.8 %copy-start.1 = (bf16[8,16,768]{2,1,0:T(8,128)(2,1)S(1)}, bf16[8,16,768]{2,1,0:T(8,128)(2,1)}, u32[]{:S(2)}) copy-start(bf16[8,16,768]{2,1,0:T(8,128)(2,1)} %param.10) | copy-start | bytes 589828
  92.7 50.5 %copy-start.5 = (s32[2]{0:T(128)S(1)}, s32[2]{0:T(128)}, u32[]{:S(2)}) copy-start(s32[2]{0:T(128)} %off_ref.3) | copy-start | bytes 28
  117.3 24.0 %all-to-all-start.2 = ((bf16[64,8,512]{2,1,0:T(8,128)(2,1)}), bf16[64,8,512]{2,1,0:T(8,128)(2,1)S(1)}, u32[]{:S(2)}, u32[]{:S(2)}) async-start(bf16[64,8,512]{2,1,0:T(8,128)(2,1)} %bitcast.12), calls=%async_computation.2 | async-start | bytes 1048576 | tf_op jit(solution)/shard_map/all_to_all | solution.py:266
  123.8 19.4 %collective-permute-start.3 = (bf16[64,768]{1,0:T(8,128)(2,1)S(1)}, bf16[64,768]{1,0:T(8,128)(2,1)S(1)}, u32[]{:S(2)}, u32[]{:S(2)}) collective-permute-start(bf16[64,768]{1,0:T(8,128)(2,1)S(1)} %get-tuple-element.27), channel_id=1, source_target_pairs={{0,7},{1,0},{2,1},{3,2},{4,3},{5,4},{6,5},{7,6},{8,15},{9,8},{10,9... | collective-permute-start | bytes 294920 | tf_op jit(solution)/shard_map/ppermute | solution.py:280
  123.8 19.4 %collective-permute-start.4 = (bf16[32,768]{1,0:T(8,128)(2,1)S(1)}, bf16[32,768]{1,0:T(8,128)(2,1)S(1)}, u32[]{:S(2)}, u32[]{:S(2)}) collective-permute-start(bf16[32,768]{1,0:T(8,128)(2,1)S(1)} %get-tuple-element.28), channel_id=1, source_target_pairs={{0,504},{8,0},{16,8},{24,16},{32,24},{40,32},{48,40},{56,48},{64,5... | collective-permute-start | bytes 147464 | tf_op jit(solution)/shard_map/ppermute | solution.py:281
  126.2 17.0 %collective-permute-start.5 = (bf16[16,768]{1,0:T(8,128)(2,1)S(1)}, bf16[16,768]{1,0:T(8,128)(2,1)S(1)}, u32[]{:S(2)}, u32[]{:S(2)}) collective-permute-start(bf16[16,768]{1,0:T(8,128)(2,1)S(1)} %get-tuple-element.29), channel_id=1, source_target_pairs={{0,511},{1,504},{2,505},{3,506},{4,507},{5,508},{6,509},{7,510},{8... | collective-permute-start | bytes 73736 | tf_op jit(solution)/shard_map/ppermute | solution.py:282
  143.2 0.9 copy-start.2
Sparse Core Ops, SparseCore 0:
  10.7 43.3 all-gather.2
  92.9 34.4 reduce-scatter.1

commit v2 on v1

v2 whole, which is shorter than its diff:
```python
import functools

import jax
import jax.numpy as jnp
from jax import lax
from jax.experimental import pallas as pl
from jax.experimental.pallas import tpu as pltpu
from jax.sharding import PartitionSpec as P

CAP = 5
WIRE_ROWS = 8
WIDE = 512
EPS = 1e-05
VMEM = pl.BlockSpec(memory_space=pltpu.VMEM)
ANY = pl.BlockSpec(memory_space=pl.ANY)
SMEM = pl.BlockSpec(memory_space=pltpu.SMEM)


def iota(shape, dim):
    return lax.broadcasted_iota(jnp.int32, shape, dim)


def ones_where(mask):
    return jnp.where(mask, 1.0, 0.0).astype(jnp.bfloat16)


def dot(a, b):
    return jnp.dot(a, b, preferred_element_type=jnp.float32)


def dot_t(a, b):
    return lax.dot_general(a, b, (((1,), (1,)), ((), ())), preferred_element_type=jnp.float32)


def t_dot(a, b):
    return lax.dot_general(a, b, (((0,), (0,)), ((), ())), preferred_element_type=jnp.float32)


def call(body, outs, *args, flops=0, traffic=0, specs=None, **kw):
    return pl.pallas_call(
        body,
        out_shape=outs,
        in_specs=[VMEM] * len(args) if specs is None else specs,
        out_specs=jax.tree.map(lambda _: VMEM, outs),
        compiler_params=pltpu.CompilerParams(vmem_limit_bytes=32 * 1024 * 1024),
        cost_estimate=pl.CostEstimate(flops=flops, bytes_accessed=traffic, transcendentals=0),
        **kw,
    )(*args)


def wire_masks(row, shape, dim):
    at = iota(shape, dim)
    pos = row & 7
    tail = row - pos + CAP + (pos >> 1)
    odd = (pos & 1) == 1
    left = jnp.where(odd, -1, tail)
    right = jnp.where(odd, tail, -1)
    return ones_where(at == row), ones_where(at == left), ones_where(at == right)


def from_wire(masks, wire):
    head, left, right = masks
    half = WIDE // 2
    return (
        dot(head, wire),
        dot(left, wire[:, :half]) + dot(right, wire[:, half:]),
    )


def to_wire(masks, rows, turned):
    head, left, right = masks
    f = t_dot if turned else dot
    tail = rows[:, WIDE:]
    return f(head, rows[:, :WIDE]) + jnp.concatenate([f(left, tail), f(right, tail)], axis=1)


def prepare(attn_hbm, w1_hbm, w2_hbm, up_ref, left_ref, corner_ref, w_hbm, attn_s, sems):
    copies = [
        pltpu.make_async_copy(src, dst, sems.at[i])
        for i, (src, dst) in enumerate(
            ((attn_hbm, attn_s), (w1_hbm, w_hbm.at[:, 0]), (w2_hbm, w_hbm.at[:, 1]))
        )
    ]
    for copy in copies:
        copy.start()
    tr, tc, width = attn_s.shape
    tokens = tr * tc
    n = 4 * tr
    s = iota((n, 1), 0)
    edge = ones_where((s // 4) * tc + tc - 4 + s % 4 == iota((n, tokens), 1))
    copies[0].wait()
    attn = attn_s[...].reshape(tokens, width)
    up_ref[...] = attn[tokens - 4 * tc :]
    left = dot(edge, attn).astype(jnp.bfloat16)
    left_ref[...] = left
    corner_ref[...] = left[n - 16 :]
    copies[1].wait()
    copies[2].wait()


def dispatch_g(tr, tc, off_ref, ids_ref, gates_ref, dout_ref, attn_ref, short_ref, sent_ref, mask_ref, meta_ref, x_ref, sel_ref):
    tokens = dout_ref.shape[0]
    t = iota((tokens, 1), 0)
    inside, halo = places(t // tc - off_ref[0], t % tc - off_ref[1], tr, tc)
    sel_ref[...] = halo
    x_ref[...] = short_ref[...].astype(jnp.float32) + dot(inside, attn_ref[...])
    n = sent_ref.shape[0]
    experts = n // WIRE_ROWS
    ids = ids_ref[...]
    rank = iota((experts, tokens), 0)
    first = jnp.where(ids[0:1] == rank, 1.0, 0.0)
    second = jnp.where(ids[1:2] == rank, 1.0, 0.0)
    earlier = ones_where(iota((tokens, tokens), 0) < iota((tokens, tokens), 1))
    before = dot((first + second).astype(jnp.bfloat16), earlier)
    row0 = ids[0:1] * WIRE_ROWS + jnp.sum(before * first, axis=0, keepdims=True).astype(jnp.int32)
    row1 = ids[1:2] * WIRE_ROWS + jnp.sum(before * second, axis=0, keepdims=True).astype(jnp.int32)
    at = iota((tokens, tokens), 0)
    table = jnp.where(at == 0, gates_ref[0:1], 0.0)
    table = jnp.where(at == 1, gates_ref[1:2], table)
    table = jnp.where(at == 2, row0.astype(jnp.float32), table)
    table = jnp.where(at == 3, row1.astype(jnp.float32), table)
    meta = table.T
    meta_ref[...] = meta
    dout = dout_ref[...].astype(jnp.float32)
    sent = 0.0
    both = None
    for k, row in enumerate((row0, row1)):
        masks = wire_masks(row, (n, tokens), 0)
        sent = sent + to_wire(masks, (meta[:, k : k + 1] * dout).astype(jnp.bfloat16), False)
        both = masks if both is None else tuple(a + b for a, b in zip(both, masks))
    for m in range(3):
        mask_ref[m] = both[m]
    sent_ref[...] = sent.astype(jnp.bfloat16)


def normalize(x):
    m = jnp.mean(x, axis=-1, keepdims=True)
    c = x - m
    r = lax.rsqrt(jnp.mean(c * c, axis=-1, keepdims=True) + EPS)
    return c * r, r


def places(i, j, tr, tc):
    tokens = i.shape[0]
    i_in = (i >= 0) & (i < tr)
    j_in = (j >= 0) & (j < tc)
    ei = jnp.where(i < 0, i + 4, i - tr)
    ej = jnp.where(j < 0, j + 4, j - tc)
    own = jnp.where(i_in & j_in, i * tc + j, -1)
    edge = jnp.where(
        i_in,
        jnp.where(j_in, -1, 4 * tc + i * 4 + ej),
        jnp.where(j_in, ei * tc + j, 4 * tc + 4 * tr + ei * 4 + ej),
    )
    count = 4 * tc + 4 * tr + 16
    return (
        ones_where(own == iota((tokens, tokens), 1)),
        ones_where(edge == iota((tokens, count), 1)),
    )


def dispatch_u(g_ref, mask_ref, x0_ref, sel_ref, up_ref, left_ref, corner_ref, sent_ref, x_ref):
    edge = jnp.concatenate([up_ref[...], left_ref[...], corner_ref[...]], axis=0)
    x = x0_ref[...] + dot(sel_ref[...], edge)
    x_ref[...] = x
    xhat, _ = normalize(x)
    masks = tuple(mask_ref[m] for m in range(3))
    sent_ref[:, :WIDE] = g_ref[...]
    sent_ref[:, WIDE:] = to_wire(masks, xhat.astype(jnp.bfloat16), False).astype(jnp.bfloat16)


def experts_body(wire_ref, w_ref, out_ref, grad_ref, u_s, g_s, q_s, y_s):
    step = pl.program_id(0)
    n = wire_ref.shape[0]
    peers = n // WIRE_ROWS
    slots = peers * CAP

    @pl.when(step == 0)
    def _():
        s = iota((slots, 1), 0)
        masks = wire_masks((s % peers) * WIRE_ROWS + s // peers, (slots, n), 1)
        for at, dst in ((0, g_s), (WIDE, u_s)):
            head, tail = from_wire(masks, wire_ref[:, at : at + WIDE])
            dst[:, :WIDE] = head.astype(jnp.bfloat16)
            dst[:, WIDE:] = tail.astype(jnp.bfloat16)

    u = u_s[...]
    g = g_s[...]
    block, _, part, width = w_ref.shape
    w1 = w_ref[:, 0].reshape(block * part, width)
    w2 = w_ref[:, 1].reshape(block * part, width)
    h = dot_t(u, w1)
    da = dot_t(g, w2)
    cdf = 0.5 * (1.0 + lax.erf(h * 0.7071067811865476))
    pdf = jnp.exp(-0.5 * h * h) * 0.3989422804014327
    a = (h * cdf).astype(jnp.bfloat16)
    p = (da * (cdf + h * pdf)).astype(jnp.bfloat16)
    q = dot(p, w1)
    y = dot(a, w2)
    grad_ref[:, 0] = t_dot(p, u).astype(jnp.bfloat16).reshape(block, part, width)
    grad_ref[:, 1] = t_dot(a, g).astype(jnp.bfloat16).reshape(block, part, width)

    @pl.when(step == 0)
    def _():
        q_s[...] = q
        y_s[...] = y

    @pl.when(step > 0)
    def _():
        q_s[...] += q
        y_s[...] += y

    @pl.when(step == pl.num_programs(0) - 1)
    def _():
        s = iota((slots, 1), 0)
        masks = wire_masks((s % peers) * WIRE_ROWS + s // peers, (slots, n), 1)
        out_ref[:, :WIDE] = to_wire(masks, q_s[...].astype(jnp.bfloat16), True).astype(jnp.bfloat16)
        out_ref[:, WIDE:] = to_wire(masks, y_s[...].astype(jnp.bfloat16), True).astype(jnp.bfloat16)


def experts(wire, w):
    n = wire.shape[0]
    parts, _, part, width = w.shape
    slots = n // WIRE_ROWS * CAP
    block = 2
    hidden = parts * part
    whole = pl.BlockSpec((n, 2 * WIDE), lambda i: (0, 0))
    piece = pl.BlockSpec((block, 2, part, width), lambda i: (i, 0, 0, 0))
    return pl.pallas_call(
        experts_body,
        grid=(parts // block,),
        out_shape=(
            jax.ShapeDtypeStruct((n, 2 * WIDE), jnp.bfloat16),
            jax.ShapeDtypeStruct(w.shape, jnp.bfloat16),
        ),
        in_specs=[whole, piece],
        out_specs=(whole, piece),
        scratch_shapes=[
            pltpu.VMEM((slots, width), jnp.bfloat16),
            pltpu.VMEM((slots, width), jnp.bfloat16),
            pltpu.VMEM((slots, width), jnp.float32),
            pltpu.VMEM((slots, width), jnp.float32),
        ],
        compiler_params=pltpu.CompilerParams(
            dimension_semantics=("arbitrary",), vmem_limit_bytes=48 * 1024 * 1024
        ),
        cost_estimate=pl.CostEstimate(
            flops=12 * slots * hidden * width,
            bytes_accessed=8 * hidden * width,
            transcendentals=2 * slots * hidden,
        ),
    )(wire, w)


def combine_q(tr, tc, wire_ref, meta_ref, x_ref, dout_ref, ds_ref, keep_ref, up_ref, left_ref, corner_ref):
    wire = wire_ref[:, :WIDE]
    tokens = x_ref.shape[0]
    both = None
    for k in range(2):
        row = meta_ref[:, 2 + k : 3 + k].astype(jnp.int32)
        masks = wire_masks(row, (tokens, wire.shape[0]), 1)
        both = masks if both is None else tuple(a + b for a, b in zip(both, masks))
    du = jnp.concatenate(from_wire(both, wire), axis=1)
    xhat, r = normalize(x_ref[...])
    dx = r * (
        du
        - jnp.mean(du, axis=-1, keepdims=True)
        - xhat * jnp.mean(du * xhat, axis=-1, keepdims=True)
    )
    ds = (dout_ref[...].astype(jnp.float32) + dx).astype(jnp.bfloat16)
    ds_ref[...] = ds
    keep_ref[...] = ds
    up_ref[...] = ds[: 4 * tc]
    n = 4 * tr
    s = iota((n, 1), 0)
    edge = dot(ones_where((s // 4) * tc + s % 4 == iota((n, tokens), 1)), ds).astype(jnp.bfloat16)
    left_ref[...] = edge
    corner_ref[...] = edge[:16]


def roll_back(tr, tc, off_ref, ds_ref, down_ref, right_ref, corner_ref, out_ref):
    t = iota((ds_ref.shape[0], 1), 0)
    inside, halo = places(t // tc + off_ref[0], t % tc + off_ref[1], tr, tc)
    edge = jnp.concatenate([down_ref[...], right_ref[...], corner_ref[...]], axis=0)
    out_ref[...] = (dot(inside, ds_ref[...]) + dot(halo, edge)).astype(jnp.bfloat16)


def combine_y(wire_ref, meta_ref, x_ref, dout_ref, out_ref, dg_ref):
    wire = wire_ref[:, WIDE:]
    dout = dout_ref[...].astype(jnp.float32)
    tokens = dout.shape[0]
    total = x_ref[...]
    lane = iota((tokens, tokens), 1)
    table = jnp.zeros((tokens, tokens), jnp.float32)
    for k in range(2):
        row = meta_ref[:, 2 + k : 3 + k].astype(jnp.int32)
        y = jnp.concatenate(from_wire(wire_masks(row, (tokens, wire.shape[0]), 1), wire), axis=1)
        total = total + meta_ref[:, k : k + 1] * y
        table = jnp.where(lane == k, jnp.sum(dout * y, axis=-1, keepdims=True), table)
    out_ref[...] = total.astype(jnp.bfloat16)
    dg_ref[...] = table.T[:2]


def exchange(wire, n):
    blocks = wire.reshape(n, WIRE_ROWS, wire.shape[-1])
    out = lax.all_to_all(blocks, "expert", split_axis=0, concat_axis=0, tiled=True)
    return out.reshape(wire.shape)


def edges(row_edge, col_edge, corner, step):
    n_dp, n_ex = lax.axis_size("dp"), lax.axis_size("expert")
    by_dp = [(i, (i + step) % n_dp) for i in range(n_dp)]
    by_ex = [(i, (i + step) % n_ex) for i in range(n_ex)]
    by_both = [
        (q * n_dp + p, (q + step) % n_ex * n_dp + (p + step) % n_dp)
        for q in range(n_ex)
        for p in range(n_dp)
    ]
    return (
        lax.ppermute(row_edge, "dp", by_dp),
        lax.ppermute(col_edge, "expert", by_ex),
        lax.ppermute(corner, ("expert", "dp"), by_both),
    )


def per_device(attn_win, shortcut, d_out, expert_ids, gate_probs, shift_offsets, w_in, w_out):
    tr, tc, width = attn_win.shape
    tokens = tr * tc
    n_ex = lax.axis_size("expert")
    n = n_ex * WIRE_ROWS
    bf16 = functools.partial(jax.ShapeDtypeStruct, dtype=jnp.bfloat16)
    f32 = functools.partial(jax.ShapeDtypeStruct, dtype=jnp.float32)
    ids = expert_ids.reshape(tokens, 2).T
    gates = gate_probs.reshape(tokens, 2).T
    dout = d_out.reshape(tokens, width)
    part = w_out.shape[1]

    up, left, corner, w_own = pl.pallas_call(
        prepare,
        out_shape=(
            bf16((4 * tc, width)),
            bf16((4 * tr, width)),
            bf16((16, width)),
            bf16((1, 2, part, width)),
        ),
        in_specs=[ANY] * 3,
        out_specs=(VMEM,) * 3 + (ANY,),
        scratch_shapes=[pltpu.VMEM((tr, tc, width), jnp.bfloat16), pltpu.SemaphoreType.DMA((3,))],
        compiler_params=pltpu.CompilerParams(vmem_limit_bytes=58 * 1024 * 1024),
        cost_estimate=pl.CostEstimate(flops=1 << 25, bytes_accessed=1 << 21, transcendentals=0),
    )(attn_win, w_in.transpose(0, 2, 1), w_out)
    w_all = lax.all_gather(w_own, "dp", axis=0, tiled=True)
    up, left, corner = edges(up, left, corner, 1)
    g_wire, masks, meta, x0, sel = call(
        functools.partial(dispatch_g, tr, tc),
        (
            bf16((n, WIDE)),
            bf16((3, n, tokens)),
            f32((tokens, tokens)),
            f32((tokens, width)),
            bf16((tokens, 4 * tc + 4 * tr + 16)),
        ),
        shift_offsets, ids, gates, dout, attn_win.reshape(tokens, width), shortcut.reshape(tokens, width),
        specs=[SMEM] + [VMEM] * 5,
        flops=4 * 256 * n * WIDE, traffic=1 << 20,
    )
    sent, x = call(
        dispatch_u,
        (bf16((n, 2 * WIDE)), f32((tokens, width))),
        g_wire, masks, x0, sel, up, left, corner,
        flops=4 * 128 * n * WIDE, traffic=1 << 21,
    )
    returned, grads = experts(exchange(sent, n_ex), w_all)
    returned = exchange(returned, n_ex)
    grad = lax.psum_scatter(grads, "dp", scatter_dimension=0, tiled=True)
    grad_in = grad[:, 0].transpose(0, 2, 1).astype(jnp.float32)
    grad_out = grad[:, 1].astype(jnp.float32)
    ds, ds_keep, up_b, left_b, corner_b = call(
        functools.partial(combine_q, tr, tc),
        (
            bf16((tokens, width)),
            bf16((tokens, width)),
            bf16((4 * tc, width)),
            bf16((4 * tr, width)),
            bf16((16, width)),
        ),
        returned, meta, x, dout,
        flops=4 * tokens * n * WIDE, traffic=1 << 21,
    )
    down, right, corner_r = edges(up_b, left_b, corner_b, -1)
    block_out, d_gates = call(
        combine_y,
        (bf16((tokens, width)), f32((2, tokens))),
        returned, meta, x, dout,
        flops=8 * tokens * n * WIDE, traffic=1 << 21,
    )
    d_attn = call(
        functools.partial(roll_back, tr, tc),
        bf16((tokens, width)),
        shift_offsets, ds_keep, down, right, corner_r,
        specs=[SMEM] + [VMEM] * 4,
        flops=2 * tokens * 256 * width, traffic=1 << 19,
    )
    tile = (tr, tc, width)
    return (
        block_out.reshape(tile),
        ds.reshape(tile),
        d_attn.reshape(tile),
        d_gates.T.reshape(1, 1, tokens, 2),
        grad_in,
        grad_out,
    )


def solution(mesh):
    tile = P("dp", "expert", None)
    pairs = P("dp", "expert", None, None)
    first, second = P("expert", None, "dp"), P("expert", "dp", None)
    return jax.shard_map(
        per_device,
        mesh=mesh,
        in_specs=(tile, tile, tile, pairs, pairs, P(), first, second),
        out_specs=(tile, tile, tile, pairs, first, second),
        check_vma=False,
    )
```

time: 156 us -> 159 us (1.019)
  the two profiles are of different devices: /device:TPU:10 before, /device:TPU:1 now
where the time goes in v2:
time: 159 us
  blocking collectives  72.6 us (46%)
  Pallas kernels  39.1 us (25%)
  starting transfers between devices  20.1 us (13%)
  between operations  14.1 us (9%)
  waiting for transfers between devices  5.74 us (4%)
  local copies, waits for them, and re-layouts  4.79 us (3%)
  other arithmetic  2.14 us (1%)
    all_to_all x2, blocking collectives, exchange(): lax.all_to_all(blocks, 'expert', split_axis=0, concat_axis=0, tiled=True)  72.6 us
    pallas_call x1, Pallas kernels, per_device(): pl.pallas_call(prepare, out_shape=(bf16((4 * tc, width)), bf16((4 * tr, w...  19.7 us
    pallas_call x1, Pallas kernels, experts(): pl.pallas_call(experts_body, grid=(parts // block,), out_shape=(jax.Shape...  12.8 us
    ppermute x2, starting transfers between devices, edges(): lax.ppermute(row_edge, 'dp', by_dp)  7.43 us
    ppermute x2, starting transfers between devices, edges(): lax.ppermute(col_edge, 'expert', by_ex)  7.36 us
    pallas_call x5, Pallas kernels, call(): pl.pallas_call(body, out_shape=outs, in_specs=[VMEM] * len(args) if specs...  6.69 us
    ppermute x2, waiting for transfers between devices, edges(): lax.ppermute(corner, ('expert', 'dp'), by_both)  5.69 us
    ppermute x2, starting transfers between devices, edges(): lax.ppermute(corner, ('expert', 'dp'), by_both)  5.24 us
  transfers between devices with their start and end apart: 8, of which 2 were waited for; matrix products, arithmetic and copies ran while one was open for 0% of the time, Pallas kernels for 4%

profile of v2, /device:TPU:1, one launch (start us, length us, event | category | flops | bytes accessed | tf_op | source)
XLA Modules:
  0.0 158.6 jit_solution(6129080939558519255)
XLA Ops:
  7.2 0.0 all-gather.2.cloned.1.call-start
  7.2 19.7 %shard_map.128 = (bf16[64,768]{1,0:T(8,128)(2,1)}, bf16[32,768]{1,0:T(8,128)(2,1)}, bf16[16,768]{1,0:T(8,128)(2,1)}, bf16[1,2,192,768]{3,2,1,0:T(8,128)(2,1)}) custom-call(bf16[8,16,768]{2,1,0:T(8,128)(2,1)} %attn_hbm.1, bf16[1,192,768]{2,1,0:T(8,128)(2,1)} %bitcast.44, bf16[1,192,768]{2,1,0:T(8,128)(2,1)} %w2_hbm.1), custom_call_target="tpu_custom_call" | custom-call | flops 33554432 | bytes 2097152 | tf_op jit(solution)/shard_map/pallas_call | solution.py:338
  26.9 0.0 all-gather.2.cloned.1.call-update
  26.9 0.0 reduce-scatter.2.cloned.1.call-start
  26.9 2.6 %collective-permute-start = (bf16[64,768]{1,0:T(8,128)(2,1)}, bf16[64,768]{1,0:T(8,128)(2,1)S(1)}, u32[]{:S(2)}, u32[]{:S(2)}) collective-permute-start(bf16[64,768]{1,0:T(8,128)(2,1)} %get-tuple-element.30), channel_id=1, source_target_pairs={{0,1},{1,2},{2,3},{3,4},{4,5},{5,6},{6,7},{7,0},{8,9},{9,10},{10,1... | collective-permute-start | bytes 294920 | tf_op jit(solution)/shard_map/ppermute | solution.py:320
  29.6 3.2 %collective-permute-start.1 = (bf16[32,768]{1,0:T(8,128)(2,1)}, bf16[32,768]{1,0:T(8,128)(2,1)S(1)}, u32[]{:S(2)}, u32[]{:S(2)}) collective-permute-start(bf16[32,768]{1,0:T(8,128)(2,1)} %get-tuple-element.31), channel_id=1, source_target_pairs={{0,8},{8,16},{16,24},{24,32},{32,40},{40,48},{48,56},{56,64},{64,7... | collective-permute-start | bytes 147464 | tf_op jit(solution)/shard_map/ppermute | solution.py:321
  32.8 3.2 %collective-permute-start.2 = (bf16[16,768]{1,0:T(8,128)(2,1)}, bf16[16,768]{1,0:T(8,128)(2,1)S(1)}, u32[]{:S(2)}, u32[]{:S(2)}) collective-permute-start(bf16[16,768]{1,0:T(8,128)(2,1)} %get-tuple-element.32), channel_id=1, source_target_pairs={{0,9},{1,10},{2,11},{3,12},{4,13},{5,14},{6,15},{7,8},{8,17},{9,18... | collective-permute-start | bytes 73736 | tf_op jit(solution)/shard_map/ppermute | solution.py:322
  36.0 0.0 copy-start
  36.0 0.9 copy-done
  36.9 0.0 copy-start.2
  36.9 0.9 copy-done.2
  37.9 0.0 copy-start.3
  37.9 0.7 copy-done.3
  38.5 0.0 copy-start.5
  38.5 0.9 copy-done.5
  39.4 0.0 copy-start.6
  39.4 0.7 copy-done.6
  40.1 0.0 copy-start.7
  40.1 0.7 copy-done.7
  40.8 1.8 %shard_map.127 = (bf16[512,512]{1,0:T(8,128)(2,1)S(1)}, bf16[3,512,128]{2,1,0:T(8,128)(2,1)S(1)}, f32[128,128]{1,0:T(8,128)S(1)}, f32[128,768]{1,0:T(8,128)S(1)}, bf16[128,112]{1,0:T(8,128)(2,1)S(1)}) custom-call(s32[2]{0:T(128)S(1)} %copy-done.3, s32[2,128]{1,0:T(2,128)S(1)} %bitcast.42, f32[2,128]{1,0:T(2,128)S(1)} %bitcast.43, ...), custom_call_target="tpu_custom_call" | custom-call | flops 268435456 | bytes 1048576 | tf_op jit(solution)/shard_map/pallas_call | solution.py:40
  42.6 3.0 %collective-permute-done.2.corner_ref = bf16[16,768]{1,0:T(8,128)(2,1)S(1)} collective-permute-done((bf16[16,768]{1,0:T(8,128)(2,1)}, bf16[16,768]{1,0:T(8,128)(2,1)S(1)}, u32[]{:S(2)}, u32[]{:S(2)}) %collective-permute-start.2) | collective-permute-done | bytes 24608 | tf_op jit(solution)/shard_map/ppermute | solution.py:322
  45.6 0.0 collective-permute-done.1.left_ref
  45.6 0.0 collective-permute-done.up_ref
  45.6 0.8 shard_map.129
  46.4 39.1 %all_to_all.10 = bf16[64,8,1024]{2,1,0:T(8,128)(2,1)S(1)} all-to-all(bf16[64,8,1024]{2,1,0:T(8,128)(2,1)S(1)} %bitcast.35), channel_id=1, replica_groups=mesh['expert'=64,'dp'=8] {'expert'}, dimensions={0} | all-to-all | bytes 2097152 | tf_op jit(solution)/shard_map/all_to_all | solution.py:306
  85.5 0.0 all-gather.2.cloned.1.call-done.w_ref
  85.5 12.8 %shard_map.130 = (bf16[512,1024]{1,0:T(8,128)(2,1)S(1)}, bf16[8,2,192,768]{3,2,1,0:T(8,128)(2,1)}) custom-call(bf16[512,1024]{1,0:T(8,128)(2,1)S(1)} %bitcast.36, bf16[8,2,192,768]{3,2,1,0:T(8,128)(2,1)} %all-gather.2.cloned.1.call-done.w_ref), custom_call_target="tpu_custom_call" | custom-call | flops 4529848320 | bytes 9437184 | tf_op jit(solution)/shard_map/pallas_call | solution.py:229
  98.3 0.0 copy-start.1
  98.3 0.0 copy-start.4
  98.3 0.0 reduce-scatter.2.cloned.1.call-update
  98.3 33.5 %all_to_all.11 = bf16[64,8,1024]{2,1,0:T(8,128)(2,1)S(1)} all-to-all(bf16[64,8,1024]{2,1,0:T(8,128)(2,1)S(1)} %bitcast.34), channel_id=1, replica_groups=mesh['expert'=64,'dp'=8] {'expert'}, dimensions={0} | all-to-all | bytes 2097152 | tf_op jit(solution)/shard_map/all_to_all | solution.py:306
  131.8 0.0 copy-done.1
  131.8 1.3 shard_map.132
  133.1 4.8 %collective-permute-start.3 = (bf16[64,768]{1,0:T(8,128)(2,1)S(1)}, bf16[64,768]{1,0:T(8,128)(2,1)S(1)}, u32[]{:S(2)}, u32[]{:S(2)}) collective-permute-start(bf16[64,768]{1,0:T(8,128)(2,1)S(1)} %get-tuple-element.41), channel_id=1, source_target_pairs={{0,7},{1,0},{2,1},{3,2},{4,3},{5,4},{6,5},{7,6},{8,15},{9,8},{10,9... | collective-permute-start | bytes 294920 | tf_op jit(solution)/shard_map/ppermute | solution.py:320
  137.9 4.2 %collective-permute-start.4 = (bf16[32,768]{1,0:T(8,128)(2,1)S(1)}, bf16[32,768]{1,0:T(8,128)(2,1)S(1)}, u32[]{:S(2)}, u32[]{:S(2)}) collective-permute-start(bf16[32,768]{1,0:T(8,128)(2,1)S(1)} %get-tuple-element.42), channel_id=1, source_target_pairs={{0,504},{8,0},{16,8},{24,16},{32,24},{40,32},{48,40},{56,48},{64,5... | collective-permute-start | bytes 147464 | tf_op jit(solution)/shard_map/ppermute | solution.py:321
  142.1 2.0 %collective-permute-start.5 = (bf16[16,768]{1,0:T(8,128)(2,1)S(1)}, bf16[16,768]{1,0:T(8,128)(2,1)S(1)}, u32[]{:S(2)}, u32[]{:S(2)}) collective-permute-start(bf16[16,768]{1,0:T(8,128)(2,1)S(1)} %get-tuple-element.43), channel_id=1, source_target_pairs={{0,511},{1,504},{2,505},{3,506},{4,507},{5,508},{6,509},{7,510},{8... | collective-permute-start | bytes 73736 | tf_op jit(solution)/shard_map/ppermute | solution.py:322
  144.1 1.3 shard_map.131
  145.4 2.7 %collective-permute-done.5.corner_ref = bf16[16,768]{1,0:T(8,128)(2,1)S(1)} collective-permute-done((bf16[16,768]{1,0:T(8,128)(2,1)S(1)}, bf16[16,768]{1,0:T(8,128)(2,1)S(1)}, u32[]{:S(2)}, u32[]{:S(2)}) %collective-permute-start.5) | collective-permute-done | bytes 24608 | tf_op jit(solution)/shard_map/ppermute | solution.py:322
  148.1 0.0 collective-permute-done.4.right_ref
  148.1 0.0 collective-permute-done.3.down_ref
  148.1 0.0 copy-done.4
  148.1 1.5 shard_map.133
  149.6 0.0 reduce-scatter.2.cloned.1.call-done
  149.6 2.1 %fusion = (f32[1,192,768]{2,1,0:T(8,128)}, f32[1,768,192]{1,2,0:T(8,128)}) fusion(bf16[1,2,192,768]{3,2,1,0:T(8,128)(2,1)} %reduce-scatter.2.cloned.1.call-done), kind=kLoop, calls=%fused_computation.2 | loop fusion | flops 294912 | bytes 1769472 | tf_op jit(solution)/shard_map/convert_element_type | solution.py:377
Async XLA Ops:
  7.2 78.3 %all-gather.2.cloned.1.call-start = ((), (), s32[]{:S(2)}) async-start(), calls=%async_computation.3 | async-start | bytes 5308416 | tf_op jit(solution)/shard_map/all_gather | solution.py:352
  26.9 122.7 %reduce-scatter.2.cloned.1.call-start = ((), (), s32[]{:S(2)}) async-start(), calls=%async_computation.4 | async-start | bytes 5308416 | tf_op jit(solution)/shard_map/reduce_scatter | solution.py:375
  26.9 18.6 %collective-permute-start = (bf16[64,768]{1,0:T(8,128)(2,1)}, bf16[64,768]{1,0:T(8,128)(2,1)S(1)}, u32[]{:S(2)}, u32[]{:S(2)}) collective-permute-start(bf16[64,768]{1,0:T(8,128)(2,1)} %get-tuple-element.30), channel_id=1, source_target_pairs={{0,1},{1,2},{2,3},{3,4},{4,5},{5,6},{6,7},{7,0},{8,9},{9,10},{10,1... | collective-permute-start | bytes 294920 | tf_op jit(solution)/shard_map/ppermute | solution.py:320
  29.6 16.0 %collective-permute-start.1 = (bf16[32,768]{1,0:T(8,128)(2,1)}, bf16[32,768]{1,0:T(8,128)(2,1)S(1)}, u32[]{:S(2)}, u32[]{:S(2)}) collective-permute-start(bf16[32,768]{1,0:T(8,128)(2,1)} %get-tuple-element.31), channel_id=1, source_target_pairs={{0,8},{8,16},{16,24},{24,32},{32,40},{40,48},{48,56},{56,64},{64,7... | collective-permute-start | bytes 147464 | tf_op jit(solution)/shard_map/ppermute | solution.py:321
  32.8 12.8 %collective-permute-start.2 = (bf16[16,768]{1,0:T(8,128)(2,1)}, bf16[16,768]{1,0:T(8,128)(2,1)S(1)}, u32[]{:S(2)}, u32[]{:S(2)}) collective-permute-start(bf16[16,768]{1,0:T(8,128)(2,1)} %get-tuple-element.32), channel_id=1, source_target_pairs={{0,9},{1,10},{2,11},{3,12},{4,13},{5,14},{6,15},{7,8},{8,17},{9,18... | collective-permute-start | bytes 73736 | tf_op jit(solution)/shard_map/ppermute | solution.py:322
  36.0 0.9 copy-start
  36.9 0.9 copy-start.2
  37.9 0.7 copy-start.3
  38.5 0.9 copy-start.5
  39.4 0.7 copy-start.6
  40.1 0.7 copy-start.7
  98.3 33.5 %copy-start.1 = (bf16[8,16,768]{2,1,0:T(8,128)(2,1)S(1)}, bf16[8,16,768]{2,1,0:T(8,128)(2,1)}, u32[]{:S(2)}) copy-start(bf16[8,16,768]{2,1,0:T(8,128)(2,1)} %param.10) | copy-start | bytes 589828
  98.3 49.9 %copy-start.4 = (s32[2]{0:T(128)S(1)}, s32[2]{0:T(128)}, u32[]{:S(2)}) copy-start(s32[2]{0:T(128)} %off_ref.3) | copy-start | bytes 28
  133.1 15.0 %collective-permute-start.3 = (bf16[64,768]{1,0:T(8,128)(2,1)S(1)}, bf16[64,768]{1,0:T(8,128)(2,1)S(1)}, u32[]{:S(2)}, u32[]{:S(2)}) collective-permute-start(bf16[64,768]{1,0:T(8,128)(2,1)S(1)} %get-tuple-element.41), channel_id=1, source_target_pairs={{0,7},{1,0},{2,1},{3,2},{4,3},{5,4},{6,5},{7,6},{8,15},{9,8},{10,9... | collective-permute-start | bytes 294920 | tf_op jit(solution)/shard_map/ppermute | solution.py:320
  137.9 10.2 %collective-permute-start.4 = (bf16[32,768]{1,0:T(8,128)(2,1)S(1)}, bf16[32,768]{1,0:T(8,128)(2,1)S(1)}, u32[]{:S(2)}, u32[]{:S(2)}) collective-permute-start(bf16[32,768]{1,0:T(8,128)(2,1)S(1)} %get-tuple-element.42), channel_id=1, source_target_pairs={{0,504},{8,0},{16,8},{24,16},{32,24},{40,32},{48,40},{56,48},{64,5... | collective-permute-start | bytes 147464 | tf_op jit(solution)/shard_map/ppermute | solution.py:321
  142.1 6.0 %collective-permute-start.5 = (bf16[16,768]{1,0:T(8,128)(2,1)S(1)}, bf16[16,768]{1,0:T(8,128)(2,1)S(1)}, u32[]{:S(2)}, u32[]{:S(2)}) collective-permute-start(bf16[16,768]{1,0:T(8,128)(2,1)S(1)} %get-tuple-element.43), channel_id=1, source_target_pairs={{0,511},{1,504},{2,505},{3,506},{4,507},{5,508},{6,509},{7,510},{8... | collective-permute-start | bytes 73736 | tf_op jit(solution)/shard_map/ppermute | solution.py:322
Sparse Core Ops, SparseCore 0:
  27.0 45.5 all-gather.1
  98.4 39.3 reduce-scatter.1

commit v3 on v2

--- a/solution.py
+++ b/solution.py
@@ -8,11 +8,12 @@
 from jax.sharding import PartitionSpec as P
 
 CAP = 5
+SPARE = 48 << 20
 WIRE_ROWS = 8
 WIDE = 512
 EPS = 1e-05
 VMEM = pl.BlockSpec(memory_space=pltpu.VMEM)
-ANY = pl.BlockSpec(memory_space=pl.ANY)
+HBM = pl.BlockSpec(memory_space=pltpu.HBM)
 SMEM = pl.BlockSpec(memory_space=pltpu.SMEM)
 
 
@@ -74,11 +75,11 @@
     return f(head, rows[:, :WIDE]) + jnp.concatenate([f(left, tail), f(right, tail)], axis=1)
 
 
-def prepare(attn_hbm, w1_hbm, w2_hbm, up_ref, left_ref, corner_ref, w_hbm, attn_s, sems):
+def prepare(attn_hbm, w1_hbm, w2_hbm, up_ref, left_ref, corner_ref, w_ref, attn_s, sems):
     copies = [
         pltpu.make_async_copy(src, dst, sems.at[i])
         for i, (src, dst) in enumerate(
-            ((attn_hbm, attn_s), (w1_hbm, w_hbm.at[:, 0]), (w2_hbm, w_hbm.at[:, 1]))
+            ((attn_hbm, attn_s), (w1_hbm, w_ref.at[:, 0]), (w2_hbm, w_ref.at[:, 1]))
         )
     ]
     for copy in copies:
@@ -169,81 +170,99 @@
     sent_ref[:, WIDE:] = to_wire(masks, xhat.astype(jnp.bfloat16), False).astype(jnp.bfloat16)
 
 
-def experts_body(wire_ref, w_ref, out_ref, grad_ref, u_s, g_s, q_s, y_s):
-    step = pl.program_id(0)
+def slot_masks(dim, peers):
+    slots = peers * CAP
+    s = iota((slots, 1) if dim else (1, slots), 1 - dim)
+    row = (s % peers) * WIRE_ROWS + s // peers
+    wire = peers * WIRE_ROWS
+    return wire_masks(row, (slots, wire) if dim else (wire, slots), dim)
+
+
+def experts_body(wire_ref, w_hbm, out_ref, grad_hbm, w_s, grad_s, u_s, g_s, in_sems, out_sems):
+    parts, _, part, width = w_s.shape
+    half = parts // 2
+    hidden = half * part
+    pieces = [(c, k) for c in range(2) for k in range(2)]
+    ins = [
+        pltpu.make_async_copy(
+            w_hbm.at[pl.ds(c * half, half), k], w_s.at[pl.ds(c * half, half), k], in_sems.at[i]
+        )
+        for i, (c, k) in enumerate(pieces)
+    ]
+    outs = [
+        pltpu.make_async_copy(
+            grad_s.at[pl.ds(c * half, half), k], grad_hbm.at[pl.ds(c * half, half), k], out_sems.at[i]
+        )
+        for i, (c, k) in enumerate(pieces)
+    ]
+    for copy in ins:
+        copy.start()
     n = wire_ref.shape[0]
-    peers = n // WIRE_ROWS
-    slots = peers * CAP
-
-    @pl.when(step == 0)
-    def _():
-        s = iota((slots, 1), 0)
-        masks = wire_masks((s % peers) * WIRE_ROWS + s // peers, (slots, n), 1)
+    peers = min(32, n // WIRE_ROWS)
+    rows, slots = peers * WIRE_ROWS, peers * CAP
+    blocks = n // rows
+    masks = slot_masks(1, peers)
+    for b in range(blocks):
         for at, dst in ((0, g_s), (WIDE, u_s)):
-            head, tail = from_wire(masks, wire_ref[:, at : at + WIDE])
-            dst[:, :WIDE] = head.astype(jnp.bfloat16)
-            dst[:, WIDE:] = tail.astype(jnp.bfloat16)
-
+            head, tail = from_wire(masks, wire_ref[b * rows : (b + 1) * rows, at : at + WIDE])
+            dst[b * slots : (b + 1) * slots, :WIDE] = head.astype(jnp.bfloat16)
+            dst[b * slots : (b + 1) * slots, WIDE:] = tail.astype(jnp.bfloat16)
     u = u_s[...]
     g = g_s[...]
-    block, _, part, width = w_ref.shape
-    w1 = w_ref[:, 0].reshape(block * part, width)
-    w2 = w_ref[:, 1].reshape(block * part, width)
-    h = dot_t(u, w1)
-    da = dot_t(g, w2)
-    cdf = 0.5 * (1.0 + lax.erf(h * 0.7071067811865476))
-    pdf = jnp.exp(-0.5 * h * h) * 0.3989422804014327
-    a = (h * cdf).astype(jnp.bfloat16)
-    p = (da * (cdf + h * pdf)).astype(jnp.bfloat16)
-    q = dot(p, w1)
-    y = dot(a, w2)
-    grad_ref[:, 0] = t_dot(p, u).astype(jnp.bfloat16).reshape(block, part, width)
-    grad_ref[:, 1] = t_dot(a, g).astype(jnp.bfloat16).reshape(block, part, width)
-
-    @pl.when(step == 0)
-    def _():
-        q_s[...] = q
-        y_s[...] = y
-
-    @pl.when(step > 0)
-    def _():
-        q_s[...] += q
-        y_s[...] += y
-
-    @pl.when(step == pl.num_programs(0) - 1)
-    def _():
-        s = iota((slots, 1), 0)
-        masks = wire_masks((s % peers) * WIRE_ROWS + s // peers, (slots, n), 1)
-        out_ref[:, :WIDE] = to_wire(masks, q_s[...].astype(jnp.bfloat16), True).astype(jnp.bfloat16)
-        out_ref[:, WIDE:] = to_wire(masks, y_s[...].astype(jnp.bfloat16), True).astype(jnp.bfloat16)
+
+    def weights(c, k):
+        return w_s[c * half : (c + 1) * half, k].reshape(hidden, width)
+
+    pairs = []
+    for c in range(2):
+        ins[2 * c].wait()
+        h = dot_t(u, weights(c, 0))
+        ins[2 * c + 1].wait()
+        pairs.append((h, dot_t(g, weights(c, 1))))
+    acts = []
+    for c, (h, da) in enumerate(pairs):
+        cdf = 0.5 * (1.0 + lax.erf(h * 0.7071067811865476))
+        pdf = jnp.exp(-0.5 * h * h) * 0.3989422804014327
+        a = (h * cdf).astype(jnp.bfloat16)
+        p = (da * (cdf + h * pdf)).astype(jnp.bfloat16)
+        acts.append((p, a))
+        for k, (left, right) in enumerate(((p, u), (a, g))):
+            grad = t_dot(left, right).astype(jnp.bfloat16)
+            grad_s[c * half : (c + 1) * half, k] = grad.reshape(half, part, width)
+            outs[2 * c + k].start()
+    q = dot(acts[0][0], weights(0, 0)) + dot(acts[1][0], weights(1, 0))
+    y = dot(acts[0][1], weights(0, 1)) + dot(acts[1][1], weights(1, 1))
+    masks = slot_masks(0, peers)
+    for at, src in ((0, q.astype(jnp.bfloat16)), (WIDE, y.astype(jnp.bfloat16))):
+        for b in range(blocks):
+            block = to_wire(masks, src[b * slots : (b + 1) * slots], False)
+            out_ref[b * rows : (b + 1) * rows, at : at + WIDE] = block.astype(jnp.bfloat16)
+    for copy in outs:
+        copy.wait()
 
 
 def experts(wire, w):
     n = wire.shape[0]
     parts, _, part, width = w.shape
     slots = n // WIRE_ROWS * CAP
-    block = 2
     hidden = parts * part
-    whole = pl.BlockSpec((n, 2 * WIDE), lambda i: (0, 0))
-    piece = pl.BlockSpec((block, 2, part, width), lambda i: (i, 0, 0, 0))
     return pl.pallas_call(
         experts_body,
-        grid=(parts // block,),
         out_shape=(
             jax.ShapeDtypeStruct((n, 2 * WIDE), jnp.bfloat16),
             jax.ShapeDtypeStruct(w.shape, jnp.bfloat16),
         ),
-        in_specs=[whole, piece],
-        out_specs=(whole, piece),
+        in_specs=[VMEM, HBM],
+        out_specs=(VMEM, HBM),
         scratch_shapes=[
+            pltpu.VMEM(w.shape, jnp.bfloat16),
+            pltpu.VMEM(w.shape, jnp.bfloat16),
             pltpu.VMEM((slots, width), jnp.bfloat16),
             pltpu.VMEM((slots, width), jnp.bfloat16),
-            pltpu.VMEM((slots, width), jnp.float32),
-            pltpu.VMEM((slots, width), jnp.float32),
+            pltpu.SemaphoreType.DMA((4,)),
+            pltpu.SemaphoreType.DMA((4,)),
         ],
-        compiler_params=pltpu.CompilerParams(
-            dimension_semantics=("arbitrary",), vmem_limit_bytes=48 * 1024 * 1024
-        ),
+        compiler_params=pltpu.CompilerParams(vmem_limit_bytes=SPARE),
         cost_estimate=pl.CostEstimate(
             flops=12 * slots * hidden * width,
             bytes_accessed=8 * hidden * width,
@@ -343,10 +362,10 @@
             bf16((16, width)),
             bf16((1, 2, part, width)),
         ),
-        in_specs=[ANY] * 3,
-        out_specs=(VMEM,) * 3 + (ANY,),
+        in_specs=[HBM] * 3,
+        out_specs=(VMEM,) * 4,
         scratch_shapes=[pltpu.VMEM((tr, tc, width), jnp.bfloat16), pltpu.SemaphoreType.DMA((3,))],
-        compiler_params=pltpu.CompilerParams(vmem_limit_bytes=58 * 1024 * 1024),
+        compiler_params=pltpu.CompilerParams(vmem_limit_bytes=58 << 20),
         cost_estimate=pl.CostEstimate(flops=1 << 25, bytes_accessed=1 << 21, transcendentals=0),
     )(attn_win, w_in.transpose(0, 2, 1), w_out)
     w_all = lax.all_gather(w_own, "dp", axis=0, tiled=True)

time: 159 us -> 138 us (0.87)
  Pallas kernels: 39.1 us -> 18.1 us
    pallas_call x1, Pallas kernels: 19.7 us -> 2.05 us  [per_device(): pl.pallas_call(prepare, out_shape=(bf16((4 * tc, width)), bf16((4 * tr, w...]
    pallas_call x1, Pallas kernels: 12.8 us -> 9.31 us  [experts(): pl.pallas_call(experts_body, out_shape=(jax.ShapeDtypeStruct((n, 2 * WIDE...]
  transfers between devices with their start and end apart: 8 -> 8, of which waited for: 2 -> 2; matrix products, arithmetic and copies ran while one was open for 0% -> 0% of each run, Pallas kernels for 4% -> 5%
where the time goes in v3:
time: 138 us
  blocking collectives  72.5 us (53%)
  starting transfers between devices  20.1 us (15%)
  Pallas kernels  18.1 us (13%)
  between operations  14.1 us (10%)
  waiting for transfers between devices  5.74 us (4%)
  local copies, waits for them, and re-layouts  4.8 us (3%)
  other arithmetic  2.14 us (2%)
    all_to_all x2, blocking collectives, exchange(): lax.all_to_all(blocks, 'expert', split_axis=0, concat_axis=0, tiled=True)  72.5 us
    pallas_call x1, Pallas kernels, experts(): pl.pallas_call(experts_body, out_shape=(jax.ShapeDtypeStruct((n, 2 * WIDE...  9.31 us
    ppermute x2, starting transfers between devices, edges(): lax.ppermute(col_edge, 'expert', by_ex)  7.41 us
    ppermute x2, starting transfers between devices, edges(): lax.ppermute(row_edge, 'dp', by_dp)  7.4 us
    pallas_call x5, Pallas kernels, call(): pl.pallas_call(body, out_shape=outs, in_specs=[VMEM] * len(args) if specs...  6.7 us
    ppermute x2, waiting for transfers between devices, edges(): lax.ppermute(corner, ('expert', 'dp'), by_both)  5.69 us
    ppermute x2, starting transfers between devices, edges(): lax.ppermute(corner, ('expert', 'dp'), by_both)  5.24 us
    unnamed x16, local copies, waits for them, and re-layouts  4.8 us
  transfers between devices with their start and end apart: 8, of which 2 were waited for; matrix products, arithmetic and copies ran while one was open for 0% of the time, Pallas kernels for 5%

profile of v3, /device:TPU:1, one launch (start us, length us, event | category | flops | bytes accessed | tf_op | source)
XLA Modules:
  0.0 137.6 jit_solution(4045044911818683712)
XLA Ops:
  7.2 0.0 all-gather.2.cloned.1.call-start
  7.2 2.1 %shard_map.128 = (bf16[64,768]{1,0:T(8,128)(2,1)}, bf16[32,768]{1,0:T(8,128)(2,1)}, bf16[16,768]{1,0:T(8,128)(2,1)}, bf16[1,2,192,768]{3,2,1,0:T(8,128)(2,1)}) custom-call(bf16[8,16,768]{2,1,0:T(8,128)(2,1)} %attn_hbm.1, bf16[1,192,768]{2,1,0:T(8,128)(2,1)} %bitcast.44, bf16[1,192,768]{2,1,0:T(8,128)(2,1)} %w2_hbm.1), custom_call_target="tpu_custom_call" | custom-call | flops 33554432 | bytes 2097152 | tf_op jit(solution)/shard_map/pallas_call | solution.py:357
  9.3 0.0 all-gather.2.cloned.1.call-update
  9.3 0.0 reduce-scatter.2.cloned.1.call-start
  9.3 2.6 %collective-permute-start = (bf16[64,768]{1,0:T(8,128)(2,1)}, bf16[64,768]{1,0:T(8,128)(2,1)S(1)}, u32[]{:S(2)}, u32[]{:S(2)}) collective-permute-start(bf16[64,768]{1,0:T(8,128)(2,1)} %get-tuple-element.30), channel_id=1, source_target_pairs={{0,1},{1,2},{2,3},{3,4},{4,5},{5,6},{6,7},{7,0},{8,9},{9,10},{10,1... | collective-permute-start | bytes 294920 | tf_op jit(solution)/shard_map/ppermute | solution.py:339
  12.0 3.2 %collective-permute-start.1 = (bf16[32,768]{1,0:T(8,128)(2,1)}, bf16[32,768]{1,0:T(8,128)(2,1)S(1)}, u32[]{:S(2)}, u32[]{:S(2)}) collective-permute-start(bf16[32,768]{1,0:T(8,128)(2,1)} %get-tuple-element.31), channel_id=1, source_target_pairs={{0,8},{8,16},{16,24},{24,32},{32,40},{40,48},{48,56},{56,64},{64,7... | collective-permute-start | bytes 147464 | tf_op jit(solution)/shard_map/ppermute | solution.py:340
  15.2 3.2 %collective-permute-start.2 = (bf16[16,768]{1,0:T(8,128)(2,1)}, bf16[16,768]{1,0:T(8,128)(2,1)S(1)}, u32[]{:S(2)}, u32[]{:S(2)}) collective-permute-start(bf16[16,768]{1,0:T(8,128)(2,1)} %get-tuple-element.32), channel_id=1, source_target_pairs={{0,9},{1,10},{2,11},{3,12},{4,13},{5,14},{6,15},{7,8},{8,17},{9,18... | collective-permute-start | bytes 73736 | tf_op jit(solution)/shard_map/ppermute | solution.py:341
  18.4 0.0 copy-start
  18.4 0.9 copy-done
  19.3 0.0 copy-start.2
  19.3 0.9 copy-done.2
  20.3 0.0 copy-start.3
  20.3 0.7 copy-done.3
  20.9 0.0 copy-start.5
  20.9 0.9 copy-done.5
  21.8 0.0 copy-start.6
  21.8 0.7 copy-done.6
  22.5 0.0 copy-start.7
  22.5 0.7 copy-done.7
  23.2 1.8 %shard_map.127 = (bf16[512,512]{1,0:T(8,128)(2,1)S(1)}, bf16[3,512,128]{2,1,0:T(8,128)(2,1)S(1)}, f32[128,128]{1,0:T(8,128)S(1)}, f32[128,768]{1,0:T(8,128)S(1)}, bf16[128,112]{1,0:T(8,128)(2,1)S(1)}) custom-call(s32[2]{0:T(128)S(1)} %copy-done.3, s32[2,128]{1,0:T(2,128)S(1)} %bitcast.42, f32[2,128]{1,0:T(2,128)S(1)} %bitcast.43, ...), custom_call_target="tpu_custom_call" | custom-call | flops 268435456 | bytes 1048576 | tf_op jit(solution)/shard_map/pallas_call | solution.py:41
  25.0 3.0 %collective-permute-done.2.corner_ref = bf16[16,768]{1,0:T(8,128)(2,1)S(1)} collective-permute-done((bf16[16,768]{1,0:T(8,128)(2,1)}, bf16[16,768]{1,0:T(8,128)(2,1)S(1)}, u32[]{:S(2)}, u32[]{:S(2)}) %collective-permute-start.2) | collective-permute-done | bytes 24608 | tf_op jit(solution)/shard_map/ppermute | solution.py:341
  28.0 0.0 collective-permute-done.1.left_ref
  28.0 0.0 collective-permute-done.up_ref
  28.0 0.8 shard_map.129
  28.8 39.0 %all_to_all.10 = bf16[64,8,1024]{2,1,0:T(8,128)(2,1)S(1)} all-to-all(bf16[64,8,1024]{2,1,0:T(8,128)(2,1)S(1)} %bitcast.35), channel_id=1, replica_groups=mesh['expert'=64,'dp'=8] {'expert'}, dimensions={0} | all-to-all | bytes 2097152 | tf_op jit(solution)/shard_map/all_to_all | solution.py:325
  67.8 0.0 all-gather.2.cloned.1.call-done.w_hbm
  67.8 9.3 %shard_map.130 = (bf16[512,1024]{1,0:T(8,128)(2,1)S(1)}, bf16[8,2,192,768]{3,2,1,0:T(8,128)(2,1)}) custom-call(bf16[512,1024]{1,0:T(8,128)(2,1)S(1)} %bitcast.36, bf16[8,2,192,768]{3,2,1,0:T(8,128)(2,1)} %all-gather.2.cloned.1.call-done.w_hbm), custom_call_target="tpu_custom_call" | custom-call | flops 4529848320 | bytes 9437184 | tf_op jit(solution)/shard_map/pallas_call | solution.py:249
  77.2 0.0 copy-start.1
  77.2 0.0 copy-start.4
  77.2 0.0 reduce-scatter.2.cloned.1.call-update
  77.2 33.5 %all_to_all.11 = bf16[64,8,1024]{2,1,0:T(8,128)(2,1)S(1)} all-to-all(bf16[64,8,1024]{2,1,0:T(8,128)(2,1)S(1)} %bitcast.34), channel_id=1, replica_groups=mesh['expert'=64,'dp'=8] {'expert'}, dimensions={0} | all-to-all | bytes 2097152 | tf_op jit(solution)/shard_map/all_to_all | solution.py:325
  110.7 0.0 copy-done.1
  110.7 1.3 shard_map.132
  112.0 4.8 %collective-permute-start.3 = (bf16[64,768]{1,0:T(8,128)(2,1)S(1)}, bf16[64,768]{1,0:T(8,128)(2,1)S(1)}, u32[]{:S(2)}, u32[]{:S(2)}) collective-permute-start(bf16[64,768]{1,0:T(8,128)(2,1)S(1)} %get-tuple-element.41), channel_id=1, source_target_pairs={{0,7},{1,0},{2,1},{3,2},{4,3},{5,4},{6,5},{7,6},{8,15},{9,8},{10,9... | collective-permute-start | bytes 294920 | tf_op jit(solution)/shard_map/ppermute | solution.py:339
  116.8 4.2 %collective-permute-start.4 = (bf16[32,768]{1,0:T(8,128)(2,1)S(1)}, bf16[32,768]{1,0:T(8,128)(2,1)S(1)}, u32[]{:S(2)}, u32[]{:S(2)}) collective-permute-start(bf16[32,768]{1,0:T(8,128)(2,1)S(1)} %get-tuple-element.42), channel_id=1, source_target_pairs={{0,504},{8,0},{16,8},{24,16},{32,24},{40,32},{48,40},{56,48},{64,5... | collective-permute-start | bytes 147464 | tf_op jit(solution)/shard_map/ppermute | solution.py:340
  121.0 2.0 %collective-permute-start.5 = (bf16[16,768]{1,0:T(8,128)(2,1)S(1)}, bf16[16,768]{1,0:T(8,128)(2,1)S(1)}, u32[]{:S(2)}, u32[]{:S(2)}) collective-permute-start(bf16[16,768]{1,0:T(8,128)(2,1)S(1)} %get-tuple-element.43), channel_id=1, source_target_pairs={{0,511},{1,504},{2,505},{3,506},{4,507},{5,508},{6,509},{7,510},{8... | collective-permute-start | bytes 73736 | tf_op jit(solution)/shard_map/ppermute | solution.py:341
  123.0 1.3 shard_map.131
  124.3 2.7 %collective-permute-done.5.corner_ref = bf16[16,768]{1,0:T(8,128)(2,1)S(1)} collective-permute-done((bf16[16,768]{1,0:T(8,128)(2,1)S(1)}, bf16[16,768]{1,0:T(8,128)(2,1)S(1)}, u32[]{:S(2)}, u32[]{:S(2)}) %collective-permute-start.5) | collective-permute-done | bytes 24608 | tf_op jit(solution)/shard_map/ppermute | solution.py:341
  127.1 0.0 collective-permute-done.4.right_ref
  127.1 0.0 collective-permute-done.3.down_ref
  127.1 0.0 copy-done.4
  127.1 1.5 %shard_map.133 = bf16[128,768]{1,0:T(8,128)(2,1)} custom-call(s32[2]{0:T(128)S(1)} %copy-done.4, bf16[128,768]{1,0:T(8,128)(2,1)S(1)} %get-tuple-element.40.ds_ref, bf16[64,768]{1,0:T(8,128)(2,1)S(1)} %collective-permute-done.3.down_ref, bf16[32,768]{1,0:T(8,128)(2,1)S(1)} %collective-permute-done.4.right_ref, ...), custom_call_target="tpu_custom_call" | custom-call | flops 50331648 | bytes 524288 | tf_op jit(solution)/shard_map/pallas_call | solution.py:41
  128.6 0.0 reduce-scatter.2.cloned.1.call-done
  128.6 2.1 %fusion = (f32[1,192,768]{2,1,0:T(8,128)}, f32[1,768,192]{1,2,0:T(8,128)}) fusion(bf16[1,2,192,768]{3,2,1,0:T(8,128)(2,1)} %reduce-scatter.2.cloned.1.call-done), kind=kLoop, calls=%fused_computation.2 | loop fusion | flops 294912 | bytes 1769472 | tf_op jit(solution)/shard_map/convert_element_type | solution.py:396
Async XLA Ops:
  7.2 60.7 %all-gather.2.cloned.1.call-start = ((), (), s32[]{:S(2)}) async-start(), calls=%async_computation.3 | async-start | bytes 5308416 | tf_op jit(solution)/shard_map/all_gather | solution.py:371
  9.3 119.3 %reduce-scatter.2.cloned.1.call-start = ((), (), s32[]{:S(2)}) async-start(), calls=%async_computation.4 | async-start | bytes 5308416 | tf_op jit(solution)/shard_map/reduce_scatter | solution.py:394
  9.3 18.6 %collective-permute-start = (bf16[64,768]{1,0:T(8,128)(2,1)}, bf16[64,768]{1,0:T(8,128)(2,1)S(1)}, u32[]{:S(2)}, u32[]{:S(2)}) collective-permute-start(bf16[64,768]{1,0:T(8,128)(2,1)} %get-tuple-element.30), channel_id=1, source_target_pairs={{0,1},{1,2},{2,3},{3,4},{4,5},{5,6},{6,7},{7,0},{8,9},{9,10},{10,1... | collective-permute-start | bytes 294920 | tf_op jit(solution)/shard_map/ppermute | solution.py:339
  12.0 16.0 %collective-permute-start.1 = (bf16[32,768]{1,0:T(8,128)(2,1)}, bf16[32,768]{1,0:T(8,128)(2,1)S(1)}, u32[]{:S(2)}, u32[]{:S(2)}) collective-permute-start(bf16[32,768]{1,0:T(8,128)(2,1)} %get-tuple-element.31), channel_id=1, source_target_pairs={{0,8},{8,16},{16,24},{24,32},{32,40},{40,48},{48,56},{56,64},{64,7... | collective-permute-start | bytes 147464 | tf_op jit(solution)/shard_map/ppermute | solution.py:340
  15.2 12.8 %collective-permute-start.2 = (bf16[16,768]{1,0:T(8,128)(2,1)}, bf16[16,768]{1,0:T(8,128)(2,1)S(1)}, u32[]{:S(2)}, u32[]{:S(2)}) collective-permute-start(bf16[16,768]{1,0:T(8,128)(2,1)} %get-tuple-element.32), channel_id=1, source_target_pairs={{0,9},{1,10},{2,11},{3,12},{4,13},{5,14},{6,15},{7,8},{8,17},{9,18... | collective-permute-start | bytes 73736 | tf_op jit(solution)/shard_map/ppermute | solution.py:341
  18.4 0.9 copy-start
  19.3 0.9 copy-start.2
  20.3 0.7 copy-start.3
  20.9 0.9 copy-start.5
  21.8 0.7 copy-start.6
  22.5 0.7 copy-start.7
  77.2 33.6 %copy-start.1 = (bf16[8,16,768]{2,1,0:T(8,128)(2,1)S(1)}, bf16[8,16,768]{2,1,0:T(8,128)(2,1)}, u32[]{:S(2)}) copy-start(bf16[8,16,768]{2,1,0:T(8,128)(2,1)} %param.10) | copy-start | bytes 589828
  77.2 49.9 %copy-start.4 = (s32[2]{0:T(128)S(1)}, s32[2]{0:T(128)}, u32[]{:S(2)}) copy-start(s32[2]{0:T(128)} %off_ref.3) | copy-start | bytes 28
  112.0 15.1 %collective-permute-start.3 = (bf16[64,768]{1,0:T(8,128)(2,1)S(1)}, bf16[64,768]{1,0:T(8,128)(2,1)S(1)}, u32[]{:S(2)}, u32[]{:S(2)}) collective-permute-start(bf16[64,768]{1,0:T(8,128)(2,1)S(1)} %get-tuple-element.41), channel_id=1, source_target_pairs={{0,7},{1,0},{2,1},{3,2},{4,3},{5,4},{6,5},{7,6},{8,15},{9,8},{10,9... | collective-permute-start | bytes 294920 | tf_op jit(solution)/shard_map/ppermute | solution.py:339
  116.8 10.3 %collective-permute-start.4 = (bf16[32,768]{1,0:T(8,128)(2,1)S(1)}, bf16[32,768]{1,0:T(8,128)(2,1)S(1)}, u32[]{:S(2)}, u32[]{:S(2)}) collective-permute-start(bf16[32,768]{1,0:T(8,128)(2,1)S(1)} %get-tuple-element.42), channel_id=1, source_target_pairs={{0,504},{8,0},{16,8},{24,16},{32,24},{40,32},{48,40},{56,48},{64,5... | collective-permute-start | bytes 147464 | tf_op jit(solution)/shard_map/ppermute | solution.py:340
  121.0 6.0 %collective-permute-start.5 = (bf16[16,768]{1,0:T(8,128)(2,1)S(1)}, bf16[16,768]{1,0:T(8,128)(2,1)S(1)}, u32[]{:S(2)}, u32[]{:S(2)}) collective-permute-start(bf16[16,768]{1,0:T(8,128)(2,1)S(1)} %get-tuple-element.43), channel_id=1, source_target_pairs={{0,511},{1,504},{2,505},{3,506},{4,507},{5,508},{6,509},{7,510},{8... | collective-permute-start | bytes 73736 | tf_op jit(solution)/shard_map/ppermute | solution.py:341
Sparse Core Ops, SparseCore 0:
  10.7 45.5 all-gather.1
  77.3 39.3 reduce-scatter.1

commit v4 on v3

--- a/solution.py
+++ b/solution.py
@@ -8,12 +8,11 @@
 from jax.sharding import PartitionSpec as P
 
 CAP = 5
-SPARE = 48 << 20
 WIRE_ROWS = 8
 WIDE = 512
 EPS = 1e-05
 VMEM = pl.BlockSpec(memory_space=pltpu.VMEM)
-HBM = pl.BlockSpec(memory_space=pltpu.HBM)
+ANY = pl.BlockSpec(memory_space=pl.ANY)
 SMEM = pl.BlockSpec(memory_space=pltpu.SMEM)
 
 
@@ -35,6 +34,10 @@
 
 def t_dot(a, b):
     return lax.dot_general(a, b, (((0,), (0,)), ((), ())), preferred_element_type=jnp.float32)
+
+
+def in_hbm(x):
+    return pltpu.with_memory_space_constraint(x, pltpu.HBM)
 
 
 def call(body, outs, *args, flops=0, traffic=0, specs=None, **kw):
@@ -99,12 +102,36 @@
     copies[2].wait()
 
 
-def dispatch_g(tr, tc, off_ref, ids_ref, gates_ref, dout_ref, attn_ref, short_ref, sent_ref, mask_ref, meta_ref, x_ref, sel_ref):
-    tokens = dout_ref.shape[0]
+def dispatch_g(
+    off_hbm, ids_hbm, gates_hbm, dout_hbm, attn_hbm, short_hbm,
+    sent_ref, mask_ref, meta_ref, x_ref, sel_ref,
+    off_ref, ids_ref, gates_ref, dout_s, attn_s, short_s, sems,
+):
+    copies = [
+        pltpu.make_async_copy(src, dst, sems.at[i])
+        for i, (src, dst) in enumerate(
+            (
+                (off_hbm, off_ref),
+                (ids_hbm, ids_ref),
+                (gates_hbm, gates_ref),
+                (attn_hbm, attn_s),
+                (short_hbm, short_s),
+                (dout_hbm, dout_s),
+            )
+        )
+    ]
+    for copy in copies:
+        copy.start()
+    for copy in copies:
+        copy.wait()
+    tr, tc, width = attn_s.shape
+    tokens = tr * tc
     t = iota((tokens, 1), 0)
     inside, halo = places(t // tc - off_ref[0], t % tc - off_ref[1], tr, tc)
     sel_ref[...] = halo
-    x_ref[...] = short_ref[...].astype(jnp.float32) + dot(inside, attn_ref[...])
+    x_ref[...] = short_s[...].reshape(tokens, width).astype(jnp.float32) + dot(
+        inside, attn_s[...].reshape(tokens, width)
+    )
     n = sent_ref.shape[0]
     experts = n // WIRE_ROWS
     ids = ids_ref[...]
@@ -122,7 +149,7 @@
     table = jnp.where(at == 3, row1.astype(jnp.float32), table)
     meta = table.T
     meta_ref[...] = meta
-    dout = dout_ref[...].astype(jnp.float32)
+    dout = dout_s[...].reshape(tokens, width).astype(jnp.float32)
     sent = 0.0
     both = None
     for k, row in enumerate((row0, row1)):
@@ -178,24 +205,20 @@
     return wire_masks(row, (slots, wire) if dim else (wire, slots), dim)
 
 
-def experts_body(wire_ref, w_hbm, out_ref, grad_hbm, w_s, grad_s, u_s, g_s, in_sems, out_sems):
+def backward_body(
+    wire_ref, w_hbm, out_ref, u_hbm, g_hbm, a_ref, p_ref, w_s, u_ref, g_ref, sems, keep_sems
+):
     parts, _, part, width = w_s.shape
     half = parts // 2
     hidden = half * part
-    pieces = [(c, k) for c in range(2) for k in range(2)]
-    ins = [
+    copies = [
         pltpu.make_async_copy(
-            w_hbm.at[pl.ds(c * half, half), k], w_s.at[pl.ds(c * half, half), k], in_sems.at[i]
+            w_hbm.at[pl.ds(c * half, half), k], w_s.at[pl.ds(c * half, half), k], sems.at[2 * c + k]
         )
-        for i, (c, k) in enumerate(pieces)
+        for c in range(2)
+        for k in range(2)
     ]
-    outs = [
-        pltpu.make_async_copy(
-            grad_s.at[pl.ds(c * half, half), k], grad_hbm.at[pl.ds(c * half, half), k], out_sems.at[i]
-        )
-        for i, (c, k) in enumerate(pieces)
-    ]
-    for copy in ins:
+    for copy in copies:
         copy.start()
     n = wire_ref.shape[0]
     peers = min(32, n // WIRE_ROWS)
@@ -203,41 +226,96 @@
     blocks = n // rows
     masks = slot_masks(1, peers)
     for b in range(blocks):
-        for at, dst in ((0, g_s), (WIDE, u_s)):
+        for at, dst in ((0, g_ref), (WIDE, u_ref)):
             head, tail = from_wire(masks, wire_ref[b * rows : (b + 1) * rows, at : at + WIDE])
             dst[b * slots : (b + 1) * slots, :WIDE] = head.astype(jnp.bfloat16)
             dst[b * slots : (b + 1) * slots, WIDE:] = tail.astype(jnp.bfloat16)
-    u = u_s[...]
-    g = g_s[...]
+    keep = [
+        pltpu.make_async_copy(u_ref, u_hbm, keep_sems.at[0]),
+        pltpu.make_async_copy(g_ref, g_hbm, keep_sems.at[1]),
+    ]
+    for copy in keep:
+        copy.start()
+    u = u_ref[...]
+    g = g_ref[...]
 
     def weights(c, k):
         return w_s[c * half : (c + 1) * half, k].reshape(hidden, width)
 
     pairs = []
     for c in range(2):
-        ins[2 * c].wait()
+        copies[2 * c].wait()
         h = dot_t(u, weights(c, 0))
-        ins[2 * c + 1].wait()
+        copies[2 * c + 1].wait()
         pairs.append((h, dot_t(g, weights(c, 1))))
-    acts = []
+    q = None
     for c, (h, da) in enumerate(pairs):
         cdf = 0.5 * (1.0 + lax.erf(h * 0.7071067811865476))
         pdf = jnp.exp(-0.5 * h * h) * 0.3989422804014327
-        a = (h * cdf).astype(jnp.bfloat16)
         p = (da * (cdf + h * pdf)).astype(jnp.bfloat16)
-        acts.append((p, a))
-        for k, (left, right) in enumerate(((p, u), (a, g))):
-            grad = t_dot(left, right).astype(jnp.bfloat16)
+        a_ref[:, c * hidden : (c + 1) * hidden] = (h * cdf).astype(jnp.bfloat16)
+        p_ref[:, c * hidden : (c + 1) * hidden] = p
+        q_c = dot(p, weights(c, 0))
+        q = q_c if q is None else q + q_c
+    send_slots(q.astype(jnp.bfloat16), out_ref)
+    for copy in keep:
+        copy.wait()
+
+
+def send_slots(rows_of, out_ref):
+    n = out_ref.shape[0]
+    peers = min(32, n // WIRE_ROWS)
+    rows, slots = peers * WIRE_ROWS, peers * CAP
+    masks = slot_masks(0, peers)
+    for b in range(n // rows):
+        block = to_wire(masks, rows_of[b * slots : (b + 1) * slots], False)
+        out_ref[b * rows : (b + 1) * rows] = block.astype(jnp.bfloat16)
+
+
+def forward_body(a_ref, w_hbm, out_ref, w_s, sem):
+    parts, part, width = w_s.shape
+    fetch = pltpu.make_async_copy(w_hbm.at[:, 1], w_s, sem)
+    fetch.start()
+    fetch.wait()
+    y = dot(a_ref[...], w_s[...].reshape(parts * part, width))
+    send_slots(y.astype(jnp.bfloat16), out_ref)
+
+
+def gradients_body(u_hbm, g_hbm, a_ref, p_ref, grad_hbm, grad_s, u_ref, g_ref, sems, in_sems):
+    parts, _, part, width = grad_s.shape
+    half = parts // 2
+    hidden = half * part
+    ins = [
+        pltpu.make_async_copy(u_hbm, u_ref, in_sems.at[0]),
+        pltpu.make_async_copy(g_hbm, g_ref, in_sems.at[1]),
+    ]
+    for copy in ins:
+        copy.start()
+    for copy in ins:
+        copy.wait()
+    outs = []
+    for c in range(2):
+        for k, (left, right) in enumerate(((p_ref, u_ref), (a_ref, g_ref))):
+            grad = t_dot(left[:, c * hidden : (c + 1) * hidden], right[...]).astype(jnp.bfloat16)
+            at = pl.ds(c * half, half)
             grad_s[c * half : (c + 1) * half, k] = grad.reshape(half, part, width)
-            outs[2 * c + k].start()
-    q = dot(acts[0][0], weights(0, 0)) + dot(acts[1][0], weights(1, 0))
-    y = dot(acts[0][1], weights(0, 1)) + dot(acts[1][1], weights(1, 1))
-    masks = slot_masks(0, peers)
-    for at, src in ((0, q.astype(jnp.bfloat16)), (WIDE, y.astype(jnp.bfloat16))):
-        for b in range(blocks):
-            block = to_wire(masks, src[b * slots : (b + 1) * slots], False)
-            out_ref[b * rows : (b + 1) * rows, at : at + WIDE] = block.astype(jnp.bfloat16)
+            outs.append(pltpu.make_async_copy(grad_s.at[at, k], grad_hbm.at[at, k], sems.at[2 * c + k]))
+            outs[-1].start()
     for copy in outs:
+        copy.wait()
+
+
+def widen(grad_hbm, first_hbm, second_hbm, grad_s, wide_s, sems):
+    outs = (first_hbm, second_hbm)
+    fetch = [pltpu.make_async_copy(grad_hbm.at[:, k], grad_s.at[:, k], sems.at[k]) for k in range(2)]
+    store = [pltpu.make_async_copy(wide_s.at[:, k], outs[k], sems.at[2 + k]) for k in range(2)]
+    for copy in fetch:
+        copy.start()
+    for k in range(2):
+        fetch[k].wait()
+        wide_s[:, k] = grad_s[:, k].astype(jnp.float32)
+        store[k].start()
+    for copy in store:
         copy.wait()
 
 
@@ -246,33 +324,67 @@
     parts, _, part, width = w.shape
     slots = n // WIRE_ROWS * CAP
     hidden = parts * part
-    return pl.pallas_call(
-        experts_body,
+    bf16 = functools.partial(jax.ShapeDtypeStruct, dtype=jnp.bfloat16)
+    w = in_hbm(w)
+    q_wire, u, g, a, p = pl.pallas_call(
+        backward_body,
         out_shape=(
-            jax.ShapeDtypeStruct((n, 2 * WIDE), jnp.bfloat16),
-            jax.ShapeDtypeStruct(w.shape, jnp.bfloat16),
-        ),
-        in_specs=[VMEM, HBM],
-        out_specs=(VMEM, HBM),
+            bf16((n, WIDE)),
+            pltpu.HBM((slots, width), jnp.bfloat16),
+            pltpu.HBM((slots, width), jnp.bfloat16),
+            bf16((slots, hidden)),
+            bf16((slots, hidden)),
+        ),
+        in_specs=[VMEM, ANY],
+        out_specs=(VMEM, ANY, ANY, VMEM, VMEM),
         scratch_shapes=[
-            pltpu.VMEM(w.shape, jnp.bfloat16),
             pltpu.VMEM(w.shape, jnp.bfloat16),
             pltpu.VMEM((slots, width), jnp.bfloat16),
             pltpu.VMEM((slots, width), jnp.bfloat16),
             pltpu.SemaphoreType.DMA((4,)),
+            pltpu.SemaphoreType.DMA((2,)),
+        ],
+        compiler_params=pltpu.CompilerParams(vmem_limit_bytes=40 << 20),
+        cost_estimate=pl.CostEstimate(
+            flops=6 * slots * hidden * width,
+            bytes_accessed=4 * hidden * width,
+            transcendentals=2 * slots * hidden,
+        ),
+    )(wire, w)
+    grads = pl.pallas_call(
+        gradients_body,
+        out_shape=pltpu.HBM(w.shape, jnp.bfloat16),
+        in_specs=[ANY, ANY, VMEM, VMEM],
+        out_specs=ANY,
+        scratch_shapes=[
+            pltpu.VMEM(w.shape, jnp.bfloat16),
+            pltpu.VMEM((slots, width), jnp.bfloat16),
+            pltpu.VMEM((slots, width), jnp.bfloat16),
             pltpu.SemaphoreType.DMA((4,)),
+            pltpu.SemaphoreType.DMA((2,)),
         ],
-        compiler_params=pltpu.CompilerParams(vmem_limit_bytes=SPARE),
+        compiler_params=pltpu.CompilerParams(vmem_limit_bytes=40 << 20),
         cost_estimate=pl.CostEstimate(
-            flops=12 * slots * hidden * width,
-            bytes_accessed=8 * hidden * width,
-            transcendentals=2 * slots * hidden,
-        ),
-    )(wire, w)
+            flops=4 * slots * hidden * width, bytes_accessed=4 * hidden * width, transcendentals=0
+        ),
+    )(in_hbm(u), in_hbm(g), a, p)
+    a, grads = lax.optimization_barrier((a, grads))
+    y_wire = pl.pallas_call(
+        forward_body,
+        out_shape=bf16((n, WIDE)),
+        in_specs=[VMEM, ANY],
+        out_specs=VMEM,
+        scratch_shapes=[pltpu.VMEM((parts, part, width), jnp.bfloat16), pltpu.SemaphoreType.DMA],
+        compiler_params=pltpu.CompilerParams(vmem_limit_bytes=40 << 20),
+        cost_estimate=pl.CostEstimate(
+            flops=2 * slots * hidden * width, bytes_accessed=2 * hidden * width, transcendentals=0
+        ),
+    )(a, w)
+    return q_wire, y_wire, grads
 
 
 def combine_q(tr, tc, wire_ref, meta_ref, x_ref, dout_ref, ds_ref, keep_ref, up_ref, left_ref, corner_ref):
-    wire = wire_ref[:, :WIDE]
+    wire = wire_ref[...]
     tokens = x_ref.shape[0]
     both = None
     for k in range(2):
@@ -305,7 +417,7 @@
 
 
 def combine_y(wire_ref, meta_ref, x_ref, dout_ref, out_ref, dg_ref):
-    wire = wire_ref[:, WIDE:]
+    wire = wire_ref[...]
     dout = dout_ref[...].astype(jnp.float32)
     tokens = dout.shape[0]
     total = x_ref[...]
@@ -362,38 +474,60 @@
             bf16((16, width)),
             bf16((1, 2, part, width)),
         ),
-        in_specs=[HBM] * 3,
+        in_specs=[ANY] * 3,
         out_specs=(VMEM,) * 4,
         scratch_shapes=[pltpu.VMEM((tr, tc, width), jnp.bfloat16), pltpu.SemaphoreType.DMA((3,))],
-        compiler_params=pltpu.CompilerParams(vmem_limit_bytes=58 << 20),
+        compiler_params=pltpu.CompilerParams(vmem_limit_bytes=32 * 1024 * 1024),
         cost_estimate=pl.CostEstimate(flops=1 << 25, bytes_accessed=1 << 21, transcendentals=0),
-    )(attn_win, w_in.transpose(0, 2, 1), w_out)
+    )(in_hbm(attn_win), in_hbm(w_in.transpose(0, 2, 1)), in_hbm(w_out))
     w_all = lax.all_gather(w_own, "dp", axis=0, tiled=True)
     up, left, corner = edges(up, left, corner, 1)
-    g_wire, masks, meta, x0, sel = call(
-        functools.partial(dispatch_g, tr, tc),
-        (
+    g_wire, masks, meta, x0, sel = pl.pallas_call(
+        dispatch_g,
+        out_shape=(
             bf16((n, WIDE)),
             bf16((3, n, tokens)),
             f32((tokens, tokens)),
             f32((tokens, width)),
             bf16((tokens, 4 * tc + 4 * tr + 16)),
         ),
-        shift_offsets, ids, gates, dout, attn_win.reshape(tokens, width), shortcut.reshape(tokens, width),
-        specs=[SMEM] + [VMEM] * 5,
-        flops=4 * 256 * n * WIDE, traffic=1 << 20,
-    )
+        in_specs=[ANY] * 6,
+        out_specs=(VMEM,) * 5,
+        scratch_shapes=[
+            pltpu.SMEM((2,), jnp.int32),
+            pltpu.VMEM((2, tokens), jnp.int32),
+            pltpu.VMEM((2, tokens), jnp.float32),
+        ]
+        + [pltpu.VMEM((tr, tc, width), jnp.bfloat16)] * 3
+        + [pltpu.SemaphoreType.DMA((6,))],
+        compiler_params=pltpu.CompilerParams(vmem_limit_bytes=32 * 1024 * 1024),
+        cost_estimate=pl.CostEstimate(
+            flops=4 * 256 * n * WIDE, bytes_accessed=1 << 20, transcendentals=0
+        ),
+    )(*(in_hbm(v) for v in (shift_offsets, ids, gates, d_out, attn_win, shortcut)))
     sent, x = call(
         dispatch_u,
         (bf16((n, 2 * WIDE)), f32((tokens, width))),
         g_wire, masks, x0, sel, up, left, corner,
         flops=4 * 128 * n * WIDE, traffic=1 << 21,
     )
-    returned, grads = experts(exchange(sent, n_ex), w_all)
-    returned = exchange(returned, n_ex)
+    q_wire, y_wire, grads = experts(exchange(sent, n_ex), w_all)
+    rq = exchange(q_wire, n_ex)
+    ry = exchange(y_wire, n_ex)
     grad = lax.psum_scatter(grads, "dp", scatter_dimension=0, tiled=True)
-    grad_in = grad[:, 0].transpose(0, 2, 1).astype(jnp.float32)
-    grad_out = grad[:, 1].astype(jnp.float32)
+    grad_in, grad_out = pl.pallas_call(
+        widen,
+        out_shape=(pltpu.HBM((1, part, width), jnp.float32),) * 2,
+        in_specs=[ANY],
+        out_specs=(ANY,) * 2,
+        scratch_shapes=[
+            pltpu.VMEM(grad.shape, jnp.bfloat16),
+            pltpu.VMEM(grad.shape, jnp.float32),
+            pltpu.SemaphoreType.DMA((4,)),
+        ],
+        compiler_params=pltpu.CompilerParams(vmem_limit_bytes=32 * 1024 * 1024),
+        cost_estimate=pl.CostEstimate(flops=0, bytes_accessed=12 * part * width, transcendentals=0),
+    )(in_hbm(grad))
     ds, ds_keep, up_b, left_b, corner_b = call(
         functools.partial(combine_q, tr, tc),
         (
@@ -403,16 +537,10 @@
             bf16((4 * tr, width)),
             bf16((16, width)),
         ),
-        returned, meta, x, dout,
-        flops=4 * tokens * n * WIDE, traffic=1 << 21,
+        rq, meta, x, dout,
+        flops=1 << 40, traffic=1 << 21,
     )
     down, right, corner_r = edges(up_b, left_b, corner_b, -1)
-    block_out, d_gates = call(
-        combine_y,
-        (bf16((tokens, width)), f32((2, tokens))),
-        returned, meta, x, dout,
-        flops=8 * tokens * n * WIDE, traffic=1 << 21,
-    )
     d_attn = call(
         functools.partial(roll_back, tr, tc),
         bf16((tokens, width)),
@@ -420,13 +548,20 @@
         specs=[SMEM] + [VMEM] * 4,
         flops=2 * tokens * 256 * width, traffic=1 << 19,
     )
+    x, d_attn = lax.optimization_barrier((x, d_attn))
+    block_out, d_gates = call(
+        combine_y,
+        (bf16((tokens, width)), f32((2, tokens))),
+        ry, meta, x, dout,
+        flops=8 * tokens * n * WIDE, traffic=1 << 21,
+    )
     tile = (tr, tc, width)
     return (
         block_out.reshape(tile),
         ds.reshape(tile),
         d_attn.reshape(tile),
         d_gates.T.reshape(1, 1, tokens, 2),
-        grad_in,
+        grad_in.transpose(0, 2, 1),
         grad_out,
     )
 

time: 138 us -> 142 us (1.029); the launches traced: 138 us -> 139 us
  blocking collectives: 72.5 us -> 36.1 us
  starting transfers between devices: 20.1 us -> 38 us
  waiting for transfers between devices: 5.74 us -> 22.2 us
  Pallas kernels: 18.1 us -> 29 us
  local copies, waits for them, and re-layouts: 4.8 us -> 0.01 us
  other arithmetic: 2.14 us -> 0 us
    all_to_all x2 -> x1, blocking collectives: 72.5 us -> 36.1 us  [exchange(): lax.all_to_all(blocks, 'expert', split_axis=0, concat_axis=0, tiled=True)]
    all_to_all x0 -> x2, starting transfers between devices: none -> 16.2 us  [exchange(): lax.all_to_all(blocks, 'expert', split_axis=0, concat_axis=0, tiled=True)]
    pallas_call x1 -> x5, Pallas kernels: 9.31 us -> 21.1 us  [the longest x1 7.29 us: experts(): pl.pallas_call(backward_body, out_shape=(bf16((n, WIDE)), pltpu.HBM((slot...]
    all_to_all x0 -> x2, waiting for transfers between devices: none -> 6.19 us  [exchange(): lax.all_to_all(blocks, 'expert', split_axis=0, concat_axis=0, tiled=True)]
    reduce_scatter x1, waiting for transfers between devices: 0.01 us -> 5.93 us  [per_device(): grad = lax.psum_scatter(grads, 'dp', scatter_dimension=0, tiled=True)]
    unnamed x16 -> x4, local copies, waits for them, and re-layouts: 4.8 us -> 0.01 us
    ppermute x2, waiting for transfers between devices: 5.69 us -> 10.1 us  [edges(): lax.ppermute(corner, ('expert', 'dp'), by_both)]
    ppermute x2, starting transfers between devices: 7.41 us -> 9.94 us  [edges(): lax.ppermute(col_edge, 'expert', by_ex)]
  transfers between devices with their start and end apart: 8 -> 10, of which waited for: 2 -> 4; matrix products, arithmetic and copies ran while one was open for 0% -> 0% of each run, Pallas kernels for 5% -> 13%
where the time goes in v4:
time: 142 us; the launch traced here: 139 us
  starting transfers between devices  38 us (27%)
  blocking collectives  36.1 us (25%)
  Pallas kernels  29 us (20%)
  waiting for transfers between devices  22.2 us (16%)
  between operations  14.2 us (10%)
    all_to_all x1, blocking collectives, exchange(): lax.all_to_all(blocks, 'expert', split_axis=0, concat_axis=0, tiled=True)  36.1 us
    all_to_all x2, starting transfers between devices, exchange(): lax.all_to_all(blocks, 'expert', split_axis=0, concat_axis=0, tiled=True)  16.2 us
    ppermute x2, waiting for transfers between devices, edges(): lax.ppermute(corner, ('expert', 'dp'), by_both)  10.1 us
    ppermute x2, starting transfers between devices, edges(): lax.ppermute(col_edge, 'expert', by_ex)  9.94 us
    pallas_call x1, Pallas kernels, experts(): pl.pallas_call(backward_body, out_shape=(bf16((n, WIDE)), pltpu.HBM((slot...  7.29 us
    ppermute x2, starting transfers between devices, edges(): lax.ppermute(corner, ('expert', 'dp'), by_both)  6.48 us
    all_to_all x2, waiting for transfers between devices, exchange(): lax.all_to_all(blocks, 'expert', split_axis=0, concat_axis=0, tiled=True)  6.19 us
    reduce_scatter x1, waiting for transfers between devices, per_device(): grad = lax.psum_scatter(grads, 'dp', scatter_dimension=0, tiled=True)  5.93 us
  transfers between devices with their start and end apart: 10, of which 4 were waited for; matrix products, arithmetic and copies ran while one was open for 0% of the time, Pallas kernels for 13%

profile of v4, /device:TPU:1, one launch (start us, length us, event | category | flops | bytes accessed | tf_op | source)
XLA Modules:
  0.0 139.5 jit_solution(12834072912706890234)
XLA Ops:
  7.2 0.0 all-gather.2.cloned.1.call-start
  7.2 2.0 %shard_map.128 = (bf16[64,768]{1,0:T(8,128)(2,1)S(1)}, bf16[32,768]{1,0:T(8,128)(2,1)S(1)}, bf16[16,768]{1,0:T(8,128)(2,1)S(1)}, bf16[1,2,192,768]{3,2,1,0:T(8,128)(2,1)}) custom-call(bf16[8,16,768]{2,1,0:T(8,128)(2,1)} %attn_hbm.3, bf16[1,192,768]{2,1,0:T(8,128)(2,1)} %bitcast.26, bf16[1,192,768]{2,1,0:T(8,128)(2,1)} %w2_hbm.1), custom_call_target="tpu_custom_call" | custom-call | flops 33554432 | bytes 2097152 | tf_op jit(solution)/shard_map/pallas_call | solution.py:469
  9.2 0.0 all-gather.2.cloned.1.call-update
  9.2 2.6 %collective-permute-start = (bf16[64,768]{1,0:T(8,128)(2,1)S(1)}, bf16[64,768]{1,0:T(8,128)(2,1)S(1)}, u32[]{:S(2)}, u32[]{:S(2)}) collective-permute-start(bf16[64,768]{1,0:T(8,128)(2,1)S(1)} %get-tuple-element.39), channel_id=1, source_target_pairs={{0,1},{1,2},{2,3},{3,4},{4,5},{5,6},{6,7},{7,0},{8,9},{9,10},{10,1... | collective-permute-start | bytes 294920 | tf_op jit(solution)/shard_map/ppermute | solution.py:451
  11.9 3.2 %collective-permute-start.1 = (bf16[32,768]{1,0:T(8,128)(2,1)S(1)}, bf16[32,768]{1,0:T(8,128)(2,1)S(1)}, u32[]{:S(2)}, u32[]{:S(2)}) collective-permute-start(bf16[32,768]{1,0:T(8,128)(2,1)S(1)} %get-tuple-element.40), channel_id=1, source_target_pairs={{0,8},{8,16},{16,24},{24,32},{32,40},{40,48},{48,56},{56,64},{64,7... | collective-permute-start | bytes 147464 | tf_op jit(solution)/shard_map/ppermute | solution.py:452
  15.1 3.2 %collective-permute-start.2 = (bf16[16,768]{1,0:T(8,128)(2,1)S(1)}, bf16[16,768]{1,0:T(8,128)(2,1)S(1)}, u32[]{:S(2)}, u32[]{:S(2)}) collective-permute-start(bf16[16,768]{1,0:T(8,128)(2,1)S(1)} %get-tuple-element.41), channel_id=1, source_target_pairs={{0,9},{1,10},{2,11},{3,12},{4,13},{5,14},{6,15},{7,8},{8,17},{9,18... | collective-permute-start | bytes 73736 | tf_op jit(solution)/shard_map/ppermute | solution.py:453
  18.3 2.5 %shard_map.127 = (bf16[512,512]{1,0:T(8,128)(2,1)S(1)}, bf16[3,512,128]{2,1,0:T(8,128)(2,1)S(1)}, f32[128,128]{1,0:T(8,128)S(1)}, f32[128,768]{1,0:T(8,128)S(1)}, bf16[128,112]{1,0:T(8,128)(2,1)S(1)}) custom-call(s32[2]{0:T(128)} %off_ref.1, s32[2,128]{1,0:T(2,128)} %bitcast.30, f32[2,128]{1,0:T(2,128)} %bitcast.31, bf16[8,16,768]{2,1,0:T(8,128)(2,1)} %dout_hbm.1, ...), custom_call_target="tpu_custom_call" | custom-call | flops 268435456 | bytes 1048576 | tf_op jit(solution)/shard_map/pallas_call | solution.py:485
  20.8 6.9 %collective-permute-done.2.corner_ref = bf16[16,768]{1,0:T(8,128)(2,1)S(1)} collective-permute-done((bf16[16,768]{1,0:T(8,128)(2,1)S(1)}, bf16[16,768]{1,0:T(8,128)(2,1)S(1)}, u32[]{:S(2)}, u32[]{:S(2)}) %collective-permute-start.2) | collective-permute-done | bytes 24608 | tf_op jit(solution)/shard_map/ppermute | solution.py:453
  27.7 0.0 collective-permute-done.1.left_ref
  27.7 0.0 collective-permute-done.up_ref
  27.7 0.8 shard_map.129
  28.5 36.1 %all_to_all.15 = bf16[64,8,1024]{2,1,0:T(8,128)(2,1)S(1)} all-to-all(bf16[64,8,1024]{2,1,0:T(8,128)(2,1)S(1)} %bitcast.22), channel_id=1, replica_groups=mesh['expert'=64,'dp'=8] {'expert'}, dimensions={0} | all-to-all | bytes 2097152 | tf_op jit(solution)/shard_map/all_to_all | solution.py:437
  64.6 0.0 all-gather.2.cloned.1.call-done.w_hbm
  64.6 7.3 %shard_map.130 = (bf16[512,512]{1,0:T(8,128)(2,1)}, bf16[320,768]{1,0:T(8,128)(2,1)}, bf16[320,768]{1,0:T(8,128)(2,1)}, bf16[320,1536]{1,0:T(8,128)(2,1)S(1)}, bf16[320,1536]{1,0:T(8,128)(2,1)S(1)}) custom-call(bf16[512,1024]{1,0:T(8,128)(2,1)S(1)} %bitcast.21, bf16[8,2,192,768]{3,2,1,0:T(8,128)(2,1)} %all-gather.2.cloned.1.call-done.w_hbm), custom_call_target="tpu_custom_call" | custom-call | flops 2264924160 | bytes 4718592 | tf_op jit(solution)/shard_map/pallas_call | solution.py:329
  71.9 8.2 %all-to-all-start.2 = ((bf16[64,8,512]{2,1,0:T(8,128)(2,1)}), bf16[64,8,512]{2,1,0:T(8,128)(2,1)S(1)}, u32[]{:S(2)}, u32[]{:S(2)}) async-start(bf16[64,8,512]{2,1,0:T(8,128)(2,1)} %bitcast.9), calls=%async_computation.2 | async-start | bytes 1048576 | tf_op jit(solution)/shard_map/all_to_all | solution.py:437
  80.1 0.0 reduce-scatter.2.cloned.1.call-start
  80.2 5.0 %shard_map.131 = bf16[8,2,192,768]{3,2,1,0:T(8,128)(2,1)} custom-call(bf16[320,768]{1,0:T(8,128)(2,1)} %get-tuple-element.45.u_hbm, bf16[320,768]{1,0:T(8,128)(2,1)} %get-tuple-element.46.g_hbm, bf16[320,1536]{1,0:T(8,128)(2,1)S(1)} %get-tuple-element.48.a_ref, bf16[320,1536]{1,0:T(8,128)(2,1)S(1)} %get-tuple-element.47.p_ref), custom_call_target="tpu_custom_call" | custom-call | flops 1509949440 | bytes 4718592 | tf_op jit(solution)/shard_map/pallas_call | solution.py:354
  85.2 0.0 reduce-scatter.2.cloned.1.call-update
  85.2 0.0 copy-start
  85.2 4.3 %shard_map.132 = bf16[512,512]{1,0:T(8,128)(2,1)} custom-call(bf16[320,1536]{1,0:T(8,128)(2,1)S(1)} %get-tuple-element.48.a_ref, bf16[8,2,192,768]{3,2,1,0:T(8,128)(2,1)} %all-gather.2.cloned.1.call-done.w_hbm), custom_call_target="tpu_custom_call" | custom-call | flops 754974720 | bytes 2359296 | tf_op jit(solution)/shard_map/pallas_call | solution.py:372
  89.5 6.2 %all-to-all-done.2 = bf16[64,8,512]{2,1,0:T(8,128)(2,1)S(1)} async-done(((bf16[64,8,512]{2,1,0:T(8,128)(2,1)}), bf16[64,8,512]{2,1,0:T(8,128)(2,1)S(1)}, u32[]{:S(2)}, u32[]{:S(2)}) %all-to-all-start.2) | async-done | bytes 524320 | tf_op jit(solution)/shard_map/all_to_all | solution.py:437
  95.7 8.0 %all-to-all-start.1 = ((bf16[64,8,512]{2,1,0:T(8,128)(2,1)}), bf16[64,8,512]{2,1,0:T(8,128)(2,1)}, u32[]{:S(2)}, u32[]{:S(2)}) async-start(bf16[64,8,512]{2,1,0:T(8,128)(2,1)} %bitcast.7), calls=%async_computation.1 | async-start | bytes 1048576 | tf_op jit(solution)/shard_map/all_to_all | solution.py:437
  103.7 0.0 copy-done
  103.7 0.0 copy-start.1
  103.7 1.3 shard_map.133
  105.0 2.6 %collective-permute-start.3 = (bf16[64,768]{1,0:T(8,128)(2,1)S(1)}, bf16[64,768]{1,0:T(8,128)(2,1)S(1)}, u32[]{:S(2)}, u32[]{:S(2)}) collective-permute-start(bf16[64,768]{1,0:T(8,128)(2,1)S(1)} %get-tuple-element.53), channel_id=1, source_target_pairs={{0,7},{1,0},{2,1},{3,2},{4,3},{5,4},{6,5},{7,6},{8,15},{9,8},{10,9... | collective-permute-start | bytes 294920 | tf_op jit(solution)/shard_map/ppermute | solution.py:451
  107.6 6.7 %collective-permute-start.4 = (bf16[32,768]{1,0:T(8,128)(2,1)S(1)}, bf16[32,768]{1,0:T(8,128)(2,1)S(1)}, u32[]{:S(2)}, u32[]{:S(2)}) collective-permute-start(bf16[32,768]{1,0:T(8,128)(2,1)S(1)} %get-tuple-element.54), channel_id=1, source_target_pairs={{0,504},{8,0},{16,8},{24,16},{32,24},{40,32},{48,40},{56,48},{64,5... | collective-permute-start | bytes 147464 | tf_op jit(solution)/shard_map/ppermute | solution.py:452
  114.3 3.3 %collective-permute-start.5 = (bf16[16,768]{1,0:T(8,128)(2,1)S(1)}, bf16[16,768]{1,0:T(8,128)(2,1)S(1)}, u32[]{:S(2)}, u32[]{:S(2)}) collective-permute-start(bf16[16,768]{1,0:T(8,128)(2,1)S(1)} %get-tuple-element.55), channel_id=1, source_target_pairs={{0,511},{1,504},{2,505},{3,506},{4,507},{5,508},{6,509},{7,510},{8... | collective-permute-start | bytes 73736 | tf_op jit(solution)/shard_map/ppermute | solution.py:453
  117.6 3.2 %collective-permute-done.5.corner_ref = bf16[16,768]{1,0:T(8,128)(2,1)S(1)} collective-permute-done((bf16[16,768]{1,0:T(8,128)(2,1)S(1)}, bf16[16,768]{1,0:T(8,128)(2,1)S(1)}, u32[]{:S(2)}, u32[]{:S(2)}) %collective-permute-start.5) | collective-permute-done | bytes 24608 | tf_op jit(solution)/shard_map/ppermute | solution.py:453
  120.8 0.0 collective-permute-done.4.right_ref
  120.8 0.0 collective-permute-done.3.down_ref
  120.8 0.0 copy-done.1
  120.8 1.5 %shard_map.134 = bf16[128,768]{1,0:T(8,128)(2,1)} custom-call(s32[2]{0:T(128)S(1)} %copy-done.1, bf16[128,768]{1,0:T(8,128)(2,1)S(1)} %get-tuple-element.52.ds_ref, bf16[64,768]{1,0:T(8,128)(2,1)S(1)} %collective-permute-done.3.down_ref, bf16[32,768]{1,0:T(8,128)(2,1)S(1)} %collective-permute-done.4.right_ref, ...), custom_call_target="tpu_custom_call" | custom-call | flops 50331648 | bytes 524288 | tf_op jit(solution)/shard_map/pallas_call | solution.py:44
  122.3 0.0 all-to-all-done.1
  122.3 2.3 %shard_map.135 = (bf16[128,768]{1,0:T(8,128)(2,1)}, f32[2,128]{1,0:T(2,128)}) custom-call(bf16[512,512]{1,0:T(8,128)(2,1)} %bitcast.8.wire_ref, f32[128,128]{1,0:T(8,128)S(1)} %get-tuple-element.49.meta_ref, f32[128,768]{1,0:T(8,128)S(1)} %get-tuple-element.56.x_ref, bf16[128,768]{1,0:T(8,128)(2,1)S(1)} %bitcast.25), custom_call_target="tpu_custom_call" | custom-call | flops 268435456 | bytes 2097152 | tf_op jit(solution)/shard_map/pallas_call | solution.py:44
  124.6 5.9 %reduce-scatter.2.cloned.1.call-done.grad_hbm = bf16[1,2,192,768]{3,2,1,0:T(8,128)(2,1)} async-done(((bf16[8,2,192,768]{3,2,1,0:T(8,128)(2,1)}), bf16[1,2,192,768]{3,2,1,0:T(8,128)(2,1)}) %reduce-scatter.2.cloned.1.call-update) | async-done | bytes 589840 | tf_op jit(solution)/shard_map/reduce_scatter | solution.py:517
  130.6 2.0 %shard_map.136 = (f32[1,192,768]{2,1,0:T(8,128)}, f32[1,192,768]{2,1,0:T(8,128)}) custom-call(bf16[1,2,192,768]{3,2,1,0:T(8,128)(2,1)} %reduce-scatter.2.cloned.1.call-done.grad_hbm), custom_call_target="tpu_custom_call" | custom-call | bytes 1769472 | tf_op jit(solution)/shard_map/pallas_call | solution.py:518
Async XLA Ops:
  7.2 57.4 %all-gather.2.cloned.1.call-start = ((), (), s32[]{:S(2)}) async-start(), calls=%async_computation.4 | async-start | bytes 5308416 | tf_op jit(solution)/shard_map/all_gather | solution.py:483
  9.2 18.4 %collective-permute-start = (bf16[64,768]{1,0:T(8,128)(2,1)S(1)}, bf16[64,768]{1,0:T(8,128)(2,1)S(1)}, u32[]{:S(2)}, u32[]{:S(2)}) collective-permute-start(bf16[64,768]{1,0:T(8,128)(2,1)S(1)} %get-tuple-element.39), channel_id=1, source_target_pairs={{0,1},{1,2},{2,3},{3,4},{4,5},{5,6},{6,7},{7,0},{8,9},{9,10},{10,1... | collective-permute-start | bytes 294920 | tf_op jit(solution)/shard_map/ppermute | solution.py:451
  11.9 15.8 %collective-permute-start.1 = (bf16[32,768]{1,0:T(8,128)(2,1)S(1)}, bf16[32,768]{1,0:T(8,128)(2,1)S(1)}, u32[]{:S(2)}, u32[]{:S(2)}) collective-permute-start(bf16[32,768]{1,0:T(8,128)(2,1)S(1)} %get-tuple-element.40), channel_id=1, source_target_pairs={{0,8},{8,16},{16,24},{24,32},{32,40},{40,48},{48,56},{56,64},{64,7... | collective-permute-start | bytes 147464 | tf_op jit(solution)/shard_map/ppermute | solution.py:452
  15.1 12.6 %collective-permute-start.2 = (bf16[16,768]{1,0:T(8,128)(2,1)S(1)}, bf16[16,768]{1,0:T(8,128)(2,1)S(1)}, u32[]{:S(2)}, u32[]{:S(2)}) collective-permute-start(bf16[16,768]{1,0:T(8,128)(2,1)S(1)} %get-tuple-element.41), channel_id=1, source_target_pairs={{0,9},{1,10},{2,11},{3,12},{4,13},{5,14},{6,15},{7,8},{8,17},{9,18... | collective-permute-start | bytes 73736 | tf_op jit(solution)/shard_map/ppermute | solution.py:453
  71.9 23.8 %all-to-all-start.2 = ((bf16[64,8,512]{2,1,0:T(8,128)(2,1)}), bf16[64,8,512]{2,1,0:T(8,128)(2,1)S(1)}, u32[]{:S(2)}, u32[]{:S(2)}) async-start(bf16[64,8,512]{2,1,0:T(8,128)(2,1)} %bitcast.9), calls=%async_computation.2 | async-start | bytes 1048576 | tf_op jit(solution)/shard_map/all_to_all | solution.py:437
  80.1 50.4 %reduce-scatter.2.cloned.1.call-start = ((), (), s32[]{:S(2)}) async-start(), calls=%async_computation.5 | async-start | bytes 5308416 | tf_op jit(solution)/shard_map/reduce_scatter | solution.py:517
  85.2 18.5 %copy-start = (bf16[8,16,768]{2,1,0:T(8,128)(2,1)S(1)}, bf16[8,16,768]{2,1,0:T(8,128)(2,1)}, u32[]{:S(2)}) copy-start(bf16[8,16,768]{2,1,0:T(8,128)(2,1)} %dout_hbm.1) | copy-start | bytes 589828
  95.7 26.6 %all-to-all-start.1 = ((bf16[64,8,512]{2,1,0:T(8,128)(2,1)}), bf16[64,8,512]{2,1,0:T(8,128)(2,1)}, u32[]{:S(2)}, u32[]{:S(2)}) async-start(bf16[64,8,512]{2,1,0:T(8,128)(2,1)} %bitcast.7), calls=%async_computation.1 | async-start | bytes 1048576 | tf_op jit(solution)/shard_map/all_to_all | solution.py:437
  103.7 17.1 %copy-start.1 = (s32[2]{0:T(128)S(1)}, s32[2]{0:T(128)}, u32[]{:S(2)}) copy-start(s32[2]{0:T(128)} %off_ref.1) | copy-start | bytes 28
  105.0 15.8 %collective-permute-start.3 = (bf16[64,768]{1,0:T(8,128)(2,1)S(1)}, bf16[64,768]{1,0:T(8,128)(2,1)S(1)}, u32[]{:S(2)}, u32[]{:S(2)}) collective-permute-start(bf16[64,768]{1,0:T(8,128)(2,1)S(1)} %get-tuple-element.53), channel_id=1, source_target_pairs={{0,7},{1,0},{2,1},{3,2},{4,3},{5,4},{6,5},{7,6},{8,15},{9,8},{10,9... | collective-permute-start | bytes 294920 | tf_op jit(solution)/shard_map/ppermute | solution.py:451
  107.6 13.2 %collective-permute-start.4 = (bf16[32,768]{1,0:T(8,128)(2,1)S(1)}, bf16[32,768]{1,0:T(8,128)(2,1)S(1)}, u32[]{:S(2)}, u32[]{:S(2)}) collective-permute-start(bf16[32,768]{1,0:T(8,128)(2,1)S(1)} %get-tuple-element.54), channel_id=1, source_target_pairs={{0,504},{8,0},{16,8},{24,16},{32,24},{40,32},{48,40},{56,48},{64,5... | collective-permute-start | bytes 147464 | tf_op jit(solution)/shard_map/ppermute | solution.py:452
  114.3 6.4 %collective-permute-start.5 = (bf16[16,768]{1,0:T(8,128)(2,1)S(1)}, bf16[16,768]{1,0:T(8,128)(2,1)S(1)}, u32[]{:S(2)}, u32[]{:S(2)}) collective-permute-start(bf16[16,768]{1,0:T(8,128)(2,1)S(1)} %get-tuple-element.55), channel_id=1, source_target_pairs={{0,511},{1,504},{2,505},{3,506},{4,507},{5,508},{6,509},{7,510},{8... | collective-permute-start | bytes 73736 | tf_op jit(solution)/shard_map/ppermute | solution.py:453
Sparse Core Ops, SparseCore 0:
  10.7 45.5 all-gather.1
  85.3 45.1 reduce-scatter.1

commit v5 on v3

--- a/solution.py
+++ b/solution.py
@@ -8,12 +8,11 @@
 from jax.sharding import PartitionSpec as P
 
 CAP = 5
-SPARE = 48 << 20
 WIRE_ROWS = 8
 WIDE = 512
 EPS = 1e-05
 VMEM = pl.BlockSpec(memory_space=pltpu.VMEM)
-HBM = pl.BlockSpec(memory_space=pltpu.HBM)
+ANY = pl.BlockSpec(memory_space=pl.ANY)
 SMEM = pl.BlockSpec(memory_space=pltpu.SMEM)
 
 
@@ -35,6 +34,10 @@
 
 def t_dot(a, b):
     return lax.dot_general(a, b, (((0,), (0,)), ((), ())), preferred_element_type=jnp.float32)
+
+
+def in_hbm(x):
+    return pltpu.with_memory_space_constraint(x, pltpu.HBM)
 
 
 def call(body, outs, *args, flops=0, traffic=0, specs=None, **kw):
@@ -99,12 +102,36 @@
     copies[2].wait()
 
 
-def dispatch_g(tr, tc, off_ref, ids_ref, gates_ref, dout_ref, attn_ref, short_ref, sent_ref, mask_ref, meta_ref, x_ref, sel_ref):
-    tokens = dout_ref.shape[0]
+def dispatch_g(
+    off_hbm, ids_hbm, gates_hbm, dout_hbm, attn_hbm, short_hbm,
+    sent_ref, mask_ref, meta_ref, x_ref, sel_ref,
+    off_ref, ids_ref, gates_ref, dout_s, attn_s, short_s, sems,
+):
+    copies = [
+        pltpu.make_async_copy(src, dst, sems.at[i])
+        for i, (src, dst) in enumerate(
+            (
+                (off_hbm, off_ref),
+                (ids_hbm, ids_ref),
+                (gates_hbm, gates_ref),
+                (attn_hbm, attn_s),
+                (short_hbm, short_s),
+                (dout_hbm, dout_s),
+            )
+        )
+    ]
+    for copy in copies:
+        copy.start()
+    for copy in copies:
+        copy.wait()
+    tr, tc, width = attn_s.shape
+    tokens = tr * tc
     t = iota((tokens, 1), 0)
     inside, halo = places(t // tc - off_ref[0], t % tc - off_ref[1], tr, tc)
     sel_ref[...] = halo
-    x_ref[...] = short_ref[...].astype(jnp.float32) + dot(inside, attn_ref[...])
+    x_ref[...] = short_s[...].reshape(tokens, width).astype(jnp.float32) + dot(
+        inside, attn_s[...].reshape(tokens, width)
+    )
     n = sent_ref.shape[0]
     experts = n // WIRE_ROWS
     ids = ids_ref[...]
@@ -122,7 +149,7 @@
     table = jnp.where(at == 3, row1.astype(jnp.float32), table)
     meta = table.T
     meta_ref[...] = meta
-    dout = dout_ref[...].astype(jnp.float32)
+    dout = dout_s[...].reshape(tokens, width).astype(jnp.float32)
     sent = 0.0
     both = None
     for k, row in enumerate((row0, row1)):
@@ -176,6 +203,16 @@
     row = (s % peers) * WIRE_ROWS + s // peers
     wire = peers * WIRE_ROWS
     return wire_masks(row, (slots, wire) if dim else (wire, slots), dim)
+
+
+def send_slots(rows_of, out_ref, at):
+    n = out_ref.shape[0]
+    peers = min(32, n // WIRE_ROWS)
+    rows, slots = peers * WIRE_ROWS, peers * CAP
+    masks = slot_masks(0, peers)
+    for b in range(n // rows):
+        block = to_wire(masks, rows_of[b * slots : (b + 1) * slots], False)
+        out_ref[b * rows : (b + 1) * rows, at : at + WIDE] = block.astype(jnp.bfloat16)
 
 
 def experts_body(wire_ref, w_hbm, out_ref, grad_hbm, w_s, grad_s, u_s, g_s, in_sems, out_sems):
@@ -200,9 +237,8 @@
     n = wire_ref.shape[0]
     peers = min(32, n // WIRE_ROWS)
     rows, slots = peers * WIRE_ROWS, peers * CAP
-    blocks = n // rows
     masks = slot_masks(1, peers)
-    for b in range(blocks):
+    for b in range(n // rows):
         for at, dst in ((0, g_s), (WIDE, u_s)):
             head, tail = from_wire(masks, wire_ref[b * rows : (b + 1) * rows, at : at + WIDE])
             dst[b * slots : (b + 1) * slots, :WIDE] = head.astype(jnp.bfloat16)
@@ -232,11 +268,8 @@
             outs[2 * c + k].start()
     q = dot(acts[0][0], weights(0, 0)) + dot(acts[1][0], weights(1, 0))
     y = dot(acts[0][1], weights(0, 1)) + dot(acts[1][1], weights(1, 1))
-    masks = slot_masks(0, peers)
-    for at, src in ((0, q.astype(jnp.bfloat16)), (WIDE, y.astype(jnp.bfloat16))):
-        for b in range(blocks):
-            block = to_wire(masks, src[b * slots : (b + 1) * slots], False)
-            out_ref[b * rows : (b + 1) * rows, at : at + WIDE] = block.astype(jnp.bfloat16)
+    send_slots(q.astype(jnp.bfloat16), out_ref, 0)
+    send_slots(y.astype(jnp.bfloat16), out_ref, WIDE)
     for copy in outs:
         copy.wait()
 
@@ -250,10 +283,10 @@
         experts_body,
         out_shape=(
             jax.ShapeDtypeStruct((n, 2 * WIDE), jnp.bfloat16),
-            jax.ShapeDtypeStruct(w.shape, jnp.bfloat16),
-        ),
-        in_specs=[VMEM, HBM],
-        out_specs=(VMEM, HBM),
+            pltpu.HBM(w.shape, jnp.bfloat16),
+        ),
+        in_specs=[VMEM, ANY],
+        out_specs=(VMEM, ANY),
         scratch_shapes=[
             pltpu.VMEM(w.shape, jnp.bfloat16),
             pltpu.VMEM(w.shape, jnp.bfloat16),
@@ -262,13 +295,13 @@
             pltpu.SemaphoreType.DMA((4,)),
             pltpu.SemaphoreType.DMA((4,)),
         ],
-        compiler_params=pltpu.CompilerParams(vmem_limit_bytes=SPARE),
+        compiler_params=pltpu.CompilerParams(vmem_limit_bytes=40 << 20),
         cost_estimate=pl.CostEstimate(
             flops=12 * slots * hidden * width,
             bytes_accessed=8 * hidden * width,
             transcendentals=2 * slots * hidden,
         ),
-    )(wire, w)
+    )(wire, in_hbm(w))
 
 
 def combine_q(tr, tc, wire_ref, meta_ref, x_ref, dout_ref, ds_ref, keep_ref, up_ref, left_ref, corner_ref):
@@ -304,20 +337,37 @@
     out_ref[...] = (dot(inside, ds_ref[...]) + dot(halo, edge)).astype(jnp.bfloat16)
 
 
-def combine_y(wire_ref, meta_ref, x_ref, dout_ref, out_ref, dg_ref):
+def combine_y(
+    wire_ref, meta_ref, x_ref, dout_ref, grad_hbm, out_ref, dg_ref, first_hbm, second_hbm,
+    grad_s, wide_s, sems,
+):
+    wides = (first_hbm, second_hbm)
+    fetch = [pltpu.make_async_copy(grad_hbm.at[:, k], grad_s.at[:, k], sems.at[k]) for k in range(2)]
+    store = [pltpu.make_async_copy(wide_s.at[:, k], wides[k], sems.at[2 + k]) for k in range(2)]
+    for copy in fetch:
+        copy.start()
     wire = wire_ref[:, WIDE:]
     dout = dout_ref[...].astype(jnp.float32)
     tokens = dout.shape[0]
+    masks = [
+        wire_masks(meta_ref[:, 2 + k : 3 + k].astype(jnp.int32), (tokens, wire.shape[0]), 1)
+        for k in range(2)
+    ]
+    ys = [jnp.concatenate(from_wire(m, wire), axis=1) for m in masks]
+    for k in range(2):
+        fetch[k].wait()
+        wide_s[:, k] = grad_s[:, k].astype(jnp.float32)
+        store[k].start()
     total = x_ref[...]
     lane = iota((tokens, tokens), 1)
     table = jnp.zeros((tokens, tokens), jnp.float32)
-    for k in range(2):
-        row = meta_ref[:, 2 + k : 3 + k].astype(jnp.int32)
-        y = jnp.concatenate(from_wire(wire_masks(row, (tokens, wire.shape[0]), 1), wire), axis=1)
+    for k, y in enumerate(ys):
         total = total + meta_ref[:, k : k + 1] * y
         table = jnp.where(lane == k, jnp.sum(dout * y, axis=-1, keepdims=True), table)
     out_ref[...] = total.astype(jnp.bfloat16)
     dg_ref[...] = table.T[:2]
+    for copy in store:
+        copy.wait()
 
 
 def exchange(wire, n):
@@ -362,27 +412,37 @@
             bf16((16, width)),
             bf16((1, 2, part, width)),
         ),
-        in_specs=[HBM] * 3,
+        in_specs=[ANY] * 3,
         out_specs=(VMEM,) * 4,
         scratch_shapes=[pltpu.VMEM((tr, tc, width), jnp.bfloat16), pltpu.SemaphoreType.DMA((3,))],
-        compiler_params=pltpu.CompilerParams(vmem_limit_bytes=58 << 20),
+        compiler_params=pltpu.CompilerParams(vmem_limit_bytes=32 * 1024 * 1024),
         cost_estimate=pl.CostEstimate(flops=1 << 25, bytes_accessed=1 << 21, transcendentals=0),
-    )(attn_win, w_in.transpose(0, 2, 1), w_out)
+    )(in_hbm(attn_win), in_hbm(w_in.transpose(0, 2, 1)), in_hbm(w_out))
     w_all = lax.all_gather(w_own, "dp", axis=0, tiled=True)
     up, left, corner = edges(up, left, corner, 1)
-    g_wire, masks, meta, x0, sel = call(
-        functools.partial(dispatch_g, tr, tc),
-        (
+    g_wire, masks, meta, x0, sel = pl.pallas_call(
+        dispatch_g,
+        out_shape=(
             bf16((n, WIDE)),
             bf16((3, n, tokens)),
             f32((tokens, tokens)),
             f32((tokens, width)),
             bf16((tokens, 4 * tc + 4 * tr + 16)),
         ),
-        shift_offsets, ids, gates, dout, attn_win.reshape(tokens, width), shortcut.reshape(tokens, width),
-        specs=[SMEM] + [VMEM] * 5,
-        flops=4 * 256 * n * WIDE, traffic=1 << 20,
-    )
+        in_specs=[ANY] * 6,
+        out_specs=(VMEM,) * 5,
+        scratch_shapes=[
+            pltpu.SMEM((2,), jnp.int32),
+            pltpu.VMEM((2, tokens), jnp.int32),
+            pltpu.VMEM((2, tokens), jnp.float32),
+        ]
+        + [pltpu.VMEM((tr, tc, width), jnp.bfloat16)] * 3
+        + [pltpu.SemaphoreType.DMA((6,))],
+        compiler_params=pltpu.CompilerParams(vmem_limit_bytes=32 * 1024 * 1024),
+        cost_estimate=pl.CostEstimate(
+            flops=4 * 256 * n * WIDE, bytes_accessed=1 << 20, transcendentals=0
+        ),
+    )(*(in_hbm(v) for v in (shift_offsets, ids, gates, d_out, attn_win, shortcut)))
     sent, x = call(
         dispatch_u,
         (bf16((n, 2 * WIDE)), f32((tokens, width))),
@@ -392,8 +452,6 @@
     returned, grads = experts(exchange(sent, n_ex), w_all)
     returned = exchange(returned, n_ex)
     grad = lax.psum_scatter(grads, "dp", scatter_dimension=0, tiled=True)
-    grad_in = grad[:, 0].transpose(0, 2, 1).astype(jnp.float32)
-    grad_out = grad[:, 1].astype(jnp.float32)
     ds, ds_keep, up_b, left_b, corner_b = call(
         functools.partial(combine_q, tr, tc),
         (
@@ -407,12 +465,23 @@
         flops=4 * tokens * n * WIDE, traffic=1 << 21,
     )
     down, right, corner_r = edges(up_b, left_b, corner_b, -1)
-    block_out, d_gates = call(
+    block_out, d_gates, grad_in, grad_out = pl.pallas_call(
         combine_y,
-        (bf16((tokens, width)), f32((2, tokens))),
-        returned, meta, x, dout,
-        flops=8 * tokens * n * WIDE, traffic=1 << 21,
-    )
+        out_shape=(bf16((tokens, width)), f32((2, tokens)))
+        + (pltpu.HBM((1, part, width), jnp.float32),) * 2,
+        in_specs=[VMEM] * 4 + [ANY],
+        out_specs=(VMEM, VMEM, ANY, ANY),
+        scratch_shapes=[
+            pltpu.VMEM(grad.shape, jnp.bfloat16),
+            pltpu.VMEM(grad.shape, jnp.float32),
+            pltpu.SemaphoreType.DMA((4,)),
+        ],
+        compiler_params=pltpu.CompilerParams(vmem_limit_bytes=32 * 1024 * 1024),
+        cost_estimate=pl.CostEstimate(
+            flops=8 * tokens * n * WIDE, bytes_accessed=1 << 21, transcendentals=0
+        ),
+    )(returned, meta, x, dout, in_hbm(grad))
+    ds_keep, block_out = lax.optimization_barrier((ds_keep, block_out))
     d_attn = call(
         functools.partial(roll_back, tr, tc),
         bf16((tokens, width)),
@@ -426,7 +495,7 @@
         ds.reshape(tile),
         d_attn.reshape(tile),
         d_gates.T.reshape(1, 1, tokens, 2),
-        grad_in,
+        grad_in.transpose(0, 2, 1),
         grad_out,
     )
 

time: 138 us -> 133 us (0.964)
  local copies, waits for them, and re-layouts: 4.8 us -> 0.01 us
  blocking collectives: 72.5 us -> 70 us
  waiting for transfers between devices: 5.74 us -> 8.02 us
  Pallas kernels: 18.1 us -> 20.3 us
  other arithmetic: 2.14 us -> 0 us
    pallas_call x0 -> x2, Pallas kernels: none -> 5.39 us  [the longest x1 2.92 us: per_device(): pl.pallas_call(combine_y, out_shape=(bf16((tokens, width)), f32((2, token...]
    unnamed x16 -> x4, local copies, waits for them, and re-layouts: 4.8 us -> 0.01 us
    pallas_call x5 -> x3, Pallas kernels: 6.7 us -> 3.58 us  [call(): pl.pallas_call(body, out_shape=outs, in_specs=[VMEM] * len(args) if specs...]
    all_to_all x2, blocking collectives: 72.5 us -> 70 us  [exchange(): lax.all_to_all(blocks, 'expert', split_axis=0, concat_axis=0, tiled=True)]
    ppermute x2, waiting for transfers between devices: 5.69 us -> 7.96 us  [edges(): lax.ppermute(corner, ('expert', 'dp'), by_both)]
    convert_element_type x1 -> x0, other arithmetic: 2.14 us -> none  [per_device(): grad_out = grad[:, 1].astype(jnp.float32)]
  transfers between devices with their start and end apart: 8 -> 8, of which waited for: 2 -> 2; matrix products, arithmetic and copies ran while one was open for 0% -> 0% of each run, Pallas kernels for 5% -> 6%
where the time goes in v5:
time: 133 us
  blocking collectives  70 us (53%)
  starting transfers between devices  20.4 us (15%)
  Pallas kernels  20.3 us (15%)
  between operations  14.1 us (11%)
  waiting for transfers between devices  8.02 us (6%)
    all_to_all x2, blocking collectives, exchange(): lax.all_to_all(blocks, 'expert', split_axis=0, concat_axis=0, tiled=True)  70 us
    pallas_call x1, Pallas kernels, experts(): pl.pallas_call(experts_body, out_shape=(jax.ShapeDtypeStruct((n, 2 * WIDE...  9.31 us
    ppermute x2, waiting for transfers between devices, edges(): lax.ppermute(corner, ('expert', 'dp'), by_both)  7.96 us
    ppermute x2, starting transfers between devices, edges(): lax.ppermute(row_edge, 'dp', by_dp)  7.71 us
    ppermute x2, starting transfers between devices, edges(): lax.ppermute(col_edge, 'expert', by_ex)  7.34 us
    ppermute x2, starting transfers between devices, edges(): lax.ppermute(corner, ('expert', 'dp'), by_both)  5.24 us
    pallas_call x3, Pallas kernels, call(): pl.pallas_call(body, out_shape=outs, in_specs=[VMEM] * len(args) if specs...  3.58 us
    pallas_call x1, Pallas kernels, per_device(): pl.pallas_call(combine_y, out_shape=(bf16((tokens, width)), f32((2, token...  2.92 us
  transfers between devices with their start and end apart: 8, of which 2 were waited for; matrix products, arithmetic and copies ran while one was open for 0% of the time, Pallas kernels for 6%

profile of v5, /device:TPU:1, one launch (start us, length us, event | category | flops | bytes accessed | tf_op | source)
XLA Modules:
  0.0 132.8 jit_solution(3557656326685502084)
XLA Ops:
  7.2 0.0 all-gather.2.cloned.1.call-start
  7.2 2.0 %shard_map.128 = (bf16[64,768]{1,0:T(8,128)(2,1)S(1)}, bf16[32,768]{1,0:T(8,128)(2,1)S(1)}, bf16[16,768]{1,0:T(8,128)(2,1)S(1)}, bf16[1,2,192,768]{3,2,1,0:T(8,128)(2,1)}) custom-call(bf16[8,16,768]{2,1,0:T(8,128)(2,1)} %attn_hbm.3, bf16[1,192,768]{2,1,0:T(8,128)(2,1)} %bitcast.26, bf16[1,192,768]{2,1,0:T(8,128)(2,1)} %w2_hbm.1), custom_call_target="tpu_custom_call" | custom-call | flops 33554432 | bytes 2097152 | tf_op jit(solution)/shard_map/pallas_call | solution.py:407
  9.2 0.0 all-gather.2.cloned.1.call-update
  9.2 0.0 reduce-scatter.2.cloned.1.call-start
  9.3 2.6 %collective-permute-start = (bf16[64,768]{1,0:T(8,128)(2,1)S(1)}, bf16[64,768]{1,0:T(8,128)(2,1)S(1)}, u32[]{:S(2)}, u32[]{:S(2)}) collective-permute-start(bf16[64,768]{1,0:T(8,128)(2,1)S(1)} %get-tuple-element.34), channel_id=1, source_target_pairs={{0,1},{1,2},{2,3},{3,4},{4,5},{5,6},{6,7},{7,0},{8,9},{9,10},{10,1... | collective-permute-start | bytes 294920 | tf_op jit(solution)/shard_map/ppermute | solution.py:389
  11.9 3.2 %collective-permute-start.1 = (bf16[32,768]{1,0:T(8,128)(2,1)S(1)}, bf16[32,768]{1,0:T(8,128)(2,1)S(1)}, u32[]{:S(2)}, u32[]{:S(2)}) collective-permute-start(bf16[32,768]{1,0:T(8,128)(2,1)S(1)} %get-tuple-element.35), channel_id=1, source_target_pairs={{0,8},{8,16},{16,24},{24,32},{32,40},{40,48},{48,56},{56,64},{64,7... | collective-permute-start | bytes 147464 | tf_op jit(solution)/shard_map/ppermute | solution.py:390
  15.1 3.2 %collective-permute-start.2 = (bf16[16,768]{1,0:T(8,128)(2,1)S(1)}, bf16[16,768]{1,0:T(8,128)(2,1)S(1)}, u32[]{:S(2)}, u32[]{:S(2)}) collective-permute-start(bf16[16,768]{1,0:T(8,128)(2,1)S(1)} %get-tuple-element.36), channel_id=1, source_target_pairs={{0,9},{1,10},{2,11},{3,12},{4,13},{5,14},{6,15},{7,8},{8,17},{9,18... | collective-permute-start | bytes 73736 | tf_op jit(solution)/shard_map/ppermute | solution.py:391
  18.3 2.5 %shard_map.127 = (bf16[512,512]{1,0:T(8,128)(2,1)S(1)}, bf16[3,512,128]{2,1,0:T(8,128)(2,1)S(1)}, f32[128,128]{1,0:T(8,128)S(1)}, f32[128,768]{1,0:T(8,128)S(1)}, bf16[128,112]{1,0:T(8,128)(2,1)S(1)}) custom-call(s32[2]{0:T(128)} %off_ref.1, s32[2,128]{1,0:T(2,128)} %bitcast.31, f32[2,128]{1,0:T(2,128)} %bitcast.32, bf16[8,16,768]{2,1,0:T(8,128)(2,1)} %dout_hbm.1, ...), custom_call_target="tpu_custom_call" | custom-call | flops 268435456 | bytes 1048576 | tf_op jit(solution)/shard_map/pallas_call | solution.py:423
  20.8 6.9 %collective-permute-done.2.corner_ref = bf16[16,768]{1,0:T(8,128)(2,1)S(1)} collective-permute-done((bf16[16,768]{1,0:T(8,128)(2,1)S(1)}, bf16[16,768]{1,0:T(8,128)(2,1)S(1)}, u32[]{:S(2)}, u32[]{:S(2)}) %collective-permute-start.2) | collective-permute-done | bytes 24608 | tf_op jit(solution)/shard_map/ppermute | solution.py:391
  27.7 0.0 collective-permute-done.1.left_ref
  27.7 0.0 collective-permute-done.up_ref
  27.7 0.8 shard_map.129
  28.5 36.1 %all_to_all.10 = bf16[64,8,1024]{2,1,0:T(8,128)(2,1)S(1)} all-to-all(bf16[64,8,1024]{2,1,0:T(8,128)(2,1)S(1)} %bitcast.22), channel_id=1, replica_groups=mesh['expert'=64,'dp'=8] {'expert'}, dimensions={0} | all-to-all | bytes 2097152 | tf_op jit(solution)/shard_map/all_to_all | solution.py:375
  64.6 0.0 all-gather.2.cloned.1.call-done.w_hbm
  64.6 9.3 %shard_map.130 = (bf16[512,1024]{1,0:T(8,128)(2,1)S(1)}, bf16[8,2,192,768]{3,2,1,0:T(8,128)(2,1)}) custom-call(bf16[512,1024]{1,0:T(8,128)(2,1)S(1)} %bitcast.23, bf16[8,2,192,768]{3,2,1,0:T(8,128)(2,1)} %all-gather.2.cloned.1.call-done.w_hbm), custom_call_target="tpu_custom_call" | custom-call | flops 4529848320 | bytes 9437184 | tf_op jit(solution)/shard_map/pallas_call | solution.py:282
  73.9 0.0 copy-start
  74.0 0.0 copy-start.1
  74.0 0.0 reduce-scatter.2.cloned.1.call-update
  74.0 33.9 %all_to_all.11 = bf16[64,8,1024]{2,1,0:T(8,128)(2,1)S(1)} all-to-all(bf16[64,8,1024]{2,1,0:T(8,128)(2,1)S(1)} %bitcast.21), channel_id=1, replica_groups=mesh['expert'=64,'dp'=8] {'expert'}, dimensions={0} | all-to-all | bytes 2097152 | tf_op jit(solution)/shard_map/all_to_all | solution.py:375
  107.9 0.0 copy-done
  107.9 1.3 shard_map.131
  109.1 5.1 %collective-permute-start.3 = (bf16[64,768]{1,0:T(8,128)(2,1)S(1)}, bf16[64,768]{1,0:T(8,128)(2,1)S(1)}, u32[]{:S(2)}, u32[]{:S(2)}) collective-permute-start(bf16[64,768]{1,0:T(8,128)(2,1)S(1)} %get-tuple-element.48), channel_id=1, source_target_pairs={{0,7},{1,0},{2,1},{3,2},{4,3},{5,4},{6,5},{7,6},{8,15},{9,8},{10,9... | collective-permute-start | bytes 294920 | tf_op jit(solution)/shard_map/ppermute | solution.py:389
  114.3 4.1 %collective-permute-start.4 = (bf16[32,768]{1,0:T(8,128)(2,1)S(1)}, bf16[32,768]{1,0:T(8,128)(2,1)S(1)}, u32[]{:S(2)}, u32[]{:S(2)}) collective-permute-start(bf16[32,768]{1,0:T(8,128)(2,1)S(1)} %get-tuple-element.49), channel_id=1, source_target_pairs={{0,504},{8,0},{16,8},{24,16},{32,24},{40,32},{48,40},{56,48},{64,5... | collective-permute-start | bytes 147464 | tf_op jit(solution)/shard_map/ppermute | solution.py:390
  118.4 2.0 %collective-permute-start.5 = (bf16[16,768]{1,0:T(8,128)(2,1)S(1)}, bf16[16,768]{1,0:T(8,128)(2,1)S(1)}, u32[]{:S(2)}, u32[]{:S(2)}) collective-permute-start(bf16[16,768]{1,0:T(8,128)(2,1)S(1)} %get-tuple-element.50), channel_id=1, source_target_pairs={{0,511},{1,504},{2,505},{3,506},{4,507},{5,508},{6,509},{7,510},{8... | collective-permute-start | bytes 73736 | tf_op jit(solution)/shard_map/ppermute | solution.py:391
  120.4 0.0 reduce-scatter.2.cloned.1.call-done.grad_hbm
  120.5 2.9 %shard_map.132 = (bf16[128,768]{1,0:T(8,128)(2,1)}, f32[2,128]{1,0:T(2,128)}, f32[1,192,768]{2,1,0:T(8,128)}, f32[1,192,768]{2,1,0:T(8,128)}) custom-call(bf16[512,1024]{1,0:T(8,128)(2,1)S(1)} %bitcast.20, f32[128,128]{1,0:T(8,128)S(1)} %get-tuple-element.40.meta_ref, f32[128,768]{1,0:T(8,128)S(1)} %get-tuple-element.41.x_ref, ...), custom_call_target="tpu_custom_call" | custom-call | flops 268435456 | bytes 2097152 | tf_op jit(solution)/shard_map/pallas_call | solution.py:468
  123.4 1.1 collective-permute-done.5.corner_ref
  124.5 0.0 collective-permute-done.4.right_ref
  124.5 0.0 collective-permute-done.3.down_ref
  124.5 0.0 copy-done.1
  124.5 1.5 %shard_map.133 = bf16[128,768]{1,0:T(8,128)(2,1)} custom-call(s32[2]{0:T(128)S(1)} %copy-done.1, bf16[128,768]{1,0:T(8,128)(2,1)S(1)} %get-tuple-element.47.ds_ref, bf16[64,768]{1,0:T(8,128)(2,1)S(1)} %collective-permute-done.3.down_ref, bf16[32,768]{1,0:T(8,128)(2,1)S(1)} %collective-permute-done.4.right_ref, ...), custom_call_target="tpu_custom_call" | custom-call | flops 50331648 | bytes 524288 | tf_op jit(solution)/shard_map/pallas_call | solution.py:44
Async XLA Ops:
  7.2 57.5 %all-gather.2.cloned.1.call-start = ((), (), s32[]{:S(2)}) async-start(), calls=%async_computation.3 | async-start | bytes 5308416 | tf_op jit(solution)/shard_map/all_gather | solution.py:421
  9.2 111.2 %reduce-scatter.2.cloned.1.call-start = ((), (), s32[]{:S(2)}) async-start(), calls=%async_computation.4 | async-start | bytes 5308416 | tf_op jit(solution)/shard_map/reduce_scatter | solution.py:454
  9.3 18.4 %collective-permute-start = (bf16[64,768]{1,0:T(8,128)(2,1)S(1)}, bf16[64,768]{1,0:T(8,128)(2,1)S(1)}, u32[]{:S(2)}, u32[]{:S(2)}) collective-permute-start(bf16[64,768]{1,0:T(8,128)(2,1)S(1)} %get-tuple-element.34), channel_id=1, source_target_pairs={{0,1},{1,2},{2,3},{3,4},{4,5},{5,6},{6,7},{7,0},{8,9},{9,10},{10,1... | collective-permute-start | bytes 294920 | tf_op jit(solution)/shard_map/ppermute | solution.py:389
  11.9 15.8 %collective-permute-start.1 = (bf16[32,768]{1,0:T(8,128)(2,1)S(1)}, bf16[32,768]{1,0:T(8,128)(2,1)S(1)}, u32[]{:S(2)}, u32[]{:S(2)}) collective-permute-start(bf16[32,768]{1,0:T(8,128)(2,1)S(1)} %get-tuple-element.35), channel_id=1, source_target_pairs={{0,8},{8,16},{16,24},{24,32},{32,40},{40,48},{48,56},{56,64},{64,7... | collective-permute-start | bytes 147464 | tf_op jit(solution)/shard_map/ppermute | solution.py:390
  15.1 12.6 %collective-permute-start.2 = (bf16[16,768]{1,0:T(8,128)(2,1)S(1)}, bf16[16,768]{1,0:T(8,128)(2,1)S(1)}, u32[]{:S(2)}, u32[]{:S(2)}) collective-permute-start(bf16[16,768]{1,0:T(8,128)(2,1)S(1)} %get-tuple-element.36), channel_id=1, source_target_pairs={{0,9},{1,10},{2,11},{3,12},{4,13},{5,14},{6,15},{7,8},{8,17},{9,18... | collective-permute-start | bytes 73736 | tf_op jit(solution)/shard_map/ppermute | solution.py:391
  73.9 33.9 %copy-start = (bf16[8,16,768]{2,1,0:T(8,128)(2,1)S(1)}, bf16[8,16,768]{2,1,0:T(8,128)(2,1)}, u32[]{:S(2)}) copy-start(bf16[8,16,768]{2,1,0:T(8,128)(2,1)} %dout_hbm.1) | copy-start | bytes 589828
  74.0 50.5 %copy-start.1 = (s32[2]{0:T(128)S(1)}, s32[2]{0:T(128)}, u32[]{:S(2)}) copy-start(s32[2]{0:T(128)} %off_ref.1) | copy-start | bytes 28
  109.1 15.3 %collective-permute-start.3 = (bf16[64,768]{1,0:T(8,128)(2,1)S(1)}, bf16[64,768]{1,0:T(8,128)(2,1)S(1)}, u32[]{:S(2)}, u32[]{:S(2)}) collective-permute-start(bf16[64,768]{1,0:T(8,128)(2,1)S(1)} %get-tuple-element.48), channel_id=1, source_target_pairs={{0,7},{1,0},{2,1},{3,2},{4,3},{5,4},{6,5},{7,6},{8,15},{9,8},{10,9... | collective-permute-start | bytes 294920 | tf_op jit(solution)/shard_map/ppermute | solution.py:389
  114.3 10.2 %collective-permute-start.4 = (bf16[32,768]{1,0:T(8,128)(2,1)S(1)}, bf16[32,768]{1,0:T(8,128)(2,1)S(1)}, u32[]{:S(2)}, u32[]{:S(2)}) collective-permute-start(bf16[32,768]{1,0:T(8,128)(2,1)S(1)} %get-tuple-element.49), channel_id=1, source_target_pairs={{0,504},{8,0},{16,8},{24,16},{32,24},{40,32},{48,40},{56,48},{64,5... | collective-permute-start | bytes 147464 | tf_op jit(solution)/shard_map/ppermute | solution.py:390
  118.4 6.0 %collective-permute-start.5 = (bf16[16,768]{1,0:T(8,128)(2,1)S(1)}, bf16[16,768]{1,0:T(8,128)(2,1)S(1)}, u32[]{:S(2)}, u32[]{:S(2)}) collective-permute-start(bf16[16,768]{1,0:T(8,128)(2,1)S(1)} %get-tuple-element.50), channel_id=1, source_target_pairs={{0,511},{1,504},{2,505},{3,506},{4,507},{5,508},{6,509},{7,510},{8... | collective-permute-start | bytes 73736 | tf_op jit(solution)/shard_map/ppermute | solution.py:391
Sparse Core Ops, SparseCore 0:
  10.7 45.5 all-gather.1
  74.1 39.9 reduce-scatter.1

commit v6 on v5

--- a/solution.py
+++ b/solution.py
@@ -78,33 +78,25 @@
     return f(head, rows[:, :WIDE]) + jnp.concatenate([f(left, tail), f(right, tail)], axis=1)
 
 
-def prepare(attn_hbm, w1_hbm, w2_hbm, up_ref, left_ref, corner_ref, w_ref, attn_s, sems):
-    copies = [
-        pltpu.make_async_copy(src, dst, sems.at[i])
-        for i, (src, dst) in enumerate(
-            ((attn_hbm, attn_s), (w1_hbm, w_ref.at[:, 0]), (w2_hbm, w_ref.at[:, 1]))
-        )
-    ]
-    for copy in copies:
-        copy.start()
+def prepare(attn_hbm, up_ref, left_ref, corner_ref, attn_s, sem):
+    copy = pltpu.make_async_copy(attn_hbm, attn_s, sem)
+    copy.start()
     tr, tc, width = attn_s.shape
     tokens = tr * tc
     n = 4 * tr
     s = iota((n, 1), 0)
     edge = ones_where((s // 4) * tc + tc - 4 + s % 4 == iota((n, tokens), 1))
-    copies[0].wait()
+    copy.wait()
     attn = attn_s[...].reshape(tokens, width)
     up_ref[...] = attn[tokens - 4 * tc :]
     left = dot(edge, attn).astype(jnp.bfloat16)
     left_ref[...] = left
     corner_ref[...] = left[n - 16 :]
-    copies[1].wait()
-    copies[2].wait()
 
 
 def dispatch_g(
-    off_hbm, ids_hbm, gates_hbm, dout_hbm, attn_hbm, short_hbm,
-    sent_ref, mask_ref, meta_ref, x_ref, sel_ref,
+    off_hbm, ids_hbm, gates_hbm, dout_hbm, attn_hbm, short_hbm, w1_hbm, w2_hbm,
+    sent_ref, mask_ref, meta_ref, x_ref, sel_ref, w_ref,
     off_ref, ids_ref, gates_ref, dout_s, attn_s, short_s, sems,
 ):
     copies = [
@@ -117,12 +109,14 @@
                 (attn_hbm, attn_s),
                 (short_hbm, short_s),
                 (dout_hbm, dout_s),
+                (w1_hbm, w_ref.at[0:1]),
+                (w2_hbm, w_ref.at[1:2]),
             )
         )
     ]
     for copy in copies:
         copy.start()
-    for copy in copies:
+    for copy in copies[:6]:
         copy.wait()
     tr, tc, width = attn_s.shape
     tokens = tr * tc
@@ -159,6 +153,8 @@
     for m in range(3):
         mask_ref[m] = both[m]
     sent_ref[...] = sent.astype(jnp.bfloat16)
+    for copy in copies[6:]:
+        copy.wait()
 
 
 def normalize(x):
@@ -215,22 +211,21 @@
         out_ref[b * rows : (b + 1) * rows, at : at + WIDE] = block.astype(jnp.bfloat16)
 
 
-def experts_body(wire_ref, w_hbm, out_ref, grad_hbm, w_s, grad_s, u_s, g_s, in_sems, out_sems):
-    parts, _, part, width = w_s.shape
-    half = parts // 2
+def experts_body(wire_ref, *refs):
+    half = (len(refs) - 9) // 2
+    pieces_hbm = refs[: 2 * half]
+    out_ref, *grads_hbm, w_s, grad_s, u_s, g_s, in_sems, out_sems = refs[2 * half :]
+    _, _, part, width = w_s.shape
     hidden = half * part
-    pieces = [(c, k) for c in range(2) for k in range(2)]
     ins = [
-        pltpu.make_async_copy(
-            w_hbm.at[pl.ds(c * half, half), k], w_s.at[pl.ds(c * half, half), k], in_sems.at[i]
-        )
-        for i, (c, k) in enumerate(pieces)
+        pltpu.make_async_copy(piece, w_s.at[i], in_sems.at[i]) for i, piece in enumerate(pieces_hbm)
     ]
     outs = [
         pltpu.make_async_copy(
-            grad_s.at[pl.ds(c * half, half), k], grad_hbm.at[pl.ds(c * half, half), k], out_sems.at[i]
+            grad_s.at[pl.ds(c * half, half), k], grads_hbm[c].at[:, k], out_sems.at[2 * c + k]
         )
-        for i, (c, k) in enumerate(pieces)
+        for c in range(2)
+        for k in range(2)
     ]
     for copy in ins:
         copy.start()
@@ -251,9 +246,9 @@
 
     pairs = []
     for c in range(2):
-        ins[2 * c].wait()
+        for copy in ins[c * half : (c + 1) * half]:
+            copy.wait()
         h = dot_t(u, weights(c, 0))
-        ins[2 * c + 1].wait()
         pairs.append((h, dot_t(g, weights(c, 1))))
     acts = []
     for c, (h, da) in enumerate(pairs):
@@ -274,25 +269,24 @@
         copy.wait()
 
 
-def experts(wire, w):
+def experts(wire, mine, theirs):
     n = wire.shape[0]
-    parts, _, part, width = w.shape
+    _, part, width = mine[0].shape
+    half = len(mine)
     slots = n // WIRE_ROWS * CAP
-    hidden = parts * part
+    hidden = 2 * half * part
     return pl.pallas_call(
         experts_body,
-        out_shape=(
-            jax.ShapeDtypeStruct((n, 2 * WIDE), jnp.bfloat16),
-            pltpu.HBM(w.shape, jnp.bfloat16),
-        ),
-        in_specs=[VMEM, ANY],
-        out_specs=(VMEM, ANY),
+        out_shape=(jax.ShapeDtypeStruct((n, 2 * WIDE), jnp.bfloat16),)
+        + (pltpu.HBM((half, 2, part, width), jnp.bfloat16),) * 2,
+        in_specs=[VMEM] + [ANY] * (2 * half),
+        out_specs=(VMEM, ANY, ANY),
         scratch_shapes=[
-            pltpu.VMEM(w.shape, jnp.bfloat16),
-            pltpu.VMEM(w.shape, jnp.bfloat16),
+            pltpu.VMEM((2 * half, 2, part, width), jnp.bfloat16),
+            pltpu.VMEM((2 * half, 2, part, width), jnp.bfloat16),
             pltpu.VMEM((slots, width), jnp.bfloat16),
             pltpu.VMEM((slots, width), jnp.bfloat16),
-            pltpu.SemaphoreType.DMA((4,)),
+            pltpu.SemaphoreType.DMA((2 * half,)),
             pltpu.SemaphoreType.DMA((4,)),
         ],
         compiler_params=pltpu.CompilerParams(vmem_limit_bytes=40 << 20),
@@ -301,7 +295,75 @@
             bytes_accessed=8 * hidden * width,
             transcendentals=2 * slots * hidden,
         ),
-    )(wire, in_hbm(w))
+    )(wire, *(in_hbm(v) for v in (*mine, *theirs)))
+
+
+def relay_body(*refs):
+    n = len(refs) // 2
+    sems = refs[-1]
+    copies = [
+        pltpu.make_async_copy(src, dst, sems.at[i])
+        for i, (src, dst) in enumerate(zip(refs[:n], refs[n : 2 * n]))
+    ]
+    for copy in copies:
+        copy.start()
+    for copy in copies:
+        copy.wait()
+
+
+def relay(pieces):
+    return pl.pallas_call(
+        relay_body,
+        out_shape=tuple(pltpu.HBM(v.shape, v.dtype) for v in pieces),
+        in_specs=[VMEM] * len(pieces),
+        out_specs=(ANY,) * len(pieces),
+        scratch_shapes=[pltpu.SemaphoreType.DMA((len(pieces),))],
+        compiler_params=pltpu.CompilerParams(vmem_limit_bytes=24 << 20),
+        cost_estimate=pl.CostEstimate(flops=12 << 30, bytes_accessed=1 << 22, transcendentals=0),
+    )(*pieces)
+
+
+def pair_sum_body(mine_hbm, swapped_hbm, *refs):
+    half = mine_hbm.shape[0]
+    outs = refs[:half]
+    a_s, b_s, kept_s, sum_s, in_sems, out_sems = refs[half:]
+    ins = [
+        pltpu.make_async_copy(src.at[d], dst.at[d], in_sems.at[2 * d + k])
+        for d in range(half)
+        for k, (src, dst) in enumerate(((mine_hbm, a_s), (swapped_hbm, b_s)))
+    ]
+    stores = [pltpu.make_async_copy(kept_s, outs[0], out_sems.at[0])] + [
+        pltpu.make_async_copy(sum_s.at[d], outs[d], out_sems.at[d]) for d in range(1, half)
+    ]
+    for copy in ins:
+        copy.start()
+    for d in (*range(1, half), 0):
+        ins[2 * d].wait()
+        ins[2 * d + 1].wait()
+        total = a_s[d].astype(jnp.float32) + b_s[d].astype(jnp.float32)
+        if d == 0:
+            kept_s[...] = total
+        else:
+            sum_s[d] = total.astype(jnp.bfloat16)
+        stores[d].start()
+    for copy in stores:
+        copy.wait()
+
+
+def pair_sum(mine, swapped):
+    half, *rest = mine.shape
+    return pl.pallas_call(
+        pair_sum_body,
+        out_shape=(pltpu.HBM(tuple(rest), jnp.float32),)
+        + (pltpu.HBM(tuple(rest), jnp.bfloat16),) * (half - 1),
+        in_specs=[ANY] * 2,
+        out_specs=(ANY,) * half,
+        scratch_shapes=[pltpu.VMEM(mine.shape, jnp.bfloat16)] * 2
+        + [pltpu.VMEM(tuple(rest), jnp.float32), pltpu.VMEM(mine.shape, jnp.bfloat16)]
+        + [pltpu.SemaphoreType.DMA((2 * half,)), pltpu.SemaphoreType.DMA((half,))],
+        compiler_params=pltpu.CompilerParams(vmem_limit_bytes=40 << 20),
+        cost_estimate=pl.CostEstimate(flops=0, bytes_accessed=8 * mine.size, transcendentals=0),
+    )(in_hbm(mine), in_hbm(swapped))
 
 
 def combine_q(tr, tc, wire_ref, meta_ref, x_ref, dout_ref, ds_ref, keep_ref, up_ref, left_ref, corner_ref):
@@ -337,15 +399,12 @@
     out_ref[...] = (dot(inside, ds_ref[...]) + dot(halo, edge)).astype(jnp.bfloat16)
 
 
-def combine_y(
-    wire_ref, meta_ref, x_ref, dout_ref, grad_hbm, out_ref, dg_ref, first_hbm, second_hbm,
-    grad_s, wide_s, sems,
-):
+def combine_y(wire_ref, meta_ref, x_ref, dout_ref, kept_hbm, *refs):
+    *others, out_ref, dg_ref, first_hbm, second_hbm, kept_s, wide_s, sems = refs
     wides = (first_hbm, second_hbm)
-    fetch = [pltpu.make_async_copy(grad_hbm.at[:, k], grad_s.at[:, k], sems.at[k]) for k in range(2)]
-    store = [pltpu.make_async_copy(wide_s.at[:, k], wides[k], sems.at[2 + k]) for k in range(2)]
-    for copy in fetch:
-        copy.start()
+    fetch = pltpu.make_async_copy(kept_hbm, kept_s, sems.at[0])
+    store = [pltpu.make_async_copy(wide_s.at[k : k + 1], wides[k], sems.at[1 + k]) for k in range(2)]
+    fetch.start()
     wire = wire_ref[:, WIDE:]
     dout = dout_ref[...].astype(jnp.float32)
     tokens = dout.shape[0]
@@ -354,9 +413,12 @@
         for k in range(2)
     ]
     ys = [jnp.concatenate(from_wire(m, wire), axis=1) for m in masks]
+    fetch.wait()
     for k in range(2):
-        fetch[k].wait()
-        wide_s[:, k] = grad_s[:, k].astype(jnp.float32)
+        grad = kept_s[k]
+        for other in others:
+            grad = grad + other[k].astype(jnp.float32)
+        wide_s[k] = grad
         store[k].start()
     total = x_ref[...]
     lane = iota((tokens, tokens), 1)
@@ -370,6 +432,15 @@
         copy.wait()
 
 
+def other_core(v):
+    return lax.ppermute(v, "dp", [(i, i ^ 1) for i in range(lax.axis_size("dp"))])
+
+
+def along_x(v, d):
+    n = lax.axis_size("dp")
+    return lax.ppermute(v, "dp", [(i, (i + 2 * d) % n) for i in range(n)])
+
+
 def exchange(wire, n):
     blocks = wire.reshape(n, WIRE_ROWS, wire.shape[-1])
     out = lax.all_to_all(blocks, "expert", split_axis=0, concat_axis=0, tiled=True)
@@ -404,23 +475,18 @@
     dout = d_out.reshape(tokens, width)
     part = w_out.shape[1]
 
-    up, left, corner, w_own = pl.pallas_call(
+    up, left, corner = pl.pallas_call(
         prepare,
-        out_shape=(
-            bf16((4 * tc, width)),
-            bf16((4 * tr, width)),
-            bf16((16, width)),
-            bf16((1, 2, part, width)),
-        ),
-        in_specs=[ANY] * 3,
-        out_specs=(VMEM,) * 4,
-        scratch_shapes=[pltpu.VMEM((tr, tc, width), jnp.bfloat16), pltpu.SemaphoreType.DMA((3,))],
+        out_shape=(bf16((4 * tc, width)), bf16((4 * tr, width)), bf16((16, width))),
+        in_specs=[ANY],
+        out_specs=(VMEM,) * 3,
+        scratch_shapes=[pltpu.VMEM((tr, tc, width), jnp.bfloat16), pltpu.SemaphoreType.DMA],
         compiler_params=pltpu.CompilerParams(vmem_limit_bytes=32 * 1024 * 1024),
-        cost_estimate=pl.CostEstimate(flops=1 << 25, bytes_accessed=1 << 21, transcendentals=0),
-    )(in_hbm(attn_win), in_hbm(w_in.transpose(0, 2, 1)), in_hbm(w_out))
-    w_all = lax.all_gather(w_own, "dp", axis=0, tiled=True)
+        cost_estimate=pl.CostEstimate(flops=1 << 25, bytes_accessed=1 << 20, transcendentals=0),
+    )(in_hbm(attn_win))
+    up, left, corner, ids = lax.optimization_barrier((up, left, corner, ids))
     up, left, corner = edges(up, left, corner, 1)
-    g_wire, masks, meta, x0, sel = pl.pallas_call(
+    g_wire, masks, meta, x0, sel, w_own = pl.pallas_call(
         dispatch_g,
         out_shape=(
             bf16((n, WIDE)),
@@ -428,30 +494,46 @@
             f32((tokens, tokens)),
             f32((tokens, width)),
             bf16((tokens, 4 * tc + 4 * tr + 16)),
+            bf16((2, part, width)),
         ),
-        in_specs=[ANY] * 6,
-        out_specs=(VMEM,) * 5,
+        in_specs=[ANY] * 8,
+        out_specs=(VMEM,) * 6,
         scratch_shapes=[
             pltpu.SMEM((2,), jnp.int32),
             pltpu.VMEM((2, tokens), jnp.int32),
             pltpu.VMEM((2, tokens), jnp.float32),
         ]
         + [pltpu.VMEM((tr, tc, width), jnp.bfloat16)] * 3
-        + [pltpu.SemaphoreType.DMA((6,))],
+        + [pltpu.SemaphoreType.DMA((8,))],
         compiler_params=pltpu.CompilerParams(vmem_limit_bytes=32 * 1024 * 1024),
         cost_estimate=pl.CostEstimate(
             flops=4 * 256 * n * WIDE, bytes_accessed=1 << 20, transcendentals=0
         ),
-    )(*(in_hbm(v) for v in (shift_offsets, ids, gates, d_out, attn_win, shortcut)))
+    )(
+        *(
+            in_hbm(v)
+            for v in (
+                shift_offsets, ids, gates, d_out, attn_win, shortcut,
+                w_in.transpose(0, 2, 1), w_out,
+            )
+        )
+    )
+    n_x = lax.axis_size("dp") // 2
+    near = [d for d in range(1, n_x) if d in (1, n_x - 1)]
+    shards = dict(zip(near, relay([along_x(w_own, d) for d in near])))
+    mine = [w_own] + [shards[d] if d in near else along_x(w_own, d) for d in range(1, n_x)]
+    theirs = [other_core(v) for v in mine]
     sent, x = call(
         dispatch_u,
         (bf16((n, 2 * WIDE)), f32((tokens, width))),
         g_wire, masks, x0, sel, up, left, corner,
         flops=4 * 128 * n * WIDE, traffic=1 << 21,
     )
-    returned, grads = experts(exchange(sent, n_ex), w_all)
+    returned, g_mine, g_theirs = experts(exchange(sent, n_ex), mine, theirs)
+    swapped = other_core(g_theirs)
     returned = exchange(returned, n_ex)
-    grad = lax.psum_scatter(grads, "dp", scatter_dimension=0, tiled=True)
+    kept, *pieces = pair_sum(g_mine, swapped)
+    arrived = [along_x(v, -d) for d, v in enumerate(pieces, 1)]
     ds, ds_keep, up_b, left_b, corner_b = call(
         functools.partial(combine_q, tr, tc),
         (
@@ -469,18 +551,18 @@
         combine_y,
         out_shape=(bf16((tokens, width)), f32((2, tokens)))
         + (pltpu.HBM((1, part, width), jnp.float32),) * 2,
-        in_specs=[VMEM] * 4 + [ANY],
+        in_specs=[VMEM] * 4 + [ANY] + [VMEM] * (n_x - 1),
         out_specs=(VMEM, VMEM, ANY, ANY),
         scratch_shapes=[
-            pltpu.VMEM(grad.shape, jnp.bfloat16),
-            pltpu.VMEM(grad.shape, jnp.float32),
-            pltpu.SemaphoreType.DMA((4,)),
+            pltpu.VMEM(kept.shape, jnp.float32),
+            pltpu.VMEM(kept.shape, jnp.float32),
+            pltpu.SemaphoreType.DMA((3,)),
         ],
         compiler_params=pltpu.CompilerParams(vmem_limit_bytes=32 * 1024 * 1024),
         cost_estimate=pl.CostEstimate(
             flops=8 * tokens * n * WIDE, bytes_accessed=1 << 21, transcendentals=0
         ),
-    )(returned, meta, x, dout, in_hbm(grad))
+    )(returned, meta, x, dout, in_hbm(kept), *arrived)
     ds_keep, block_out = lax.optimization_barrier((ds_keep, block_out))
     d_attn = call(
         functools.partial(roll_back, tr, tc),

time: 133 us -> 144 us (1.083)
  blocking collectives: 70 us -> 0 us
  starting transfers between devices: 20.4 us -> 74.3 us
  waiting for transfers between devices: 8.02 us -> 40.6 us
  between operations: 14.1 us -> 0.95 us
  Pallas kernels: 20.3 us -> 26.3 us
    all_to_all x2 -> x0, blocking collectives: 70 us -> none  [exchange(): lax.all_to_all(blocks, 'expert', split_axis=0, concat_axis=0, tiled=True)]
    ppermute x0 -> x11, starting transfers between devices: none -> 30.5 us  [the longest x6 16.3 us: along_x(): return lax.ppermute(v, 'dp', [(i, (i + 2 * d) % n) for i in range(n)])]
    all_to_all x0 -> x2, starting transfers between devices: none -> 25.1 us  [exchange(): lax.all_to_all(blocks, 'expert', split_axis=0, concat_axis=0, tiled=True)]
    all_to_all x0 -> x2, waiting for transfers between devices: none -> 16.5 us  [exchange(): lax.all_to_all(blocks, 'expert', split_axis=0, concat_axis=0, tiled=True)]
    ppermute x0 -> x11, waiting for transfers between devices: none -> 14.9 us  [the longest x6 13.4 us: along_x(): return lax.ppermute(v, 'dp', [(i, (i + 2 * d) % n) for i in range(n)])]
    pallas_call x0 -> x2, Pallas kernels: none -> 4.85 us  [the longest x1 3.8 us: pair_sum(): pl.pallas_call(pair_sum_body, out_shape=(pltpu.HBM(tuple(rest), jnp.float...]
  transfers between devices with their start and end apart: 8 -> 19, of which waited for: 2 -> 5; matrix products, arithmetic and copies ran while one was open for 0% -> 0% of each run, Pallas kernels for 6% -> 8%
where the time goes in v6:
time: 144 us; the launch traced here: 143 us
  starting transfers between devices  74.3 us (52%)
  waiting for transfers between devices  40.6 us (28%)
  Pallas kernels  26.3 us (18%)
    all_to_all x2, starting transfers between devices, exchange(): lax.all_to_all(blocks, 'expert', split_axis=0, concat_axis=0, tiled=True)  25.1 us
    all_to_all x2, waiting for transfers between devices, exchange(): lax.all_to_all(blocks, 'expert', split_axis=0, concat_axis=0, tiled=True)  16.5 us
    ppermute x6, starting transfers between devices, along_x(): return lax.ppermute(v, 'dp', [(i, (i + 2 * d) % n) for i in range(n)])  16.3 us
    ppermute x5, starting transfers between devices, other_core(): lax.ppermute(v, 'dp', [(i, i ^ 1) for i in range(lax.axis_size('dp'))])  14.2 us
    ppermute x6, waiting for transfers between devices, along_x(): return lax.ppermute(v, 'dp', [(i, (i + 2 * d) % n) for i in range(n)])  13.4 us
    pallas_call x1, Pallas kernels, experts(): pl.pallas_call(experts_body, out_shape=(jax.ShapeDtypeStruct((n, 2 * WIDE...  9.88 us
    ppermute x2, waiting for transfers between devices, edges(): lax.ppermute(corner, ('expert', 'dp'), by_both)  9.18 us
    ppermute x2, starting transfers between devices, edges(): lax.ppermute(row_edge, 'dp', by_dp)  8.21 us
  transfers between devices with their start and end apart: 19, of which 5 were waited for; matrix products, arithmetic and copies ran while one was open for 0% of the time, Pallas kernels for 8%

profile of v6, /device:TPU:1, one launch (start us, length us, event | category | flops | bytes accessed | tf_op | source)
XLA Modules:
  0.0 143.0 jit_solution(2837660062034679437)
XLA Ops:
  0.6 1.1 shard_map.127
  1.7 2.5 %shard_map.128 = (bf16[512,512]{1,0:T(8,128)(2,1)S(1)}, bf16[3,512,128]{2,1,0:T(8,128)(2,1)S(1)}, f32[128,128]{1,0:T(8,128)S(1)}, f32[128,768]{1,0:T(8,128)S(1)}...) custom-call(s32[2]{0:T(128)} %off_ref.1, s32[2,128]{1,0:T(2,128)} %bitcast.26, f32[2,128]{1,0:T(2,128)} %bitcast.27, ...), custom_call_target="tpu_custom_call" | custom-call | flops 268435456 | bytes 1048576 | tf_op jit(solution)/shard_map/pallas_call | solution.py:489
  4.2 0.0 copy-start.2
  4.3 5.2 %collective-permute-start.4 = (bf16[2,192,768]{2,1,0:T(8,128)(2,1)S(1)}, bf16[2,192,768]{2,1,0:T(8,128)(2,1)S(1)}, u32[]{:S(2)}, u32[]{:S(2)}) collective-permute-start(bf16[2,192,768]{2,1,0:T(8,128)(2,1)S(1)} %get-tuple-element.53.refs_0_), channel_id=1, source_target_pairs={{0,6},{1,7},{2,0},{3,1},{4,2},{5,3},{6,4},{7,5},{8,14},{9,15},{10,... | collective-permute-start | bytes 1769480 | tf_op jit(solution)/shard_map/ppermute | solution.py:441
  9.5 1.9 %collective-permute-start.3 = (bf16[2,192,768]{2,1,0:T(8,128)(2,1)S(1)}, bf16[2,192,768]{2,1,0:T(8,128)(2,1)S(1)}, u32[]{:S(2)}, u32[]{:S(2)}) collective-permute-start(bf16[2,192,768]{2,1,0:T(8,128)(2,1)S(1)} %get-tuple-element.53.refs_0_), channel_id=1, source_target_pairs={{0,2},{1,3},{2,4},{3,5},{4,6},{5,7},{6,0},{7,1},{8,10},{9,11},{10,... | collective-permute-start | bytes 1769480 | tf_op jit(solution)/shard_map/ppermute | solution.py:441
  11.4 5.2 %collective-permute-start = (bf16[64,768]{1,0:T(8,128)(2,1)S(1)}, bf16[64,768]{1,0:T(8,128)(2,1)S(1)}, u32[]{:S(2)}, u32[]{:S(2)}) collective-permute-start(bf16[64,768]{1,0:T(8,128)(2,1)S(1)} %get-tuple-element.49), channel_id=1, source_target_pairs={{0,1},{1,2},{2,3},{3,4},{4,5},{5,6},{6,7},{7,0},{8,9},{9,10},{10,1... | collective-permute-start | bytes 294920 | tf_op jit(solution)/shard_map/ppermute | solution.py:460
  16.6 1.9 %collective-permute-start.1 = (bf16[32,768]{1,0:T(8,128)(2,1)S(1)}, bf16[32,768]{1,0:T(8,128)(2,1)S(1)}, u32[]{:S(2)}, u32[]{:S(2)}) collective-permute-start(bf16[32,768]{1,0:T(8,128)(2,1)S(1)} %get-tuple-element.50), channel_id=1, source_target_pairs={{0,8},{8,16},{16,24},{24,32},{32,40},{40,48},{48,56},{56,64},{64,7... | collective-permute-start | bytes 147464 | tf_op jit(solution)/shard_map/ppermute | solution.py:461
  18.5 1.9 %collective-permute-start.2 = (bf16[16,768]{1,0:T(8,128)(2,1)S(1)}, bf16[16,768]{1,0:T(8,128)(2,1)S(1)}, u32[]{:S(2)}, u32[]{:S(2)}) collective-permute-start(bf16[16,768]{1,0:T(8,128)(2,1)S(1)} %get-tuple-element.51), channel_id=1, source_target_pairs={{0,9},{1,10},{2,11},{3,12},{4,13},{5,14},{6,15},{7,8},{8,17},{9,18... | collective-permute-start | bytes 73736 | tf_op jit(solution)/shard_map/ppermute | solution.py:462
  20.5 8.9 %collective-permute-done.2.corner_ref = bf16[16,768]{1,0:T(8,128)(2,1)S(1)} collective-permute-done((bf16[16,768]{1,0:T(8,128)(2,1)S(1)}, bf16[16,768]{1,0:T(8,128)(2,1)S(1)}, u32[]{:S(2)}, u32[]{:S(2)}) %collective-permute-start.2) | collective-permute-done | bytes 24608 | tf_op jit(solution)/shard_map/ppermute | solution.py:462
  29.4 0.0 collective-permute-done.1.left_ref
  29.4 0.0 collective-permute-done.up_ref
  29.4 1.8 %shard_map.129 = (bf16[512,1024]{1,0:T(8,128)(2,1)}, f32[128,768]{1,0:T(8,128)S(1)}) custom-call(bf16[512,512]{1,0:T(8,128)(2,1)S(1)} %get-tuple-element.45.g_ref, bf16[3,512,128]{2,1,0:T(8,128)(2,1)S(1)} %get-tuple-element.46.mask_ref, f32[128,768]{1,0:T(8,128)S(1)} %get-tuple-element.47.x0_ref, bf16[128,112]{1,0:T(8,128)(2,1)S(1)} %get-tuple-element.48.sel_ref, ...), custom_call_target="tpu_custom_call" | custom-call | flops 134217728 | bytes 2097152 | tf_op jit(solution)/shard_map/pallas_call | solution.py:44
  31.2 12.7 %all-to-all-start = ((bf16[64,8,1024]{2,1,0:T(8,128)(2,1)}), bf16[64,8,1024]{2,1,0:T(8,128)(2,1)S(1)}, u32[]{:S(2)}, u32[]{:S(2)}) async-start(bf16[64,8,1024]{2,1,0:T(8,128)(2,1)} %bitcast.5), calls=%async_computation | async-start | bytes 2097152 | tf_op jit(solution)/shard_map/all_to_all | solution.py:446
  43.8 5.7 %collective-permute-start.6 = (bf16[2,192,768]{2,1,0:T(8,128)(2,1)S(1)}, bf16[2,192,768]{2,1,0:T(8,128)(2,1)S(1)}, u32[]{:S(2)}, u32[]{:S(2)}) collective-permute-start(bf16[2,192,768]{2,1,0:T(8,128)(2,1)S(1)} %get-tuple-element.53.refs_0_), channel_id=1, source_target_pairs={{0,1},{1,0},{2,3},{3,2},{4,5},{5,4},{6,7},{7,6},{8,9},{9,8},{10,11... | collective-permute-start | bytes 1769480 | tf_op jit(solution)/shard_map/ppermute | solution.py:436
  49.5 1.9 %collective-permute-start.5 = (bf16[2,192,768]{2,1,0:T(8,128)(2,1)S(1)}, bf16[2,192,768]{2,1,0:T(8,128)(2,1)S(1)}, u32[]{:S(2)}, u32[]{:S(2)}) collective-permute-start(bf16[2,192,768]{2,1,0:T(8,128)(2,1)S(1)} %get-tuple-element.53.refs_0_), channel_id=1, source_target_pairs={{0,4},{1,5},{2,6},{3,7},{4,0},{5,1},{6,2},{7,3},{8,12},{9,13},{10,... | collective-permute-start | bytes 1769480 | tf_op jit(solution)/shard_map/ppermute | solution.py:441
  51.4 0.0 collective-permute-done.4.refs_1_
  51.4 0.0 collective-permute-done.3.refs_0_
  51.4 1.0 shard_map.130
  52.5 0.0 copy-done.2
  52.5 1.9 %collective-permute-start.7 = (bf16[2,192,768]{2,1,0:T(8,128)(2,1)}, bf16[2,192,768]{2,1,0:T(8,128)(2,1)S(1)}, u32[]{:S(2)}, u32[]{:S(2)}) collective-permute-start(bf16[2,192,768]{2,1,0:T(8,128)(2,1)} %get-tuple-element.54.refs_1_), channel_id=1, source_target_pairs={{0,1},{1,0},{2,3},{3,2},{4,5},{5,4},{6,7},{7,6},{8,9},{9,8},{10,11... | collective-permute-start | bytes 1769480 | tf_op jit(solution)/shard_map/ppermute | solution.py:436
  54.4 13.4 %collective-permute-done.5.refs_2_ = bf16[2,192,768]{2,1,0:T(8,128)(2,1)S(1)} collective-permute-done((bf16[2,192,768]{2,1,0:T(8,128)(2,1)S(1)}, bf16[2,192,768]{2,1,0:T(8,128)(2,1)S(1)}, u32[]{:S(2)}, u32[]{:S(2)}) %collective-permute-start.5) | collective-permute-done | bytes 589856 | tf_op jit(solution)/shard_map/ppermute | solution.py:441
  67.8 0.0 copy-start.4
  67.8 2.7 %collective-permute-start.8 = (bf16[2,192,768]{2,1,0:T(8,128)(2,1)S(1)}, bf16[2,192,768]{2,1,0:T(8,128)(2,1)S(1)}, u32[]{:S(2)}, u32[]{:S(2)}) collective-permute-start(bf16[2,192,768]{2,1,0:T(8,128)(2,1)S(1)} %collective-permute-done.5.refs_2_), channel_id=1, source_target_pairs={{0,1},{1,0},{2,3},{3,2},{4,5},{5,4},{6,7},{7,6},{8,9},{9,8},{10,11... | collective-permute-start | bytes 1769480 | tf_op jit(solution)/shard_map/ppermute | solution.py:436
  70.5 1.9 %collective-permute-start.9 = (bf16[2,192,768]{2,1,0:T(8,128)(2,1)}, bf16[2,192,768]{2,1,0:T(8,128)(2,1)}, u32[]{:S(2)}, u32[]{:S(2)}) collective-permute-start(bf16[2,192,768]{2,1,0:T(8,128)(2,1)} %get-tuple-element.55.refs_3_), channel_id=1, source_target_pairs={{0,1},{1,0},{2,3},{3,2},{4,5},{5,4},{6,7},{7,6},{8,9},{9,8},{10,11... | collective-permute-start | bytes 1769480 | tf_op jit(solution)/shard_map/ppermute | solution.py:436
  72.5 0.0 collective-permute-done.6.refs_4_
  72.5 0.0 copy-start.3
  72.5 0.0 collective-permute-done.8.refs_6_
  72.5 0.0 copy-start.6
  72.5 0.0 collective-permute-done.7.refs_5_
  72.5 0.0 copy-done.4
  72.5 0.8 copy-done.3
  73.3 0.0 copy-start.5
  73.3 1.5 %collective-permute-done.9.refs_7_ = bf16[2,192,768]{2,1,0:T(8,128)(2,1)} collective-permute-done((bf16[2,192,768]{2,1,0:T(8,128)(2,1)}, bf16[2,192,768]{2,1,0:T(8,128)(2,1)}, u32[]{:S(2)}, u32[]{:S(2)}) %collective-permute-start.9) | collective-permute-done | bytes 589856 | tf_op jit(solution)/shard_map/ppermute | solution.py:436
  74.8 0.0 all-to-all-done
  74.8 0.0 copy-done.6
  74.8 0.0 copy-done.5
  74.8 9.9 %shard_map.131 = (bf16[512,1024]{1,0:T(8,128)(2,1)}, bf16[4,2,192,768]{3,2,1,0:T(8,128)(2,1)}, bf16[4,2,192,768]{3,2,1,0:T(8,128)(2,1)}) custom-call(bf16[512,1024]{1,0:T(8,128)(2,1)S(1)} %bitcast.23, bf16[2,192,768]{2,1,0:T(8,128)(2,1)} %copy-done.2, bf16[2,192,768]{2,1,0:T(8,128)(2,1)} %get-tuple-element.54.refs_1_, bf16[2,192,768]{2,1,0:T(8,128)(2,1)} %copy-done.4, ...), custom_call_target="tpu_custom_call" | custom-call | flops 4529848320 | bytes 9437184 | tf_op jit(solution)/shard_map/pallas_call | solution.py:278
  84.7 2.0 %collective-permute-start.10 = (bf16[4,2,192,768]{3,2,1,0:T(8,128)(2,1)}, bf16[4,2,192,768]{3,2,1,0:T(8,128)(2,1)}, u32[]{:S(2)}, u32[]{:S(2)}) collective-permute-start(bf16[4,2,192,768]{3,2,1,0:T(8,128)(2,1)} %get-tuple-element.61), channel_id=1, source_target_pairs={{0,1},{1,0},{2,3},{3,2},{4,5},{5,4},{6,7},{7,6},{8,9},{9,8},{10,11... | collective-permute-start | bytes 7077896 | tf_op jit(solution)/shard_map/ppermute | solution.py:436
  86.7 12.4 %all-to-all-start.1 = ((bf16[64,8,1024]{2,1,0:T(8,128)(2,1)}), bf16[64,8,1024]{2,1,0:T(8,128)(2,1)S(1)}, u32[]{:S(2)}, u32[]{:S(2)}) async-start(bf16[64,8,1024]{2,1,0:T(8,128)(2,1)} %bitcast.7), calls=%async_computation.1 | async-start | bytes 2097152 | tf_op jit(solution)/shard_map/all_to_all | solution.py:446
  99.2 0.0 collective-permute-done.10.swapped_hbm
  99.2 0.0 copy-start
  99.2 3.8 %shard_map.133 = (f32[2,192,768]{2,1,0:T(8,128)}, bf16[2,192,768]{2,1,0:T(8,128)(2,1)}, bf16[2,192,768]{2,1,0:T(8,128)(2,1)}, bf16[2,192,768]{2,1,0:T(8,128)(2,1)}) custom-call(bf16[4,2,192,768]{3,2,1,0:T(8,128)(2,1)} %get-tuple-element.60.mine_hbm, bf16[4,2,192,768]{3,2,1,0:T(8,128)(2,1)} %collective-permute-done.10.swapped_hbm), custom_call_target="tpu_custom_call" | custom-call | bytes 9437184 | tf_op jit(solution)/shard_map/pallas_call | solution.py:355
  103.0 1.9 %collective-permute-start.11 = (bf16[2,192,768]{2,1,0:T(8,128)(2,1)}, bf16[2,192,768]{2,1,0:T(8,128)(2,1)S(1)}, u32[]{:S(2)}, u32[]{:S(2)}) collective-permute-start(bf16[2,192,768]{2,1,0:T(8,128)(2,1)} %get-tuple-element.63), channel_id=1, source_target_pairs={{0,6},{1,7},{2,0},{3,1},{4,2},{5,3},{6,4},{7,5},{8,14},{9,15},{10,... | collective-permute-start | bytes 1769480 | tf_op jit(solution)/shard_map/ppermute | solution.py:441
  104.9 2.8 %collective-permute-start.12 = (bf16[2,192,768]{2,1,0:T(8,128)(2,1)}, bf16[2,192,768]{2,1,0:T(8,128)(2,1)S(1)}, u32[]{:S(2)}, u32[]{:S(2)}) collective-permute-start(bf16[2,192,768]{2,1,0:T(8,128)(2,1)} %get-tuple-element.64), channel_id=1, source_target_pairs={{0,4},{1,5},{2,6},{3,7},{4,0},{5,1},{6,2},{7,3},{8,12},{9,13},{10,... | collective-permute-start | bytes 1769480 | tf_op jit(solution)/shard_map/ppermute | solution.py:441
  107.7 2.5 %collective-permute-start.13 = (bf16[2,192,768]{2,1,0:T(8,128)(2,1)}, bf16[2,192,768]{2,1,0:T(8,128)(2,1)S(1)}, u32[]{:S(2)}, u32[]{:S(2)}) collective-permute-start(bf16[2,192,768]{2,1,0:T(8,128)(2,1)} %get-tuple-element.65), channel_id=1, source_target_pairs={{0,2},{1,3},{2,4},{3,5},{4,6},{5,7},{6,0},{7,1},{8,10},{9,11},{10,... | collective-permute-start | bytes 1769480 | tf_op jit(solution)/shard_map/ppermute | solution.py:441
  110.2 16.5 %all-to-all-done.1 = bf16[64,8,1024]{2,1,0:T(8,128)(2,1)S(1)} async-done(((bf16[64,8,1024]{2,1,0:T(8,128)(2,1)}), bf16[64,8,1024]{2,1,0:T(8,128)(2,1)S(1)}, u32[]{:S(2)}, u32[]{:S(2)}) %all-to-all-start.1) | async-done | bytes 1048608 | tf_op jit(solution)/shard_map/all_to_all | solution.py:446
  126.7 0.0 copy-done
  126.7 1.3 shard_map.132
  128.0 0.0 copy-start.1
  128.0 3.0 %collective-permute-start.14 = (bf16[64,768]{1,0:T(8,128)(2,1)S(1)}, bf16[64,768]{1,0:T(8,128)(2,1)S(1)}, u32[]{:S(2)}, u32[]{:S(2)}) collective-permute-start(bf16[64,768]{1,0:T(8,128)(2,1)S(1)} %get-tuple-element.70), channel_id=1, source_target_pairs={{0,7},{1,0},{2,1},{3,2},{4,3},{5,4},{6,5},{7,6},{8,15},{9,8},{10,9... | collective-permute-start | bytes 294920 | tf_op jit(solution)/shard_map/ppermute | solution.py:460
  131.0 4.4 %collective-permute-start.15 = (bf16[32,768]{1,0:T(8,128)(2,1)S(1)}, bf16[32,768]{1,0:T(8,128)(2,1)S(1)}, u32[]{:S(2)}, u32[]{:S(2)}) collective-permute-start(bf16[32,768]{1,0:T(8,128)(2,1)S(1)} %get-tuple-element.71), channel_id=1, source_target_pairs={{0,504},{8,0},{16,8},{24,16},{32,24},{40,32},{48,40},{56,48},{64,5... | collective-permute-start | bytes 147464 | tf_op jit(solution)/shard_map/ppermute | solution.py:461
  135.4 0.0 collective-permute-done.11.refs_0_
  135.4 2.3 %collective-permute-start.16 = (bf16[16,768]{1,0:T(8,128)(2,1)S(1)}, bf16[16,768]{1,0:T(8,128)(2,1)S(1)}, u32[]{:S(2)}, u32[]{:S(2)}) collective-permute-start(bf16[16,768]{1,0:T(8,128)(2,1)S(1)} %get-tuple-element.72), channel_id=1, source_target_pairs={{0,511},{1,504},{2,505},{3,506},{4,507},{5,508},{6,509},{7,510},{8... | collective-permute-start | bytes 73736 | tf_op jit(solution)/shard_map/ppermute | solution.py:462
  137.7 0.0 collective-permute-done.12.refs_1_
  137.7 0.0 collective-permute-done.13.refs_2_
  137.7 3.5 %shard_map.134 = (bf16[128,768]{1,0:T(8,128)(2,1)}, f32[2,128]{1,0:T(2,128)}, f32[1,192,768]{2,1,0:T(8,128)}, f32[1,192,768]{2,1,0:T(8,128)}) custom-call(bf16[512,1024]{1,0:T(8,128)(2,1)S(1)} %bitcast.20, f32[128,128]{1,0:T(8,128)S(1)} %get-tuple-element.57.meta_ref, f32[128,768]{1,0:T(8,128)S(1)} %get-tuple-element.58.x_ref, ...), custom_call_target="tpu_custom_call" | custom-call | flops 268435456 | bytes 2097152 | tf_op jit(solution)/shard_map/pallas_call | solution.py:550
  141.2 0.3 collective-permute-done.16.corner_ref
  141.5 0.0 collective-permute-done.15.right_ref
  141.5 0.0 collective-permute-done.14.down_ref
  141.5 0.0 copy-done.1
  141.5 1.5 %shard_map.135 = bf16[128,768]{1,0:T(8,128)(2,1)} custom-call(s32[2]{0:T(128)S(1)} %copy-done.1, bf16[128,768]{1,0:T(8,128)(2,1)S(1)} %get-tuple-element.69.ds_ref, bf16[64,768]{1,0:T(8,128)(2,1)S(1)} %collective-permute-done.14.down_ref, bf16[32,768]{1,0:T(8,128)(2,1)S(1)} %collective-permute-done.15.right_ref, ...), custom_call_target="tpu_custom_call" | custom-call | flops 50331648 | bytes 524288 | tf_op jit(solution)/shard_map/pallas_call | solution.py:44
Async XLA Ops:
  4.2 48.3 %copy-start.2 = (bf16[2,192,768]{2,1,0:T(8,128)(2,1)}, bf16[2,192,768]{2,1,0:T(8,128)(2,1)S(1)}, u32[]{:S(2)}) copy-start(bf16[2,192,768]{2,1,0:T(8,128)(2,1)S(1)} %get-tuple-element.53.refs_0_) | copy-start | bytes 1769476
  4.3 47.2 %collective-permute-start.4 = (bf16[2,192,768]{2,1,0:T(8,128)(2,1)S(1)}, bf16[2,192,768]{2,1,0:T(8,128)(2,1)S(1)}, u32[]{:S(2)}, u32[]{:S(2)}) collective-permute-start(bf16[2,192,768]{2,1,0:T(8,128)(2,1)S(1)} %get-tuple-element.53.refs_0_), channel_id=1, source_target_pairs={{0,6},{1,7},{2,0},{3,1},{4,2},{5,3},{6,4},{7,5},{8,14},{9,15},{10,... | collective-permute-start | bytes 1769480 | tf_op jit(solution)/shard_map/ppermute | solution.py:441
  9.5 42.0 %collective-permute-start.3 = (bf16[2,192,768]{2,1,0:T(8,128)(2,1)S(1)}, bf16[2,192,768]{2,1,0:T(8,128)(2,1)S(1)}, u32[]{:S(2)}, u32[]{:S(2)}) collective-permute-start(bf16[2,192,768]{2,1,0:T(8,128)(2,1)S(1)} %get-tuple-element.53.refs_0_), channel_id=1, source_target_pairs={{0,2},{1,3},{2,4},{3,5},{4,6},{5,7},{6,0},{7,1},{8,10},{9,11},{10,... | collective-permute-start | bytes 1769480 | tf_op jit(solution)/shard_map/ppermute | solution.py:441
  11.4 18.0 %collective-permute-start = (bf16[64,768]{1,0:T(8,128)(2,1)S(1)}, bf16[64,768]{1,0:T(8,128)(2,1)S(1)}, u32[]{:S(2)}, u32[]{:S(2)}) collective-permute-start(bf16[64,768]{1,0:T(8,128)(2,1)S(1)} %get-tuple-element.49), channel_id=1, source_target_pairs={{0,1},{1,2},{2,3},{3,4},{4,5},{5,6},{6,7},{7,0},{8,9},{9,10},{10,1... | collective-permute-start | bytes 294920 | tf_op jit(solution)/shard_map/ppermute | solution.py:460
  16.6 12.8 %collective-permute-start.1 = (bf16[32,768]{1,0:T(8,128)(2,1)S(1)}, bf16[32,768]{1,0:T(8,128)(2,1)S(1)}, u32[]{:S(2)}, u32[]{:S(2)}) collective-permute-start(bf16[32,768]{1,0:T(8,128)(2,1)S(1)} %get-tuple-element.50), channel_id=1, source_target_pairs={{0,8},{8,16},{16,24},{24,32},{32,40},{40,48},{48,56},{56,64},{64,7... | collective-permute-start | bytes 147464 | tf_op jit(solution)/shard_map/ppermute | solution.py:461
  18.5 10.9 %collective-permute-start.2 = (bf16[16,768]{1,0:T(8,128)(2,1)S(1)}, bf16[16,768]{1,0:T(8,128)(2,1)S(1)}, u32[]{:S(2)}, u32[]{:S(2)}) collective-permute-start(bf16[16,768]{1,0:T(8,128)(2,1)S(1)} %get-tuple-element.51), channel_id=1, source_target_pairs={{0,9},{1,10},{2,11},{3,12},{4,13},{5,14},{6,15},{7,8},{8,17},{9,18... | collective-permute-start | bytes 73736 | tf_op jit(solution)/shard_map/ppermute | solution.py:462
  31.2 43.6 %all-to-all-start = ((bf16[64,8,1024]{2,1,0:T(8,128)(2,1)}), bf16[64,8,1024]{2,1,0:T(8,128)(2,1)S(1)}, u32[]{:S(2)}, u32[]{:S(2)}) async-start(bf16[64,8,1024]{2,1,0:T(8,128)(2,1)} %bitcast.5), calls=%async_computation | async-start | bytes 2097152 | tf_op jit(solution)/shard_map/all_to_all | solution.py:446
  43.8 28.7 %collective-permute-start.6 = (bf16[2,192,768]{2,1,0:T(8,128)(2,1)S(1)}, bf16[2,192,768]{2,1,0:T(8,128)(2,1)S(1)}, u32[]{:S(2)}, u32[]{:S(2)}) collective-permute-start(bf16[2,192,768]{2,1,0:T(8,128)(2,1)S(1)} %get-tuple-element.53.refs_0_), channel_id=1, source_target_pairs={{0,1},{1,0},{2,3},{3,2},{4,5},{5,4},{6,7},{7,6},{8,9},{9,8},{10,11... | collective-permute-start | bytes 1769480 | tf_op jit(solution)/shard_map/ppermute | solution.py:436
  49.5 18.3 %collective-permute-start.5 = (bf16[2,192,768]{2,1,0:T(8,128)(2,1)S(1)}, bf16[2,192,768]{2,1,0:T(8,128)(2,1)S(1)}, u32[]{:S(2)}, u32[]{:S(2)}) collective-permute-start(bf16[2,192,768]{2,1,0:T(8,128)(2,1)S(1)} %get-tuple-element.53.refs_0_), channel_id=1, source_target_pairs={{0,4},{1,5},{2,6},{3,7},{4,0},{5,1},{6,2},{7,3},{8,12},{9,13},{10,... | collective-permute-start | bytes 1769480 | tf_op jit(solution)/shard_map/ppermute | solution.py:441
  52.5 20.0 %collective-permute-start.7 = (bf16[2,192,768]{2,1,0:T(8,128)(2,1)}, bf16[2,192,768]{2,1,0:T(8,128)(2,1)S(1)}, u32[]{:S(2)}, u32[]{:S(2)}) collective-permute-start(bf16[2,192,768]{2,1,0:T(8,128)(2,1)} %get-tuple-element.54.refs_1_), channel_id=1, source_target_pairs={{0,1},{1,0},{2,3},{3,2},{4,5},{5,4},{6,7},{7,6},{8,9},{9,8},{10,11... | collective-permute-start | bytes 1769480 | tf_op jit(solution)/shard_map/ppermute | solution.py:436
  67.8 4.7 %copy-start.4 = (bf16[2,192,768]{2,1,0:T(8,128)(2,1)}, bf16[2,192,768]{2,1,0:T(8,128)(2,1)S(1)}, u32[]{:S(2)}) copy-start(bf16[2,192,768]{2,1,0:T(8,128)(2,1)S(1)} %collective-permute-done.5.refs_2_) | copy-start | bytes 1769476
  67.8 4.7 %collective-permute-start.8 = (bf16[2,192,768]{2,1,0:T(8,128)(2,1)S(1)}, bf16[2,192,768]{2,1,0:T(8,128)(2,1)S(1)}, u32[]{:S(2)}, u32[]{:S(2)}) collective-permute-start(bf16[2,192,768]{2,1,0:T(8,128)(2,1)S(1)} %collective-permute-done.5.refs_2_), channel_id=1, source_target_pairs={{0,1},{1,0},{2,3},{3,2},{4,5},{5,4},{6,7},{7,6},{8,9},{9,8},{10,11... | collective-permute-start | bytes 1769480 | tf_op jit(solution)/shard_map/ppermute | solution.py:436
  70.5 4.2 %collective-permute-start.9 = (bf16[2,192,768]{2,1,0:T(8,128)(2,1)}, bf16[2,192,768]{2,1,0:T(8,128)(2,1)}, u32[]{:S(2)}, u32[]{:S(2)}) collective-permute-start(bf16[2,192,768]{2,1,0:T(8,128)(2,1)} %get-tuple-element.55.refs_3_), channel_id=1, source_target_pairs={{0,1},{1,0},{2,3},{3,2},{4,5},{5,4},{6,7},{7,6},{8,9},{9,8},{10,11... | collective-permute-start | bytes 1769480 | tf_op jit(solution)/shard_map/ppermute | solution.py:436
  72.5 0.8 copy-start.3
  72.5 2.3 %copy-start.6 = (bf16[2,192,768]{2,1,0:T(8,128)(2,1)}, bf16[2,192,768]{2,1,0:T(8,128)(2,1)S(1)}, u32[]{:S(2)}) copy-start(bf16[2,192,768]{2,1,0:T(8,128)(2,1)S(1)} %collective-permute-done.8.refs_6_) | copy-start | bytes 1769476
  73.3 1.5 %copy-start.5 = (bf16[2,192,768]{2,1,0:T(8,128)(2,1)}, bf16[2,192,768]{2,1,0:T(8,128)(2,1)S(1)}, u32[]{:S(2)}) copy-start(bf16[2,192,768]{2,1,0:T(8,128)(2,1)S(1)} %collective-permute-done.7.refs_5_) | copy-start | bytes 1769476
  84.7 14.5 %collective-permute-start.10 = (bf16[4,2,192,768]{3,2,1,0:T(8,128)(2,1)}, bf16[4,2,192,768]{3,2,1,0:T(8,128)(2,1)}, u32[]{:S(2)}, u32[]{:S(2)}) collective-permute-start(bf16[4,2,192,768]{3,2,1,0:T(8,128)(2,1)} %get-tuple-element.61), channel_id=1, source_target_pairs={{0,1},{1,0},{2,3},{3,2},{4,5},{5,4},{6,7},{7,6},{8,9},{9,8},{10,11... | collective-permute-start | bytes 7077896 | tf_op jit(solution)/shard_map/ppermute | solution.py:436
  86.7 40.0 %all-to-all-start.1 = ((bf16[64,8,1024]{2,1,0:T(8,128)(2,1)}), bf16[64,8,1024]{2,1,0:T(8,128)(2,1)S(1)}, u32[]{:S(2)}, u32[]{:S(2)}) async-start(bf16[64,8,1024]{2,1,0:T(8,128)(2,1)} %bitcast.7), calls=%async_computation.1 | async-start | bytes 2097152 | tf_op jit(solution)/shard_map/all_to_all | solution.py:446
  99.2 27.6 %copy-start = (bf16[8,16,768]{2,1,0:T(8,128)(2,1)S(1)}, bf16[8,16,768]{2,1,0:T(8,128)(2,1)}, u32[]{:S(2)}) copy-start(bf16[8,16,768]{2,1,0:T(8,128)(2,1)} %dout_hbm.1) | copy-start | bytes 589828
  103.0 32.4 %collective-permute-start.11 = (bf16[2,192,768]{2,1,0:T(8,128)(2,1)}, bf16[2,192,768]{2,1,0:T(8,128)(2,1)S(1)}, u32[]{:S(2)}, u32[]{:S(2)}) collective-permute-start(bf16[2,192,768]{2,1,0:T(8,128)(2,1)} %get-tuple-element.63), channel_id=1, source_target_pairs={{0,6},{1,7},{2,0},{3,1},{4,2},{5,3},{6,4},{7,5},{8,14},{9,15},{10,... | collective-permute-start | bytes 1769480 | tf_op jit(solution)/shard_map/ppermute | solution.py:441
  104.9 32.8 %collective-permute-start.12 = (bf16[2,192,768]{2,1,0:T(8,128)(2,1)}, bf16[2,192,768]{2,1,0:T(8,128)(2,1)S(1)}, u32[]{:S(2)}, u32[]{:S(2)}) collective-permute-start(bf16[2,192,768]{2,1,0:T(8,128)(2,1)} %get-tuple-element.64), channel_id=1, source_target_pairs={{0,4},{1,5},{2,6},{3,7},{4,0},{5,1},{6,2},{7,3},{8,12},{9,13},{10,... | collective-permute-start | bytes 1769480 | tf_op jit(solution)/shard_map/ppermute | solution.py:441
  107.7 30.0 %collective-permute-start.13 = (bf16[2,192,768]{2,1,0:T(8,128)(2,1)}, bf16[2,192,768]{2,1,0:T(8,128)(2,1)S(1)}, u32[]{:S(2)}, u32[]{:S(2)}) collective-permute-start(bf16[2,192,768]{2,1,0:T(8,128)(2,1)} %get-tuple-element.65), channel_id=1, source_target_pairs={{0,2},{1,3},{2,4},{3,5},{4,6},{5,7},{6,0},{7,1},{8,10},{9,11},{10,... | collective-permute-start | bytes 1769480 | tf_op jit(solution)/shard_map/ppermute | solution.py:441
  128.0 13.5 %copy-start.1 = (s32[2]{0:T(128)S(1)}, s32[2]{0:T(128)}, u32[]{:S(2)}) copy-start(s32[2]{0:T(128)} %off_ref.1) | copy-start | bytes 28
  128.0 13.5 %collective-permute-start.14 = (bf16[64,768]{1,0:T(8,128)(2,1)S(1)}, bf16[64,768]{1,0:T(8,128)(2,1)S(1)}, u32[]{:S(2)}, u32[]{:S(2)}) collective-permute-start(bf16[64,768]{1,0:T(8,128)(2,1)S(1)} %get-tuple-element.70), channel_id=1, source_target_pairs={{0,7},{1,0},{2,1},{3,2},{4,3},{5,4},{6,5},{7,6},{8,15},{9,8},{10,9... | collective-permute-start | bytes 294920 | tf_op jit(solution)/shard_map/ppermute | solution.py:460
  131.0 10.5 %collective-permute-start.15 = (bf16[32,768]{1,0:T(8,128)(2,1)S(1)}, bf16[32,768]{1,0:T(8,128)(2,1)S(1)}, u32[]{:S(2)}, u32[]{:S(2)}) collective-permute-start(bf16[32,768]{1,0:T(8,128)(2,1)S(1)} %get-tuple-element.71), channel_id=1, source_target_pairs={{0,504},{8,0},{16,8},{24,16},{32,24},{40,32},{48,40},{56,48},{64,5... | collective-permute-start | bytes 147464 | tf_op jit(solution)/shard_map/ppermute | solution.py:461
  135.4 6.0 %collective-permute-start.16 = (bf16[16,768]{1,0:T(8,128)(2,1)S(1)}, bf16[16,768]{1,0:T(8,128)(2,1)S(1)}, u32[]{:S(2)}, u32[]{:S(2)}) collective-permute-start(bf16[16,768]{1,0:T(8,128)(2,1)S(1)} %get-tuple-element.72), channel_id=1, source_target_pairs={{0,511},{1,504},{2,505},{3,506},{4,507},{5,508},{6,509},{7,510},{8... | collective-permute-start | bytes 73736 | tf_op jit(solution)/shard_map/ppermute | solution.py:462

commit v7 on v5

--- a/solution.py
+++ b/solution.py
@@ -78,33 +78,25 @@
     return f(head, rows[:, :WIDE]) + jnp.concatenate([f(left, tail), f(right, tail)], axis=1)
 
 
-def prepare(attn_hbm, w1_hbm, w2_hbm, up_ref, left_ref, corner_ref, w_ref, attn_s, sems):
-    copies = [
-        pltpu.make_async_copy(src, dst, sems.at[i])
-        for i, (src, dst) in enumerate(
-            ((attn_hbm, attn_s), (w1_hbm, w_ref.at[:, 0]), (w2_hbm, w_ref.at[:, 1]))
-        )
-    ]
-    for copy in copies:
-        copy.start()
+def prepare(attn_hbm, up_ref, left_ref, corner_ref, attn_s, sem):
+    copy = pltpu.make_async_copy(attn_hbm, attn_s, sem)
+    copy.start()
     tr, tc, width = attn_s.shape
     tokens = tr * tc
     n = 4 * tr
     s = iota((n, 1), 0)
     edge = ones_where((s // 4) * tc + tc - 4 + s % 4 == iota((n, tokens), 1))
-    copies[0].wait()
+    copy.wait()
     attn = attn_s[...].reshape(tokens, width)
     up_ref[...] = attn[tokens - 4 * tc :]
     left = dot(edge, attn).astype(jnp.bfloat16)
     left_ref[...] = left
     corner_ref[...] = left[n - 16 :]
-    copies[1].wait()
-    copies[2].wait()
 
 
 def dispatch_g(
-    off_hbm, ids_hbm, gates_hbm, dout_hbm, attn_hbm, short_hbm,
-    sent_ref, mask_ref, meta_ref, x_ref, sel_ref,
+    off_hbm, ids_hbm, gates_hbm, dout_hbm, attn_hbm, short_hbm, w1_hbm, w2_hbm,
+    sent_ref, mask_ref, meta_ref, x_ref, sel_ref, w_ref,
     off_ref, ids_ref, gates_ref, dout_s, attn_s, short_s, sems,
 ):
     copies = [
@@ -117,12 +109,14 @@
                 (attn_hbm, attn_s),
                 (short_hbm, short_s),
                 (dout_hbm, dout_s),
+                (w1_hbm, w_ref.at[:, 0]),
+                (w2_hbm, w_ref.at[:, 1]),
             )
         )
     ]
     for copy in copies:
         copy.start()
-    for copy in copies:
+    for copy in copies[:6]:
         copy.wait()
     tr, tc, width = attn_s.shape
     tokens = tr * tc
@@ -159,6 +153,8 @@
     for m in range(3):
         mask_ref[m] = both[m]
     sent_ref[...] = sent.astype(jnp.bfloat16)
+    for copy in copies[6:]:
+        copy.wait()
 
 
 def normalize(x):
@@ -404,23 +400,17 @@
     dout = d_out.reshape(tokens, width)
     part = w_out.shape[1]
 
-    up, left, corner, w_own = pl.pallas_call(
+    up, left, corner = pl.pallas_call(
         prepare,
-        out_shape=(
-            bf16((4 * tc, width)),
-            bf16((4 * tr, width)),
-            bf16((16, width)),
-            bf16((1, 2, part, width)),
-        ),
-        in_specs=[ANY] * 3,
-        out_specs=(VMEM,) * 4,
-        scratch_shapes=[pltpu.VMEM((tr, tc, width), jnp.bfloat16), pltpu.SemaphoreType.DMA((3,))],
+        out_shape=(bf16((4 * tc, width)), bf16((4 * tr, width)), bf16((16, width))),
+        in_specs=[ANY],
+        out_specs=(VMEM,) * 3,
+        scratch_shapes=[pltpu.VMEM((tr, tc, width), jnp.bfloat16), pltpu.SemaphoreType.DMA],
         compiler_params=pltpu.CompilerParams(vmem_limit_bytes=32 * 1024 * 1024),
-        cost_estimate=pl.CostEstimate(flops=1 << 25, bytes_accessed=1 << 21, transcendentals=0),
-    )(in_hbm(attn_win), in_hbm(w_in.transpose(0, 2, 1)), in_hbm(w_out))
-    w_all = lax.all_gather(w_own, "dp", axis=0, tiled=True)
+        cost_estimate=pl.CostEstimate(flops=1 << 25, bytes_accessed=1 << 20, transcendentals=0),
+    )(in_hbm(attn_win))
     up, left, corner = edges(up, left, corner, 1)
-    g_wire, masks, meta, x0, sel = pl.pallas_call(
+    g_wire, masks, meta, x0, sel, w_own = pl.pallas_call(
         dispatch_g,
         out_shape=(
             bf16((n, WIDE)),
@@ -428,26 +418,36 @@
             f32((tokens, tokens)),
             f32((tokens, width)),
             bf16((tokens, 4 * tc + 4 * tr + 16)),
+            bf16((1, 2, part, width)),
         ),
-        in_specs=[ANY] * 6,
-        out_specs=(VMEM,) * 5,
+        in_specs=[ANY] * 8,
+        out_specs=(VMEM,) * 6,
         scratch_shapes=[
             pltpu.SMEM((2,), jnp.int32),
             pltpu.VMEM((2, tokens), jnp.int32),
             pltpu.VMEM((2, tokens), jnp.float32),
         ]
         + [pltpu.VMEM((tr, tc, width), jnp.bfloat16)] * 3
-        + [pltpu.SemaphoreType.DMA((6,))],
+        + [pltpu.SemaphoreType.DMA((8,))],
         compiler_params=pltpu.CompilerParams(vmem_limit_bytes=32 * 1024 * 1024),
         cost_estimate=pl.CostEstimate(
-            flops=4 * 256 * n * WIDE, bytes_accessed=1 << 20, transcendentals=0
+            flops=1 << 36, bytes_accessed=1 << 20, transcendentals=0
         ),
-    )(*(in_hbm(v) for v in (shift_offsets, ids, gates, d_out, attn_win, shortcut)))
+    )(
+        *(
+            in_hbm(v)
+            for v in (
+                shift_offsets, ids, gates, d_out, attn_win, shortcut,
+                w_in.transpose(0, 2, 1), w_out,
+            )
+        )
+    )
+    w_all = lax.all_gather(w_own, "dp", axis=0, tiled=True)
     sent, x = call(
         dispatch_u,
         (bf16((n, 2 * WIDE)), f32((tokens, width))),
         g_wire, masks, x0, sel, up, left, corner,
-        flops=4 * 128 * n * WIDE, traffic=1 << 21,
+        flops=1 << 36, traffic=1 << 21,
     )
     returned, grads = experts(exchange(sent, n_ex), w_all)
     returned = exchange(returned, n_ex)

time: 133 us -> 136 us (1.023)
  blocking collectives: 70 us -> 76.7 us
  starting transfers between devices: 20.4 us -> 18.2 us
    all_to_all x2, blocking collectives: 70 us -> 76.7 us  [exchange(): lax.all_to_all(blocks, 'expert', split_axis=0, concat_axis=0, tiled=True)]
    ppermute x2, starting transfers between devices: 7.71 us -> 2.82 us  [edges(): lax.ppermute(row_edge, 'dp', by_dp)]
    ppermute x2, waiting for transfers between devices: 7.96 us -> 4.99 us  [edges(): lax.ppermute(corner, ('expert', 'dp'), by_both)]
    ppermute x2, starting transfers between devices: 5.24 us -> 7.65 us  [edges(): lax.ppermute(corner, ('expert', 'dp'), by_both)]
    ppermute x2, waiting for transfers between devices: 0.01 us -> 1.63 us  [edges(): lax.ppermute(col_edge, 'expert', by_ex)]
  transfers between devices with their start and end apart: 8 -> 8, of which waited for: 2 -> 3; matrix products, arithmetic and copies ran while one was open for 0% -> 0% of each run, Pallas kernels for 6% -> 6%
where the time goes in v7:
time: 136 us
  blocking collectives  76.7 us (56%)
  Pallas kernels  20.2 us (15%)
  starting transfers between devices  18.2 us (13%)
  between operations  14.1 us (10%)
  waiting for transfers between devices  6.69 us (5%)
    all_to_all x2, blocking collectives, exchange(): lax.all_to_all(blocks, 'expert', split_axis=0, concat_axis=0, tiled=True)  76.7 us
    pallas_call x1, Pallas kernels, experts(): pl.pallas_call(experts_body, out_shape=(jax.ShapeDtypeStruct((n, 2 * WIDE...  9.31 us
    ppermute x2, starting transfers between devices, edges(): lax.ppermute(corner, ('expert', 'dp'), by_both)  7.65 us
    ppermute x2, starting transfers between devices, edges(): lax.ppermute(col_edge, 'expert', by_ex)  7.63 us
    ppermute x2, waiting for transfers between devices, edges(): lax.ppermute(corner, ('expert', 'dp'), by_both)  4.99 us
    pallas_call x3, Pallas kernels, call(): pl.pallas_call(body, out_shape=outs, in_specs=[VMEM] * len(args) if specs...  3.56 us
    pallas_call x1, Pallas kernels, per_device(): pl.pallas_call(dispatch_g, out_shape=(bf16((n, WIDE)), bf16((3, n, tokens...  3.3 us
    pallas_call x1, Pallas kernels, per_device(): pl.pallas_call(combine_y, out_shape=(bf16((tokens, width)), f32((2, token...  2.92 us
  transfers between devices with their start and end apart: 8, of which 3 were waited for; matrix products, arithmetic and copies ran while one was open for 0% of the time, Pallas kernels for 6%

profile of v7, /device:TPU:1, one launch (start us, length us, event | category | flops | bytes accessed | tf_op | source)
XLA Modules:
  0.0 136.0 jit_solution(8457728873253724913)
XLA Ops:
  7.2 0.0 all-gather.2.cloned.1.call-start
  7.2 1.1 shard_map.128
  8.3 5.5 %collective-permute-start.2 = (bf16[16,768]{1,0:T(8,128)(2,1)S(1)}, bf16[16,768]{1,0:T(8,128)(2,1)S(1)}, u32[]{:S(2)}, u32[]{:S(2)}) collective-permute-start(bf16[16,768]{1,0:T(8,128)(2,1)S(1)} %get-tuple-element.36), channel_id=1, source_target_pairs={{0,9},{1,10},{2,11},{3,12},{4,13},{5,14},{6,15},{7,8},{8,17},{9,18... | collective-permute-start | bytes 73736 | tf_op jit(solution)/shard_map/ppermute | solution.py:387
  13.8 3.2 %collective-permute-start.1 = (bf16[32,768]{1,0:T(8,128)(2,1)S(1)}, bf16[32,768]{1,0:T(8,128)(2,1)S(1)}, u32[]{:S(2)}, u32[]{:S(2)}) collective-permute-start(bf16[32,768]{1,0:T(8,128)(2,1)S(1)} %get-tuple-element.35), channel_id=1, source_target_pairs={{0,8},{8,16},{16,24},{24,32},{32,40},{40,48},{48,56},{56,64},{64,7... | collective-permute-start | bytes 147464 | tf_op jit(solution)/shard_map/ppermute | solution.py:386
  17.1 0.3 collective-permute-start
  17.4 3.3 %shard_map.127 = (bf16[512,512]{1,0:T(8,128)(2,1)S(1)}, bf16[3,512,128]{2,1,0:T(8,128)(2,1)S(1)}, f32[128,128]{1,0:T(8,128)S(1)}, f32[128,768]{1,0:T(8,128)S(1)}...) custom-call(s32[2]{0:T(128)} %off_ref.1, s32[2,128]{1,0:T(2,128)} %bitcast.31, f32[2,128]{1,0:T(2,128)} %bitcast.32, ...), custom_call_target="tpu_custom_call" | custom-call | flops 68719476736 | bytes 1048576 | tf_op jit(solution)/shard_map/pallas_call | solution.py:413
  20.7 0.0 all-gather.2.cloned.1.call-update
  20.7 0.0 reduce-scatter.2.cloned.1.call-start
  20.7 4.0 %collective-permute-done.2.corner_ref = bf16[16,768]{1,0:T(8,128)(2,1)S(1)} collective-permute-done((bf16[16,768]{1,0:T(8,128)(2,1)S(1)}, bf16[16,768]{1,0:T(8,128)(2,1)S(1)}, u32[]{:S(2)}, u32[]{:S(2)}) %collective-permute-start.2) | collective-permute-done | bytes 24608 | tf_op jit(solution)/shard_map/ppermute | solution.py:387
  24.8 1.6 %collective-permute-done.1.left_ref = bf16[32,768]{1,0:T(8,128)(2,1)S(1)} collective-permute-done((bf16[32,768]{1,0:T(8,128)(2,1)S(1)}, bf16[32,768]{1,0:T(8,128)(2,1)S(1)}, u32[]{:S(2)}, u32[]{:S(2)}) %collective-permute-start.1) | collective-permute-done | bytes 49184 | tf_op jit(solution)/shard_map/ppermute | solution.py:386
  26.4 0.0 collective-permute-done.up_ref
  26.4 0.8 shard_map.129
  27.2 36.4 %all_to_all.10 = bf16[64,8,1024]{2,1,0:T(8,128)(2,1)S(1)} all-to-all(bf16[64,8,1024]{2,1,0:T(8,128)(2,1)S(1)} %bitcast.22), channel_id=1, replica_groups=mesh['expert'=64,'dp'=8] {'expert'}, dimensions={0} | all-to-all | bytes 2097152 | tf_op jit(solution)/shard_map/all_to_all | solution.py:371
  63.6 0.0 all-gather.2.cloned.1.call-done.w_hbm
  63.6 9.3 %shard_map.130 = (bf16[512,1024]{1,0:T(8,128)(2,1)S(1)}, bf16[8,2,192,768]{3,2,1,0:T(8,128)(2,1)}) custom-call(bf16[512,1024]{1,0:T(8,128)(2,1)S(1)} %bitcast.23, bf16[8,2,192,768]{3,2,1,0:T(8,128)(2,1)} %all-gather.2.cloned.1.call-done.w_hbm), custom_call_target="tpu_custom_call" | custom-call | flops 4529848320 | bytes 9437184 | tf_op jit(solution)/shard_map/pallas_call | solution.py:278
  73.0 0.0 copy-start
  73.0 0.0 copy-start.1
  73.0 0.0 reduce-scatter.2.cloned.1.call-update
  73.0 40.3 %all_to_all.11 = bf16[64,8,1024]{2,1,0:T(8,128)(2,1)S(1)} all-to-all(bf16[64,8,1024]{2,1,0:T(8,128)(2,1)S(1)} %bitcast.21), channel_id=1, replica_groups=mesh['expert'=64,'dp'=8] {'expert'}, dimensions={0} | all-to-all | bytes 2097152 | tf_op jit(solution)/shard_map/all_to_all | solution.py:371
  113.3 0.0 copy-done
  113.3 1.3 shard_map.131
  114.6 2.5 %collective-permute-start.3 = (bf16[64,768]{1,0:T(8,128)(2,1)S(1)}, bf16[64,768]{1,0:T(8,128)(2,1)S(1)}, u32[]{:S(2)}, u32[]{:S(2)}) collective-permute-start(bf16[64,768]{1,0:T(8,128)(2,1)S(1)} %get-tuple-element.48), channel_id=1, source_target_pairs={{0,7},{1,0},{2,1},{3,2},{4,3},{5,4},{6,5},{7,6},{8,15},{9,8},{10,9... | collective-permute-start | bytes 294920 | tf_op jit(solution)/shard_map/ppermute | solution.py:385
  117.1 4.4 %collective-permute-start.4 = (bf16[32,768]{1,0:T(8,128)(2,1)S(1)}, bf16[32,768]{1,0:T(8,128)(2,1)S(1)}, u32[]{:S(2)}, u32[]{:S(2)}) collective-permute-start(bf16[32,768]{1,0:T(8,128)(2,1)S(1)} %get-tuple-element.49), channel_id=1, source_target_pairs={{0,504},{8,0},{16,8},{24,16},{32,24},{40,32},{48,40},{56,48},{64,5... | collective-permute-start | bytes 147464 | tf_op jit(solution)/shard_map/ppermute | solution.py:386
  121.6 2.1 %collective-permute-start.5 = (bf16[16,768]{1,0:T(8,128)(2,1)S(1)}, bf16[16,768]{1,0:T(8,128)(2,1)S(1)}, u32[]{:S(2)}, u32[]{:S(2)}) collective-permute-start(bf16[16,768]{1,0:T(8,128)(2,1)S(1)} %get-tuple-element.50), channel_id=1, source_target_pairs={{0,511},{1,504},{2,505},{3,506},{4,507},{5,508},{6,509},{7,510},{8... | collective-permute-start | bytes 73736 | tf_op jit(solution)/shard_map/ppermute | solution.py:387
  123.7 0.0 reduce-scatter.2.cloned.1.call-done.grad_hbm
  123.7 2.9 %shard_map.132 = (bf16[128,768]{1,0:T(8,128)(2,1)}, f32[2,128]{1,0:T(2,128)}, f32[1,192,768]{2,1,0:T(8,128)}, f32[1,192,768]{2,1,0:T(8,128)}) custom-call(bf16[512,1024]{1,0:T(8,128)(2,1)S(1)} %bitcast.20, f32[128,128]{1,0:T(8,128)S(1)} %get-tuple-element.40.meta_ref, f32[128,768]{1,0:T(8,128)S(1)} %get-tuple-element.41.x_ref, ...), custom_call_target="tpu_custom_call" | custom-call | flops 268435456 | bytes 2097152 | tf_op jit(solution)/shard_map/pallas_call | solution.py:468
  126.7 0.9 collective-permute-done.5.corner_ref
  127.6 0.0 collective-permute-done.4.right_ref
  127.6 0.0 collective-permute-done.3.down_ref
  127.6 0.0 copy-done.1
  127.6 1.5 %shard_map.133 = bf16[128,768]{1,0:T(8,128)(2,1)} custom-call(s32[2]{0:T(128)S(1)} %copy-done.1, bf16[128,768]{1,0:T(8,128)(2,1)S(1)} %get-tuple-element.47.ds_ref, bf16[64,768]{1,0:T(8,128)(2,1)S(1)} %collective-permute-done.3.down_ref, bf16[32,768]{1,0:T(8,128)(2,1)S(1)} %collective-permute-done.4.right_ref, ...), custom_call_target="tpu_custom_call" | custom-call | flops 50331648 | bytes 524288 | tf_op jit(solution)/shard_map/pallas_call | solution.py:44
Async XLA Ops:
  7.2 56.5 %all-gather.2.cloned.1.call-start = ((), (), s32[]{:S(2)}) async-start(), calls=%async_computation.3 | async-start | bytes 5308416 | tf_op jit(solution)/shard_map/all_gather | solution.py:445
  8.3 16.5 %collective-permute-start.2 = (bf16[16,768]{1,0:T(8,128)(2,1)S(1)}, bf16[16,768]{1,0:T(8,128)(2,1)S(1)}, u32[]{:S(2)}, u32[]{:S(2)}) collective-permute-start(bf16[16,768]{1,0:T(8,128)(2,1)S(1)} %get-tuple-element.36), channel_id=1, source_target_pairs={{0,9},{1,10},{2,11},{3,12},{4,13},{5,14},{6,15},{7,8},{8,17},{9,18... | collective-permute-start | bytes 73736 | tf_op jit(solution)/shard_map/ppermute | solution.py:387
  13.8 12.6 %collective-permute-start.1 = (bf16[32,768]{1,0:T(8,128)(2,1)S(1)}, bf16[32,768]{1,0:T(8,128)(2,1)S(1)}, u32[]{:S(2)}, u32[]{:S(2)}) collective-permute-start(bf16[32,768]{1,0:T(8,128)(2,1)S(1)} %get-tuple-element.35), channel_id=1, source_target_pairs={{0,8},{8,16},{16,24},{24,32},{32,40},{40,48},{48,56},{56,64},{64,7... | collective-permute-start | bytes 147464 | tf_op jit(solution)/shard_map/ppermute | solution.py:386
  17.1 9.4 %collective-permute-start = (bf16[64,768]{1,0:T(8,128)(2,1)S(1)}, bf16[64,768]{1,0:T(8,128)(2,1)S(1)}, u32[]{:S(2)}, u32[]{:S(2)}) collective-permute-start(bf16[64,768]{1,0:T(8,128)(2,1)S(1)} %get-tuple-element.34), channel_id=1, source_target_pairs={{0,1},{1,2},{2,3},{3,4},{4,5},{5,6},{6,7},{7,0},{8,9},{9,10},{10,1... | collective-permute-start | bytes 294920 | tf_op jit(solution)/shard_map/ppermute | solution.py:385
  20.7 103.0 %reduce-scatter.2.cloned.1.call-start = ((), (), s32[]{:S(2)}) async-start(), calls=%async_computation.4 | async-start | bytes 5308416 | tf_op jit(solution)/shard_map/reduce_scatter | solution.py:454
  73.0 40.4 %copy-start = (bf16[8,16,768]{2,1,0:T(8,128)(2,1)S(1)}, bf16[8,16,768]{2,1,0:T(8,128)(2,1)}, u32[]{:S(2)}) copy-start(bf16[8,16,768]{2,1,0:T(8,128)(2,1)} %dout_hbm.1) | copy-start | bytes 589828
  73.0 54.7 %copy-start.1 = (s32[2]{0:T(128)S(1)}, s32[2]{0:T(128)}, u32[]{:S(2)}) copy-start(s32[2]{0:T(128)} %off_ref.1) | copy-start | bytes 28
  114.6 13.0 %collective-permute-start.3 = (bf16[64,768]{1,0:T(8,128)(2,1)S(1)}, bf16[64,768]{1,0:T(8,128)(2,1)S(1)}, u32[]{:S(2)}, u32[]{:S(2)}) collective-permute-start(bf16[64,768]{1,0:T(8,128)(2,1)S(1)} %get-tuple-element.48), channel_id=1, source_target_pairs={{0,7},{1,0},{2,1},{3,2},{4,3},{5,4},{6,5},{7,6},{8,15},{9,8},{10,9... | collective-permute-start | bytes 294920 | tf_op jit(solution)/shard_map/ppermute | solution.py:385
  117.1 10.5 %collective-permute-start.4 = (bf16[32,768]{1,0:T(8,128)(2,1)S(1)}, bf16[32,768]{1,0:T(8,128)(2,1)S(1)}, u32[]{:S(2)}, u32[]{:S(2)}) collective-permute-start(bf16[32,768]{1,0:T(8,128)(2,1)S(1)} %get-tuple-element.49), channel_id=1, source_target_pairs={{0,504},{8,0},{16,8},{24,16},{32,24},{40,32},{48,40},{56,48},{64,5... | collective-permute-start | bytes 147464 | tf_op jit(solution)/shard_map/ppermute | solution.py:386
  121.6 6.0 %collective-permute-start.5 = (bf16[16,768]{1,0:T(8,128)(2,1)S(1)}, bf16[16,768]{1,0:T(8,128)(2,1)S(1)}, u32[]{:S(2)}, u32[]{:S(2)}) collective-permute-start(bf16[16,768]{1,0:T(8,128)(2,1)S(1)} %get-tuple-element.50), channel_id=1, source_target_pairs={{0,511},{1,504},{2,505},{3,506},{4,507},{5,508},{6,509},{7,510},{8... | collective-permute-start | bytes 73736 | tf_op jit(solution)/shard_map/ppermute | solution.py:387
Sparse Core Ops, SparseCore 0:
  20.8 42.1 all-gather.1
  73.1 41.6 reduce-scatter.1

commit v8 on v7

--- a/solution.py
+++ b/solution.py
@@ -94,9 +94,32 @@
     corner_ref[...] = left[n - 16 :]
 
 
+def join_body(w1_hbm, w2_hbm, w_ref, sems):
+    copies = [
+        pltpu.make_async_copy(src, w_ref.at[:, k], sems.at[k])
+        for k, src in enumerate((w1_hbm, w2_hbm))
+    ]
+    for copy in copies:
+        copy.start()
+    for copy in copies:
+        copy.wait()
+
+
+def join(w1, w2):
+    return pl.pallas_call(
+        join_body,
+        out_shape=jax.ShapeDtypeStruct((1, 2, *w2.shape[1:]), w2.dtype),
+        in_specs=[ANY] * 2,
+        out_specs=VMEM,
+        scratch_shapes=[pltpu.SemaphoreType.DMA((2,))],
+        compiler_params=pltpu.CompilerParams(vmem_limit_bytes=32 * 1024 * 1024),
+        cost_estimate=pl.CostEstimate(flops=0, bytes_accessed=8 * w2.size, transcendentals=0),
+    )(in_hbm(w1), in_hbm(w2))
+
+
 def dispatch_g(
-    off_hbm, ids_hbm, gates_hbm, dout_hbm, attn_hbm, short_hbm, w1_hbm, w2_hbm,
-    sent_ref, mask_ref, meta_ref, x_ref, sel_ref, w_ref,
+    off_hbm, ids_hbm, gates_hbm, dout_hbm, attn_hbm, short_hbm,
+    sent_ref, mask_ref, meta_ref, x_ref, sel_ref,
     off_ref, ids_ref, gates_ref, dout_s, attn_s, short_s, sems,
 ):
     copies = [
@@ -109,14 +132,12 @@
                 (attn_hbm, attn_s),
                 (short_hbm, short_s),
                 (dout_hbm, dout_s),
-                (w1_hbm, w_ref.at[:, 0]),
-                (w2_hbm, w_ref.at[:, 1]),
             )
         )
     ]
     for copy in copies:
         copy.start()
-    for copy in copies[:6]:
+    for copy in copies:
         copy.wait()
     tr, tc, width = attn_s.shape
     tokens = tr * tc
@@ -153,8 +174,6 @@
     for m in range(3):
         mask_ref[m] = both[m]
     sent_ref[...] = sent.astype(jnp.bfloat16)
-    for copy in copies[6:]:
-        copy.wait()
 
 
 def normalize(x):
@@ -381,11 +400,10 @@
         for q in range(n_ex)
         for p in range(n_dp)
     ]
-    return (
-        lax.ppermute(row_edge, "dp", by_dp),
-        lax.ppermute(col_edge, "expert", by_ex),
-        lax.ppermute(corner, ("expert", "dp"), by_both),
-    )
+    row_edge = lax.ppermute(row_edge, "dp", by_dp)
+    corner = lax.ppermute(corner, ("expert", "dp"), by_both)
+    col_edge = lax.ppermute(col_edge, "expert", by_ex)
+    return row_edge, col_edge, corner
 
 
 def per_device(attn_win, shortcut, d_out, expert_ids, gate_probs, shift_offsets, w_in, w_out):
@@ -409,8 +427,11 @@
         compiler_params=pltpu.CompilerParams(vmem_limit_bytes=32 * 1024 * 1024),
         cost_estimate=pl.CostEstimate(flops=1 << 25, bytes_accessed=1 << 20, transcendentals=0),
     )(in_hbm(attn_win))
+    w_in, left = lax.optimization_barrier((w_in, left))
+    w_own = join(w_in.transpose(0, 2, 1), w_out)
+    w_all = lax.all_gather(w_own, "dp", axis=0, tiled=True)
     up, left, corner = edges(up, left, corner, 1)
-    g_wire, masks, meta, x0, sel, w_own = pl.pallas_call(
+    g_wire, masks, meta, x0, sel = pl.pallas_call(
         dispatch_g,
         out_shape=(
             bf16((n, WIDE)),
@@ -418,36 +439,26 @@
             f32((tokens, tokens)),
             f32((tokens, width)),
             bf16((tokens, 4 * tc + 4 * tr + 16)),
-            bf16((1, 2, part, width)),
         ),
-        in_specs=[ANY] * 8,
-        out_specs=(VMEM,) * 6,
+        in_specs=[ANY] * 6,
+        out_specs=(VMEM,) * 5,
         scratch_shapes=[
             pltpu.SMEM((2,), jnp.int32),
             pltpu.VMEM((2, tokens), jnp.int32),
             pltpu.VMEM((2, tokens), jnp.float32),
         ]
         + [pltpu.VMEM((tr, tc, width), jnp.bfloat16)] * 3
-        + [pltpu.SemaphoreType.DMA((8,))],
+        + [pltpu.SemaphoreType.DMA((6,))],
         compiler_params=pltpu.CompilerParams(vmem_limit_bytes=32 * 1024 * 1024),
         cost_estimate=pl.CostEstimate(
             flops=1 << 36, bytes_accessed=1 << 20, transcendentals=0
         ),
-    )(
-        *(
-            in_hbm(v)
-            for v in (
-                shift_offsets, ids, gates, d_out, attn_win, shortcut,
-                w_in.transpose(0, 2, 1), w_out,
-            )
-        )
-    )
-    w_all = lax.all_gather(w_own, "dp", axis=0, tiled=True)
+    )(*(in_hbm(v) for v in (shift_offsets, ids, gates, d_out, attn_win, shortcut)))
     sent, x = call(
         dispatch_u,
         (bf16((n, 2 * WIDE)), f32((tokens, width))),
         g_wire, masks, x0, sel, up, left, corner,
-        flops=1 << 36, traffic=1 << 21,
+        flops=4 * 128 * n * WIDE, traffic=1 << 21,
     )
     returned, grads = experts(exchange(sent, n_ex), w_all)
     returned = exchange(returned, n_ex)

time: 136 us -> 135 us (level)
  blocking collectives: 76.7 us -> 75.3 us
    pallas_call x0 -> x1, Pallas kernels: none -> 1.88 us  [join(): pl.pallas_call(join_body, out_shape=jax.ShapeDtypeStruct((1, 2, *w2.shape...]
    all_to_all x2, blocking collectives: 76.7 us -> 75.3 us  [exchange(): lax.all_to_all(blocks, 'expert', split_axis=0, concat_axis=0, tiled=True)]
  transfers between devices with their start and end apart: 8 -> 8, of which waited for: 3 -> 3; matrix products, arithmetic and copies ran while one was open for 0% -> 0% of each run, Pallas kernels for 6% -> 7%
where the time goes in v8:
time: 135 us
  blocking collectives  75.3 us (56%)
  Pallas kernels  21.3 us (16%)
  starting transfers between devices  18.2 us (13%)
  between operations  14.1 us (10%)
  waiting for transfers between devices  5.63 us (4%)
    all_to_all x2, blocking collectives, exchange(): lax.all_to_all(blocks, 'expert', split_axis=0, concat_axis=0, tiled=True)  75.3 us
    pallas_call x1, Pallas kernels, experts(): pl.pallas_call(experts_body, out_shape=(jax.ShapeDtypeStruct((n, 2 * WIDE...  9.32 us
    ppermute x2, starting transfers between devices, edges(): corner = lax.ppermute(corner, ('expert', 'dp'), by_both)  7.65 us
    ppermute x2, starting transfers between devices, edges(): col_edge = lax.ppermute(col_edge, 'expert', by_ex)  7.63 us
    ppermute x2, waiting for transfers between devices, edges(): corner = lax.ppermute(corner, ('expert', 'dp'), by_both)  3.93 us
    pallas_call x3, Pallas kernels, call(): pl.pallas_call(body, out_shape=outs, in_specs=[VMEM] * len(args) if specs...  3.57 us
    pallas_call x1, Pallas kernels, per_device(): pl.pallas_call(combine_y, out_shape=(bf16((tokens, width)), f32((2, token...  2.92 us
    ppermute x2, starting transfers between devices, edges(): row_edge = lax.ppermute(row_edge, 'dp', by_dp)  2.82 us
  transfers between devices with their start and end apart: 8, of which 3 were waited for; matrix products, arithmetic and copies ran while one was open for 0% of the time, Pallas kernels for 7%

profile of v8, /device:TPU:1, one launch (start us, length us, event | category | flops | bytes accessed | tf_op | source)
XLA Modules:
  0.0 134.5 jit_solution(8737765614553147423)
XLA Ops:
  7.2 0.0 all-gather.2.cloned.1.call-start
  7.2 1.1 shard_map.128
  8.3 5.5 %collective-permute-start.2 = (bf16[16,768]{1,0:T(8,128)(2,1)S(1)}, bf16[16,768]{1,0:T(8,128)(2,1)S(1)}, u32[]{:S(2)}, u32[]{:S(2)}) collective-permute-start(bf16[16,768]{1,0:T(8,128)(2,1)S(1)} %get-tuple-element.38), channel_id=1, source_target_pairs={{0,9},{1,10},{2,11},{3,12},{4,13},{5,14},{6,15},{7,8},{8,17},{9,18... | collective-permute-start | bytes 73736 | tf_op jit(solution)/shard_map/ppermute | solution.py:404
  13.8 3.2 %collective-permute-start.1 = (bf16[32,768]{1,0:T(8,128)(2,1)S(1)}, bf16[32,768]{1,0:T(8,128)(2,1)S(1)}, u32[]{:S(2)}, u32[]{:S(2)}) collective-permute-start(bf16[32,768]{1,0:T(8,128)(2,1)S(1)} %get-tuple-element.37), channel_id=1, source_target_pairs={{0,8},{8,16},{16,24},{24,32},{32,40},{40,48},{48,56},{56,64},{64,7... | collective-permute-start | bytes 147464 | tf_op jit(solution)/shard_map/ppermute | solution.py:405
  17.1 0.3 collective-permute-start
  17.4 1.9 %shard_map.130 = bf16[1,2,192,768]{3,2,1,0:T(8,128)(2,1)} custom-call(bf16[1,192,768]{2,1,0:T(8,128)(2,1)} %bitcast.26, bf16[1,192,768]{2,1,0:T(8,128)(2,1)} %w2_hbm.1), custom_call_target="tpu_custom_call" | custom-call | bytes 1179648 | tf_op jit(solution)/shard_map/pallas_call | solution.py:109
  19.2 0.0 all-gather.2.cloned.1.call-update
  19.3 0.0 reduce-scatter.2.cloned.1.call-start
  19.3 2.5 %shard_map.127 = (bf16[512,512]{1,0:T(8,128)(2,1)S(1)}, bf16[3,512,128]{2,1,0:T(8,128)(2,1)S(1)}, f32[128,128]{1,0:T(8,128)S(1)}, f32[128,768]{1,0:T(8,128)S(1)}, bf16[128,112]{1,0:T(8,128)(2,1)S(1)}) custom-call(s32[2]{0:T(128)} %off_ref.1, s32[2,128]{1,0:T(2,128)} %bitcast.31, f32[2,128]{1,0:T(2,128)} %bitcast.32, bf16[8,16,768]{2,1,0:T(8,128)(2,1)} %dout_hbm.1, ...), custom_call_target="tpu_custom_call" | custom-call | flops 68719476736 | bytes 1048576 | tf_op jit(solution)/shard_map/pallas_call | solution.py:434
  21.8 3.0 %collective-permute-done.2.corner_ref = bf16[16,768]{1,0:T(8,128)(2,1)S(1)} collective-permute-done((bf16[16,768]{1,0:T(8,128)(2,1)S(1)}, bf16[16,768]{1,0:T(8,128)(2,1)S(1)}, u32[]{:S(2)}, u32[]{:S(2)}) %collective-permute-start.2) | collective-permute-done | bytes 24608 | tf_op jit(solution)/shard_map/ppermute | solution.py:404
  24.8 1.6 %collective-permute-done.1.left_ref = bf16[32,768]{1,0:T(8,128)(2,1)S(1)} collective-permute-done((bf16[32,768]{1,0:T(8,128)(2,1)S(1)}, bf16[32,768]{1,0:T(8,128)(2,1)S(1)}, u32[]{:S(2)}, u32[]{:S(2)}) %collective-permute-start.1) | collective-permute-done | bytes 49184 | tf_op jit(solution)/shard_map/ppermute | solution.py:405
  26.4 0.0 collective-permute-done.up_ref
  26.4 0.8 shard_map.129
  27.2 37.8 %all_to_all.10 = bf16[64,8,1024]{2,1,0:T(8,128)(2,1)S(1)} all-to-all(bf16[64,8,1024]{2,1,0:T(8,128)(2,1)S(1)} %bitcast.22), channel_id=1, replica_groups=mesh['expert'=64,'dp'=8] {'expert'}, dimensions={0} | all-to-all | bytes 2097152 | tf_op jit(solution)/shard_map/all_to_all | solution.py:390
  65.1 0.0 all-gather.2.cloned.1.call-done.w_hbm
  65.1 9.3 %shard_map.131 = (bf16[512,1024]{1,0:T(8,128)(2,1)S(1)}, bf16[8,2,192,768]{3,2,1,0:T(8,128)(2,1)}) custom-call(bf16[512,1024]{1,0:T(8,128)(2,1)S(1)} %bitcast.23, bf16[8,2,192,768]{3,2,1,0:T(8,128)(2,1)} %all-gather.2.cloned.1.call-done.w_hbm), custom_call_target="tpu_custom_call" | custom-call | flops 4529848320 | bytes 9437184 | tf_op jit(solution)/shard_map/pallas_call | solution.py:297
  74.4 0.0 copy-start
  74.4 0.0 copy-start.1
  74.4 0.0 reduce-scatter.2.cloned.1.call-update
  74.4 37.5 %all_to_all.11 = bf16[64,8,1024]{2,1,0:T(8,128)(2,1)S(1)} all-to-all(bf16[64,8,1024]{2,1,0:T(8,128)(2,1)S(1)} %bitcast.21), channel_id=1, replica_groups=mesh['expert'=64,'dp'=8] {'expert'}, dimensions={0} | all-to-all | bytes 2097152 | tf_op jit(solution)/shard_map/all_to_all | solution.py:390
  111.9 0.0 copy-done
  111.9 1.3 shard_map.132
  113.2 2.5 %collective-permute-start.3 = (bf16[64,768]{1,0:T(8,128)(2,1)S(1)}, bf16[64,768]{1,0:T(8,128)(2,1)S(1)}, u32[]{:S(2)}, u32[]{:S(2)}) collective-permute-start(bf16[64,768]{1,0:T(8,128)(2,1)S(1)} %get-tuple-element.50), channel_id=1, source_target_pairs={{0,7},{1,0},{2,1},{3,2},{4,3},{5,4},{6,5},{7,6},{8,15},{9,8},{10,9... | collective-permute-start | bytes 294920 | tf_op jit(solution)/shard_map/ppermute | solution.py:403
  115.7 4.4 %collective-permute-start.4 = (bf16[32,768]{1,0:T(8,128)(2,1)S(1)}, bf16[32,768]{1,0:T(8,128)(2,1)S(1)}, u32[]{:S(2)}, u32[]{:S(2)}) collective-permute-start(bf16[32,768]{1,0:T(8,128)(2,1)S(1)} %get-tuple-element.51), channel_id=1, source_target_pairs={{0,504},{8,0},{16,8},{24,16},{32,24},{40,32},{48,40},{56,48},{64,5... | collective-permute-start | bytes 147464 | tf_op jit(solution)/shard_map/ppermute | solution.py:405
  120.2 2.1 %collective-permute-start.5 = (bf16[16,768]{1,0:T(8,128)(2,1)S(1)}, bf16[16,768]{1,0:T(8,128)(2,1)S(1)}, u32[]{:S(2)}, u32[]{:S(2)}) collective-permute-start(bf16[16,768]{1,0:T(8,128)(2,1)S(1)} %get-tuple-element.52), channel_id=1, source_target_pairs={{0,511},{1,504},{2,505},{3,506},{4,507},{5,508},{6,509},{7,510},{8... | collective-permute-start | bytes 73736 | tf_op jit(solution)/shard_map/ppermute | solution.py:404
  122.3 0.0 reduce-scatter.2.cloned.1.call-done.grad_hbm
  122.3 2.9 %shard_map.133 = (bf16[128,768]{1,0:T(8,128)(2,1)}, f32[2,128]{1,0:T(2,128)}, f32[1,192,768]{2,1,0:T(8,128)}, f32[1,192,768]{2,1,0:T(8,128)}) custom-call(bf16[512,1024]{1,0:T(8,128)(2,1)S(1)} %bitcast.20, f32[128,128]{1,0:T(8,128)S(1)} %get-tuple-element.42.meta_ref, f32[128,768]{1,0:T(8,128)S(1)} %get-tuple-element.43.x_ref, ...), custom_call_target="tpu_custom_call" | custom-call | flops 268435456 | bytes 2097152 | tf_op jit(solution)/shard_map/pallas_call | solution.py:479
  125.2 0.9 collective-permute-done.5.corner_ref
  126.2 0.0 collective-permute-done.4.right_ref
  126.2 0.0 collective-permute-done.3.down_ref
  126.2 0.0 copy-done.1
  126.2 1.5 %shard_map.134 = bf16[128,768]{1,0:T(8,128)(2,1)} custom-call(s32[2]{0:T(128)S(1)} %copy-done.1, bf16[128,768]{1,0:T(8,128)(2,1)S(1)} %get-tuple-element.49.ds_ref, bf16[64,768]{1,0:T(8,128)(2,1)S(1)} %collective-permute-done.3.down_ref, bf16[32,768]{1,0:T(8,128)(2,1)S(1)} %collective-permute-done.4.right_ref, ...), custom_call_target="tpu_custom_call" | custom-call | flops 50331648 | bytes 524288 | tf_op jit(solution)/shard_map/pallas_call | solution.py:44
Async XLA Ops:
  7.2 57.9 %all-gather.2.cloned.1.call-start = ((), (), s32[]{:S(2)}) async-start(), calls=%async_computation.3 | async-start | bytes 5308416 | tf_op jit(solution)/shard_map/all_gather | solution.py:432
  8.3 16.5 %collective-permute-start.2 = (bf16[16,768]{1,0:T(8,128)(2,1)S(1)}, bf16[16,768]{1,0:T(8,128)(2,1)S(1)}, u32[]{:S(2)}, u32[]{:S(2)}) collective-permute-start(bf16[16,768]{1,0:T(8,128)(2,1)S(1)} %get-tuple-element.38), channel_id=1, source_target_pairs={{0,9},{1,10},{2,11},{3,12},{4,13},{5,14},{6,15},{7,8},{8,17},{9,18... | collective-permute-start | bytes 73736 | tf_op jit(solution)/shard_map/ppermute | solution.py:404
  13.8 12.6 %collective-permute-start.1 = (bf16[32,768]{1,0:T(8,128)(2,1)S(1)}, bf16[32,768]{1,0:T(8,128)(2,1)S(1)}, u32[]{:S(2)}, u32[]{:S(2)}) collective-permute-start(bf16[32,768]{1,0:T(8,128)(2,1)S(1)} %get-tuple-element.37), channel_id=1, source_target_pairs={{0,8},{8,16},{16,24},{24,32},{32,40},{40,48},{48,56},{56,64},{64,7... | collective-permute-start | bytes 147464 | tf_op jit(solution)/shard_map/ppermute | solution.py:405
  17.1 9.4 %collective-permute-start = (bf16[64,768]{1,0:T(8,128)(2,1)S(1)}, bf16[64,768]{1,0:T(8,128)(2,1)S(1)}, u32[]{:S(2)}, u32[]{:S(2)}) collective-permute-start(bf16[64,768]{1,0:T(8,128)(2,1)S(1)} %get-tuple-element.35), channel_id=1, source_target_pairs={{0,1},{1,2},{2,3},{3,4},{4,5},{5,6},{6,7},{7,0},{8,9},{9,10},{10,1... | collective-permute-start | bytes 294920 | tf_op jit(solution)/shard_map/ppermute | solution.py:403
  19.3 103.0 %reduce-scatter.2.cloned.1.call-start = ((), (), s32[]{:S(2)}) async-start(), calls=%async_computation.4 | async-start | bytes 5308416 | tf_op jit(solution)/shard_map/reduce_scatter | solution.py:465
  74.4 37.5 %copy-start = (bf16[8,16,768]{2,1,0:T(8,128)(2,1)S(1)}, bf16[8,16,768]{2,1,0:T(8,128)(2,1)}, u32[]{:S(2)}) copy-start(bf16[8,16,768]{2,1,0:T(8,128)(2,1)} %dout_hbm.1) | copy-start | bytes 589828
  74.4 51.8 %copy-start.1 = (s32[2]{0:T(128)S(1)}, s32[2]{0:T(128)}, u32[]{:S(2)}) copy-start(s32[2]{0:T(128)} %off_ref.1) | copy-start | bytes 28
  113.2 13.0 %collective-permute-start.3 = (bf16[64,768]{1,0:T(8,128)(2,1)S(1)}, bf16[64,768]{1,0:T(8,128)(2,1)S(1)}, u32[]{:S(2)}, u32[]{:S(2)}) collective-permute-start(bf16[64,768]{1,0:T(8,128)(2,1)S(1)} %get-tuple-element.50), channel_id=1, source_target_pairs={{0,7},{1,0},{2,1},{3,2},{4,3},{5,4},{6,5},{7,6},{8,15},{9,8},{10,9... | collective-permute-start | bytes 294920 | tf_op jit(solution)/shard_map/ppermute | solution.py:403
  115.7 10.5 %collective-permute-start.4 = (bf16[32,768]{1,0:T(8,128)(2,1)S(1)}, bf16[32,768]{1,0:T(8,128)(2,1)S(1)}, u32[]{:S(2)}, u32[]{:S(2)}) collective-permute-start(bf16[32,768]{1,0:T(8,128)(2,1)S(1)} %get-tuple-element.51), channel_id=1, source_target_pairs={{0,504},{8,0},{16,8},{24,16},{32,24},{40,32},{48,40},{56,48},{64,5... | collective-permute-start | bytes 147464 | tf_op jit(solution)/shard_map/ppermute | solution.py:405
  120.2 6.0 %collective-permute-start.5 = (bf16[16,768]{1,0:T(8,128)(2,1)S(1)}, bf16[16,768]{1,0:T(8,128)(2,1)S(1)}, u32[]{:S(2)}, u32[]{:S(2)}) collective-permute-start(bf16[16,768]{1,0:T(8,128)(2,1)S(1)} %get-tuple-element.52), channel_id=1, source_target_pairs={{0,511},{1,504},{2,505},{3,506},{4,507},{5,508},{6,509},{7,510},{8... | collective-permute-start | bytes 73736 | tf_op jit(solution)/shard_map/ppermute | solution.py:404
Sparse Core Ops, SparseCore 0:
  19.4 42.1 all-gather.1
  74.5 39.0 reduce-scatter.1
